TPU v7x, 1024 devices: a whole 4x4x32 slice. The times are simulated.
1024 devices in a mesh: section: 2 (over core), dp: 16 (over x, y), expert: 32 (over z).
Axes of the slice: x: 4, y: 4, z: 32, core: 2. Of those that a mesh axis runs over, the one named last changes fastest.
Arguments:
- tokens: bfloat16 [16384, 5120], P(('section', 'expert'), 'dp'), may hold values from -6 to 6
- routes: int32 [16384, 4], P(('section', 'expert')), may hold values from 0 to 127, all different within a row; in each aligned block of 256 rows (0 to 255, 256 to 511, ...) at most 10 rows name the same one
- route_weights: float32 [16384, 4], P(('section', 'expert')), may hold values from 0.05 to 0.6
- w_gate_up: bfloat16 [128, 5120, 1536], P(('section', 'expert'), 'dp'), may hold values from -0.078125 to 0.078125
- w_down: bfloat16 [128, 768, 5120], P(('section', 'expert'), None, 'dp'), may hold values from -0.21875 to 0.21875
- w_latent: bfloat16 [5120, 512], P('dp'), may hold values from -0.078125 to 0.078125
- latent_gain: float32 [512], replicated, may hold values from 0.5 to 1.5
- lengths: int32 [64, 16], P(('section', 'expert')), may hold values from 1 to 32, 256 in all within a row
- placement: int32 [64, 16], P(('section', 'expert')), may hold values from 0 to 15, each once within a row
Outputs:
- mixed_out: bfloat16 [16384, 5120], P(('section', 'expert'), 'dp')
- latent_cache: bfloat16 [16, 64, 32, 512], P('dp', ('section', 'expert'))
Inputs may be any that keep to these rules, and one draw needn't show every extreme that they name: `routes`: in each aligned block of 256 rows (the rows of one row group) no expert is named more than 10 times, a bound that some block reaches. `lengths`: each row sums to 256 and its largest entry is exactly 32. `placement`: each row holds every number of 0 to 15 once.
All inputs are finite; a program needn't handle non-finite values.
Results may differ from a plain program's by a relative error of at most 0.029.
Values may be sent and summed in bfloat16 or wider, within the bound.
No kernel may reach another device: no remote copies, remote signals or barrier semaphores. Data moves between devices by JAX's collectives and lax.ppermute only.
A program may use at most 32 MiB of HBM per device.

v0:
```python
import jax
import jax.numpy as jnp
from jax import lax
from jax.sharding import PartitionSpec as P


def body(
    tokens, routes, route_weights, w_gate_up, w_down, w_latent, latent_gain, lengths, placement
):
    group_count = lax.axis_size(("section", "expert"))
    block_count = lax.axis_size("dp")
    tok_rows = tokens.shape[0]
    width_share = tokens.shape[1]
    top_routes = routes.shape[1]
    local_experts = w_gate_up.shape[0]
    hidden_units = w_down.shape[1]
    latent_width = w_latent.shape[1]
    all_experts = local_experts * group_count
    capacity = 5 * tok_rows * top_routes // (4 * all_experts)
    longest = 2 * tok_rows // block_count
    route_ids = routes.reshape(-1)
    one_hot = (route_ids[:, None] == jnp.arange(all_experts, dtype=jnp.int32)[None, :]).astype(
        jnp.int32
    )
    earlier = jnp.cumsum(one_hot, axis=0) - one_hot
    slot_rank = jnp.sum(earlier * one_hot, axis=1)
    target = route_ids // local_experts
    resident = route_ids % local_experts
    flat_index = (resident * group_count + target) * capacity + slot_rank
    token_index = jnp.arange(route_ids.shape[0], dtype=jnp.int32) // top_routes
    outgoing = jnp.zeros((local_experts * group_count * capacity, width_share), tokens.dtype)
    outgoing = outgoing.at[flat_index].set(tokens[token_index])
    outgoing = outgoing.reshape(local_experts, group_count, capacity, width_share)
    arrived = lax.all_to_all(
        outgoing, ("section", "expert"), split_axis=1, concat_axis=1, tiled=True
    )
    expert_rows = arrived.reshape(local_experts, group_count * capacity, width_share)
    projections = jnp.einsum(
        "erd,edf->erf", expert_rows, w_gate_up, preferred_element_type=jnp.float32
    )
    projections = projections.reshape(-1, 2 * hidden_units)
    partial_latent = jnp.dot(tokens, w_latent, preferred_element_type=jnp.float32)
    length_row = lengths[0]
    request_order = placement[0]
    offsets = jnp.cumsum(length_row) - length_row
    select = (request_order[:, None] == jnp.arange(block_count, dtype=jnp.int32)[None, :]).astype(
        jnp.int32
    )
    starts = jnp.sum(select * offsets[None, :], axis=1)
    span_list = jnp.sum(select * length_row[None, :], axis=1)
    positions = jnp.arange(longest, dtype=jnp.int32)
    instance = lax.axis_index("dp")
    own_pick = (jnp.arange(block_count, dtype=jnp.int32) == instance).astype(jnp.int32)
    own_span = jnp.sum(own_pick * span_list)
    rows_index = jnp.clip(starts[:, None] + positions[None, :], 0, tok_rows - 1)
    live_all = positions[None, :] < span_list[:, None]
    padded = jnp.where(live_all[:, :, None], partial_latent[rows_index], 0.0)
    shares, received = (
        lax.psum_scatter(
            projections.astype(jnp.bfloat16), "dp", scatter_dimension=0, tiled=True
        ).astype(jnp.float32),
        lax.psum_scatter(padded.astype(jnp.bfloat16), "dp", scatter_dimension=0, tiled=True).astype(
            jnp.float32
        ),
    )
    latent_rows = received[0]
    hidden = (jax.nn.silu(shares[:, :hidden_units]) * shares[:, hidden_units:]).astype(jnp.bfloat16)
    gathered = lax.all_gather(hidden, "dp", axis=0, tiled=True)
    gathered = gathered.reshape(local_experts, group_count * capacity, hidden_units)
    produced = jnp.einsum(
        "erf,efd->erd", gathered, w_down, preferred_element_type=jnp.float32
    ).astype(jnp.bfloat16)
    produced = produced.reshape(local_experts, group_count, capacity, width_share)
    returned = lax.all_to_all(
        produced, ("section", "expert"), split_axis=1, concat_axis=1, tiled=True
    )
    per_route = returned.reshape(-1, width_share)[flat_index].reshape(
        tok_rows, top_routes, width_share
    )
    mixed_out = jnp.sum(route_weights[:, :, None] * per_route.astype(jnp.float32), axis=1).astype(
        jnp.bfloat16
    )
    live_rows = positions < own_span
    inverse_rms = lax.rsqrt(jnp.mean(latent_rows * latent_rows, axis=1, keepdims=True) + 1e-06)
    latent_cache = jnp.where(
        live_rows[:, None], latent_rows * inverse_rms * latent_gain, 0.0
    ).astype(jnp.bfloat16)
    return (mixed_out, latent_cache.reshape(1, 1, longest, latent_width))


def solution(mesh):
    return jax.shard_map(
        body,
        mesh=mesh,
        in_specs=(
            P(("section", "expert"), "dp"),
            P(("section", "expert"), None),
            P(("section", "expert"), None),
            P(("section", "expert"), "dp", None),
            P(("section", "expert"), None, "dp"),
            P("dp", None),
            P(),
            P(("section", "expert"), None),
            P(("section", "expert"), None),
        ),
        out_specs=(P(("section", "expert"), "dp"), P("dp", ("section", "expert"), None, None)),
        check_vma=False,
    )
```

profile of v0, /device:TPU:2, one launch (start us, length us, event | category | flops | bytes accessed | tf_op | source)
XLA Modules:
  0.0 506.2 jit_solution(17605061633849373091)
XLA Ops:
  7.2 1.0 copy.38
  8.7 0.2 fusion.5
  9.3 0.4 fusion.4
  9.7 9.9 %scatter_custom_fusion = bf16[1280,320]{1,0:T(8,128)(2,1)} fusion(s32[1024]{0:T(1024)S(1)} %bitcast.44, bf16[256,320]{1,0:T(8,128)(2,1)S(1)} %copy.43, s32[1024]{0:T(1024)S(1)} %broadcast_clamp_fusion.1, bf16[]{:T(256)} %constant.63.clone.1), kind=kCustom, calls=%fused_computation.9 | custom fusion | bytes 819202 | tf_op jit(solution)/shard_map/scatter | solution.py:32
  19.6 2.3 reshape.374
  21.9 1.0 copy.44
  22.9 119.3 %all_to_all.10 = bf16[2,64,10,320]{3,0,2,1:T(2,128)(2,1)S(1)} all-to-all(bf16[2,64,10,320]{3,0,2,1:T(2,128)(2,1)S(1)} %copy.44), channel_id=1, replica_groups=mesh['section'=2,'dp'=16,'expert'=32] {'section','expert'}, dimensions={1} | all-to-all | bytes 1638400 | tf_op jit(solution)/shard_map/all_to_all | solution.py:34
  142.2 4.1 convolution_convert_fusion
  146.3 108.8 %reduce-scatter.5.cloned.1.call-done = bf16[80,1536]{1,0:T(8,128)(2,1)} async-done(((bf16[1280,1536]{1,0:T(8,128)(2,1)}), bf16[80,1536]{1,0:T(8,128)(2,1)}) %reduce-scatter.5.cloned.1.call-update) | async-done | bytes 245776 | tf_op jit(solution)/shard_map/reduce_scatter | solution.py:59
  255.1 1.0 convert_element_type.53
  256.1 0.7 fusion.9
  256.8 83.0 %all-gather.2.cloned.1.call-done = bf16[1280,768]{1,0:T(8,128)(2,1)} async-done(((bf16[80,768]{1,0:T(8,128)(2,1)}), bf16[1280,768]{1,0:T(8,128)(2,1)}) %all-gather.2.cloned.1.call-update) | async-done | bytes 1966096 | tf_op jit(solution)/shard_map/all_gather | solution.py:68
  339.8 2.7 convolution_convert_fusion.1
  342.6 2.6 copy.46
  345.2 23.5 %all-to-all-start.1 = ((bf16[2,64,10,320]{3,0,2,1:T(2,128)(2,1)}), bf16[2,64,10,320]{3,0,2,1:T(2,128)(2,1)S(1)}, u32[]{:S(2)}, u32[]{:S(2)}) async-start(bf16[2,64,10,320]{3,0,2,1:T(2,128)(2,1)} %bitcast.9), calls=%async_computation.2 | async-start | bytes 1966080 | tf_op jit(solution)/shard_map/all_to_all | solution.py:74
  368.7 0.2 reduce-scatter.7.cloned.1.call-start
  369.0 0.2 reduce-window_2_clone.1
  369.5 1.3 fusion.18
  370.9 2.6 gather_fusion.1
  373.6 2.0 select_convert_fusion
  375.6 0.8 copy.37
  376.4 0.6 fusion.17
  377.1 0.6 iota_compare_fusion.5
  377.7 104.7 %reduce-scatter.7.cloned.1.call-done = bf16[1,32,512]{2,1,0:T(8,128)(2,1)} async-done(((bf16[16,32,512]{2,1,0:T(8,128)(2,1)}), bf16[1,32,512]{2,1,0:T(8,128)(2,1)}) %reduce-scatter.7.cloned.1.call-update) | async-done | bytes 32784
  482.5 0.9 fusion.14
  483.4 1.5 fusion.13
  484.8 1.4 copy.47
  486.2 2.4 reshape.378
  488.6 5.0 gather_fusion
  493.6 1.7 reshape.379
  495.3 2.6 multiply_reduce_fusion
  497.9 1.7 copy.48
  (41 shorter events, 1.5 us)
Async XLA Ops:
  7.2 135.0 %copy-start = (bf16[2,320,1536]{2,1,0:T(8,128)(2,1)S(1)}, bf16[2,320,1536]{2,1,0:T(8,128)(2,1)}, u32[]{:S(2)}) copy-start(bf16[2,320,1536]{2,1,0:T(8,128)(2,1)} %param.12) | copy-start | bytes 5898244
  7.2 1.9 copy-start.1
  7.2 247.9 %reduce-scatter.5.cloned.1.call-start = ((), (), s32[]{:S(2)}) async-start(), calls=%async_computation.4 | async-start | bytes 4177920 | tf_op jit(solution)/shard_map/reduce_scatter | solution.py:59
  146.3 193.5 %all-gather.2.cloned.1.call-start = ((), (), s32[]{:S(2)}) async-start(), calls=%async_computation.5 | async-start | bytes 2088960 | tf_op jit(solution)/shard_map/all_gather | solution.py:68
  342.5 26.4 %copy-start.5 = (s32[1,16]{1,0:T(1,128)S(1)}, s32[1,16]{1,0:T(1,128)}, u32[]{:S(2)}) copy-start(s32[1,16]{1,0:T(1,128)} %param.16) | copy-start | bytes 196
  342.6 26.6 %copy-start.6 = (s32[1,16]{1,0:T(1,128)S(1)}, s32[1,16]{1,0:T(1,128)}, u32[]{:S(2)}) copy-start(s32[1,16]{1,0:T(1,128)} %param.17) | copy-start | bytes 196
  342.6 27.0 %copy-start.2 = (bf16[256,320]{0,1:T(8,128)(2,1)S(1)}, bf16[256,320]{0,1:T(8,128)(2,1)}, u32[]{:S(2)}) copy-start(bf16[256,320]{0,1:T(8,128)(2,1)} %param.9) | copy-start | bytes 491524
  345.2 139.6 %all-to-all-start.1 = ((bf16[2,64,10,320]{3,0,2,1:T(2,128)(2,1)}), bf16[2,64,10,320]{3,0,2,1:T(2,128)(2,1)S(1)}, u32[]{:S(2)}, u32[]{:S(2)}) async-start(bf16[2,64,10,320]{3,0,2,1:T(2,128)(2,1)} %bitcast.9), calls=%async_computation.2 | async-start | bytes 1966080 | tf_op jit(solution)/shard_map/all_to_all | solution.py:74
  368.7 113.7 %reduce-scatter.7.cloned.1.call-start = ((), (), s32[]{:S(2)}) async-start(), calls=%async_computation.6 | async-start | bytes 557056
  370.8 4.8 copy-start.3
  370.8 112.5 %copy-start.4 = (f32[512]{0:T(512)S(1)}, f32[512]{0:T(512)}, u32[]{:S(2)}) copy-start(f32[512]{0:T(512)} %param.15) | copy-start | bytes 6148
Sparse Core Ops, SparseCore 0:
  146.4 108.6 reduce-scatter.4
  259.9 79.8 all-gather.1
  375.7 106.6 reduce-scatter.6
where the time goes:
time: 507 us; the launch traced here: 506 us
  waiting for transfers between devices  297 us (59%)
  blocking collectives  119 us (23%)
  local copies, waits for them, and re-layouts  33.2 us (7%)
  starting transfers between devices  23.8 us (5%)
  between operations  14 us (3%)
  other arithmetic  11.2 us (2%)
  matrix products  8.11 us (2%)
    all_to_all x1, blocking collectives, body(): lax.all_to_all(outgoing, ('section', 'expert'), split_axis=1, concat_axis...  119 us
    reduce_scatter x1, waiting for transfers between devices, body(): lax.psum_scatter(projections.astype(jnp.bfloat16), 'dp', scatter_dimensio...  109 us
    unnamed x4, waiting for transfers between devices  105 us
    all_gather x1, waiting for transfers between devices, body(): gathered = lax.all_gather(hidden, 'dp', axis=0, tiled=True)  83 us
    all_to_all x1, starting transfers between devices, body(): lax.all_to_all(produced, ('section', 'expert'), split_axis=1, concat_axis...  23.5 us
  transfers between devices with their start and end apart: 4, of which 3 were waited for; matrix products, arithmetic and copies ran while one was open for 2% of the time, Pallas kernels for 0%

commit v1 on v0

v1 whole, which is shorter than its diff:
```python
import functools

import jax
import jax.numpy as jnp
from jax import lax
from jax.experimental import pallas as pl
from jax.experimental.pallas import tpu as pltpu
from jax.sharding import PartitionSpec as P

SE = ("section", "expert")
NT = (((1,), (1,)), ((), ()))
TN = (((0,), (0,)), ((), ()))
BF = jnp.bfloat16
F32 = jnp.float32


def call(kernel, out_shape, *args, in_specs=None, scratch=(), flops=0, moved=0):
    kwargs = {}
    if in_specs is not None:
        kwargs["in_specs"] = in_specs
        kwargs["grid"] = (1,)
    return pl.pallas_call(
        kernel,
        out_shape=out_shape,
        scratch_shapes=list(scratch),
        cost_estimate=pl.CostEstimate(flops=flops, bytes_accessed=moved, transcendentals=0),
        compiler_params=pltpu.CompilerParams(vmem_limit_bytes=24 * 1024 * 1024),
        **kwargs,
    )(*args)


def iota(shape, dim):
    return lax.broadcasted_iota(jnp.int32, shape, dim)


def named_and_rank(routes_t, experts):
    tops, rows = routes_t.shape
    ids = iota((experts, rows), 0)
    named = jnp.zeros((experts, rows), F32)
    for k in range(tops):
        named = named + jnp.where(routes_t[k : k + 1, :] == ids, 1.0, 0.0)
    earlier = (iota((rows, rows), 0) < iota((rows, rows), 1)).astype(F32).astype(BF)
    rank = jnp.dot(named.astype(BF), earlier, preferred_element_type=F32)
    return named, rank


def spread(experts, resident):
    row, col = iota((experts, experts), 0), iota((experts, experts), 1)
    return (col == row - (row & 1) + resident).astype(F32).astype(BF)


def slot_masks(named, rank, resident, lanes):
    experts, rows = named.shape
    pick = spread(experts, resident)
    named_s = jnp.dot(pick, named.astype(BF), preferred_element_type=F32)
    rank_s = jnp.dot(pick, rank.astype(BF), preferred_element_type=F32)
    base = ((iota((experts, rows), 0) & 1) * lanes).astype(F32)
    return [(named_s > 0.5) & (rank_s == base + float(i)) for i in range(lanes)]


def dispatch_kernel(residents, lanes, routes_ref, tokens_ref, out):
    width = tokens_ref.shape[0]
    named, rank = named_and_rank(routes_ref[...], out.shape[0])
    for r in range(residents):
        for i, mask in enumerate(slot_masks(named, rank, r, lanes)):
            rows = lax.dot_general(
                mask.astype(F32).astype(BF), tokens_ref[...], NT, preferred_element_type=F32
            )
            at = (r * lanes + i) * width
            out[:, at : at + width] = rows.astype(BF)


def weights_kernel(residents, lanes, routes_ref, weights_ref, high_ref, low_ref):
    experts = high_ref.shape[1]
    routes_t, weights_t = routes_ref[...], weights_ref[...]
    named, rank = named_and_rank(routes_t, experts)
    ids = iota(named.shape, 0)
    gates = jnp.zeros(named.shape, F32)
    for k in range(routes_t.shape[0]):
        gates = gates + jnp.where(routes_t[k : k + 1, :] == ids, weights_t[k : k + 1, :], 0.0)
    high = gates.astype(BF)
    low = (gates - high.astype(F32)).astype(BF)
    for r in range(residents):
        pick = spread(experts, r)
        high_s = jnp.dot(pick, high, preferred_element_type=F32)
        low_s = jnp.dot(pick, low, preferred_element_type=F32)
        for i, mask in enumerate(slot_masks(named, rank, r, lanes)):
            high_ref[r * lanes + i] = jnp.where(mask, high_s, 0.0).astype(BF)
            low_ref[r * lanes + i] = jnp.where(mask, low_s, 0.0).astype(BF)


def up_kernel(lanes, rows_ref, weight_ref, out, packed):
    slots = rows_ref.shape[0]
    residents, width, columns = weight_ref.shape
    each = lanes * slots
    step = 512 if columns % 512 == 0 else columns
    for r in range(residents):
        for i in range(lanes):
            at = (r * lanes + i) * width
            packed[i * slots : (i + 1) * slots, :] = rows_ref[:, at : at + width]
        for c in range(0, columns, step):
            part = jnp.dot(
                packed[...], weight_ref[r, :, c : c + step], preferred_element_type=F32
            )
            out[r * each : (r + 1) * each, c : c + step] = part.astype(BF)


def hidden_kernel(parts_ref, out):
    blocks = parts_ref.shape[0]
    half = out.shape[2]
    total = parts_ref[0].astype(F32)
    for b in range(1, blocks):
        total = total + parts_ref[b].astype(F32)
    gate, up = total[:, :half], total[:, half:]
    hidden = (gate / (1.0 + jnp.exp(-gate)) * up).astype(BF)
    for b in range(blocks):
        out[b] = hidden


def down_kernel(lanes, hidden_ref, weight_ref, out):
    slots = out.shape[0]
    residents, width, _ = weight_ref.shape
    each = lanes * slots
    for r in range(residents):
        part = lax.dot_general(
            hidden_ref[r * each : (r + 1) * each, :],
            weight_ref[r],
            NT,
            preferred_element_type=F32,
        ).astype(BF)
        for i in range(lanes):
            at = (r * lanes + i) * width
            out[:, at : at + width] = part[i * slots : (i + 1) * slots, :]


def mix_kernel(back_ref, high_ref, low_ref, out):
    width = out.shape[0]
    total = jnp.zeros(out.shape, F32)
    for i in range(high_ref.shape[0]):
        rows = back_ref[:, i * width : (i + 1) * width]
        total = total + lax.dot_general(rows, high_ref[i], TN, preferred_element_type=F32)
        total = total + lax.dot_general(rows, low_ref[i], TN, preferred_element_type=F32)
    out[...] = total.astype(BF)


def latent_kernel(longest, lengths_ref, placement_ref, tokens_ref, weight_ref, out, select, offset):
    requests = lengths_ref.shape[1]
    rows = tokens_ref.shape[1]
    partial = lax.dot_general(tokens_ref[...], weight_ref[...], TN, preferred_element_type=F32)
    run = jnp.int32(0)
    for j in range(requests):
        offset[j] = run
        run = run + lengths_ref[0, j]
    place, position = iota((longest, rows), 0), iota((longest, rows), 1)
    for q in range(requests):
        request = placement_ref[0, q]
        hit = (position == place + offset[request]) & (place < lengths_ref[0, request])
        select[q * longest : (q + 1) * longest, :] = hit.astype(F32).astype(BF)
    picked = jnp.dot(select[...], partial.astype(BF), preferred_element_type=F32)
    out[...] = picked.astype(BF)


def norm_kernel(sum_ref, gain_ref, out):
    total = sum_ref[...].astype(F32)
    scale = lax.rsqrt(jnp.mean(total * total, axis=1, keepdims=True) + 1e-06)
    out[...] = (total * scale * gain_ref[...]).astype(BF)


def exchange(x, axes):
    return lax.all_to_all(x, axes, split_axis=0, concat_axis=0, tiled=True)


def body(
    tokens, routes, route_weights, w_gate_up, w_down, w_latent, latent_gain, lengths, placement
):
    groups = lax.axis_size(SE)
    blocks = lax.axis_size("dp")
    rows, width = tokens.shape
    tops = routes.shape[1]
    residents = w_gate_up.shape[0]
    hidden_units = w_down.shape[1]
    latent_width = w_latent.shape[1]
    experts = residents * groups
    capacity = 5 * rows * tops // (4 * experts)
    lanes = capacity // 2
    slots = 2 * groups
    longest = 2 * rows // blocks
    total_slots = experts * capacity
    share = total_slots // blocks
    row = residents * lanes * width
    shape = jax.ShapeDtypeStruct
    tokens_t, routes_t, gates_t = tokens.T, routes.T, route_weights.T
    down_t = w_down.transpose(0, 2, 1)
    vmem = pl.BlockSpec(memory_space=pltpu.VMEM)
    smem = pl.BlockSpec(memory_space=pltpu.SMEM)

    with jax.named_scope("dispatch"):
        outgoing = call(
            functools.partial(dispatch_kernel, residents, lanes),
            shape((slots, row), BF),
            routes_t,
            tokens_t,
            flops=2 * rows * width * total_slots,
            moved=2 * total_slots * width,
        )
        arrived = exchange(outgoing.reshape(groups, 2, row), SE).reshape(slots, row)

    with jax.named_scope("latent"):
        picked = call(
            functools.partial(latent_kernel, longest),
            shape((blocks * longest, latent_width), BF),
            lengths,
            placement,
            tokens_t,
            w_latent,
            in_specs=[smem, smem, vmem, vmem],
            scratch=[
                pltpu.VMEM((blocks * longest, rows), BF),
                pltpu.SMEM((blocks,), jnp.int32),
            ],
            flops=2 * rows * latent_width * (width + blocks * longest),
            moved=2 * latent_width * (width + blocks * longest),
        )
        summed = lax.psum_scatter(picked, "dp", scatter_dimension=0, tiled=True)
    with jax.named_scope("up"):
        partial = call(
            functools.partial(up_kernel, lanes),
            shape((total_slots, 2 * hidden_units), BF),
            arrived,
            w_gate_up,
            scratch=[pltpu.VMEM((lanes * slots, width), BF)],
            flops=4 * total_slots * width * hidden_units,
            moved=4 * hidden_units * (residents * width + total_slots),
        )
        shares = exchange(partial.reshape(blocks, share, 2 * hidden_units), "dp")
        shares, summed = lax.optimization_barrier((shares, summed))

    with jax.named_scope("latent"):
        latent_cache = call(
            norm_kernel,
            shape((longest, latent_width), BF),
            summed,
            latent_gain.reshape(1, latent_width),
            flops=8 * longest * latent_width,
            moved=4 * longest * latent_width,
        )

    with jax.named_scope("gates"):
        gates = call(
            functools.partial(weights_kernel, residents, lanes),
            [shape((residents * lanes, slots, rows), BF)] * 2,
            routes_t,
            gates_t,
            flops=8 * experts * experts * rows,
            moved=8 * lanes * slots * rows,
        )

    with jax.named_scope("hidden"):
        hidden = call(
            hidden_kernel,
            shape((blocks, share, hidden_units), BF),
            shares,
            flops=2 * total_slots * hidden_units,
            moved=6 * total_slots * hidden_units,
        )
        gathered = exchange(hidden, "dp")
    with jax.named_scope("down"):
        produced = call(
            functools.partial(down_kernel, lanes),
            shape((slots, row), BF),
            gathered.reshape(total_slots, hidden_units),
            down_t,
            flops=2 * total_slots * width * hidden_units,
            moved=2 * hidden_units * (residents * width + total_slots),
        )
        back = exchange(produced.reshape(groups, 2, row), SE).reshape(slots, row)

    with jax.named_scope("mix"):
        mixed = call(
            mix_kernel,
            shape((width, rows), BF),
            back,
            *gates,
            flops=4 * total_slots * width * rows,
            moved=2 * total_slots * (width + 2 * rows),
        )
    return (mixed.T, latent_cache.reshape(1, 1, longest, latent_width))


def solution(mesh):
    return jax.shard_map(
        body,
        mesh=mesh,
        in_specs=(
            P(SE, "dp"),
            P(SE, None),
            P(SE, None),
            P(SE, "dp", None),
            P(SE, None, "dp"),
            P("dp", None),
            P(),
            P(SE, None),
            P(SE, None),
        ),
        out_specs=(P(SE, "dp"), P("dp", SE, None, None)),
        check_vma=False,
    )
```

time: 507 us -> 407 us (0.80)
  the two profiles are of different devices: /device:TPU:2 before, /device:TPU:96 now
where the time goes in v1:
time: 407 us
  waiting for transfers between devices  197 us (48%)
  blocking collectives  144 us (35%)
  starting transfers between devices  30.7 us (8%)
  between operations  14.2 us (3%)
  Pallas kernels  12.4 us (3%)
  local copies, waits for them, and re-layouts  7.64 us (2%)
    all_to_all x2, blocking collectives, exchange(): return lax.all_to_all(x, axes, split_axis=0, concat_axis=0, tiled=True)  144 us
    reduce_scatter x1, waiting for transfers between devices, body(): summed = lax.psum_scatter(picked, 'dp', scatter_dimension=0, tiled=True)  113 us
    all_to_all x2, waiting for transfers between devices, exchange(): return lax.all_to_all(x, axes, split_axis=0, concat_axis=0, tiled=True)  84.9 us
    all_to_all x2, starting transfers between devices, exchange(): return lax.all_to_all(x, axes, split_axis=0, concat_axis=0, tiled=True)  30.6 us
    pallas_call x8, Pallas kernels, call(): pl.pallas_call(kernel, out_shape=out_shape, scratch_shapes=list(scratch),...  12.4 us
  transfers between devices with their start and end apart: 3, of which 2 were waited for; matrix products, arithmetic and copies ran while one was open for 0% of the time, Pallas kernels for 1%

profile of v1, /device:TPU:96, one launch (start us, length us, event | category | flops | bytes accessed | tf_op | source)
XLA Modules:
  0.0 406.5 jit_solution(6236011207028861110)
XLA Ops:
  7.2 0.0 copy-start.3
  7.2 0.9 copy-done.3
  8.1 0.7 copy-done.7
  8.8 1.2 dispatch.1
  10.0 0.3 reshape.28
  10.3 0.0 copy-start.1
  10.3 114.4 %all_to_all.20 = bf16[64,2,3200]{2,1,0:T(2,128)(2,1)} all-to-all(bf16[64,2,3200]{2,1,0:T(2,128)(2,1)S(1)} %reshape.28), channel_id=1, replica_groups=mesh['section'=2,'dp'=16,'expert'=32] {'section','expert'}, dimensions={0} | all-to-all | bytes 1638400 | tf_op jit(solution)/shard_map/dispatch/all_to_all | solution.py:170
  124.7 2.3 reshape.29.rows_ref
  127.1 0.0 copy-done.1
  127.1 2.2 up.1
  129.3 0.0 copy-start
  129.3 1.9 copy-done
  131.2 7.2 %all-to-all-start.1 = ((bf16[16,80,1536]{2,1,0:T(8,128)(2,1)}), bf16[16,80,1536]{2,1,0:T(8,128)(2,1)}, u32[]{:S(2)}, u32[]{:S(2)}) async-start(bf16[16,80,1536]{2,1,0:T(8,128)(2,1)} %bitcast.9), calls=%async_computation.1 | async-start | bytes 7864320 | tf_op jit(solution)/shard_map/up/all_to_all | solution.py:170
  138.4 0.0 reduce-scatter.2.cloned.1.call-start
  138.5 2.0 latent.2
  140.5 0.0 reduce-scatter.2.cloned.1.call-update
  140.5 112.5 %reduce-scatter.2.cloned.1.call-done.sum_ref = bf16[32,512]{1,0:T(8,128)(2,1)} async-done(((bf16[512,512]{1,0:T(8,128)(2,1)}), bf16[32,512]{1,0:T(8,128)(2,1)}) %reduce-scatter.2.cloned.1.call-update) | async-done | bytes 32784 | tf_op jit(solution)/shard_map/latent/reduce_scatter | solution.py:224
  253.1 0.0 all-to-all-done.1.parts_ref
  253.1 2.7 hidden.1
  255.7 0.0 copy-start.2
  255.8 29.7 %all_to_all.21 = bf16[16,80,768]{2,1,0:T(8,128)(2,1)S(1)} all-to-all(bf16[16,80,768]{2,1,0:T(8,128)(2,1)S(1)} %hidden.1), channel_id=1, replica_groups=mesh['section'=2,'dp'=16,'expert'=32] {'dp'}, dimensions={0} | all-to-all | bytes 3932160 | tf_op jit(solution)/shard_map/hidden/all_to_all | solution.py:170
  285.4 1.2 down.1
  286.7 0.0 copy-start.8
  286.7 0.0 copy-start.12
  286.7 0.0 copy-start.9
  286.7 1.2 reshape.32
  287.9 23.4 %all-to-all-start.3 = ((bf16[64,2,3200]{2,1,0:T(2,128)(2,1)}), bf16[64,2,3200]{2,1,0:T(2,128)(2,1)S(1)}, u32[]{:S(2)}, u32[]{:S(2)}) async-start(bf16[64,2,3200]{2,1,0:T(2,128)(2,1)} %reshape.32), calls=%async_computation.4 | async-start | bytes 1638400 | tf_op jit(solution)/shard_map/down/all_to_all | solution.py:170
  311.3 0.6 gates.1
  312.0 0.7 latent.3
  312.7 84.9 %all-to-all-done.3 = bf16[64,2,3200]{2,1,0:T(2,128)(2,1)S(1)} async-done(((bf16[64,2,3200]{2,1,0:T(2,128)(2,1)}), bf16[64,2,3200]{2,1,0:T(2,128)(2,1)S(1)}, u32[]{:S(2)}, u32[]{:S(2)}) %all-to-all-start.3) | async-done | bytes 819232 | tf_op jit(solution)/shard_map/down/all_to_all | solution.py:170
  397.6 0.3 reshape.33.back_ref
  397.9 1.8 mix.1
  (15 shorter events, 0.0 us)
Async XLA Ops:
  7.2 0.9 copy-start.3
  8.1 0.7 copy-start.7
  10.3 116.8 %copy-start.1 = (bf16[2,320,1536]{2,1,0:T(8,128)(2,1)S(1)}, bf16[2,320,1536]{2,1,0:T(8,128)(2,1)}, u32[]{:S(2)}) copy-start(bf16[2,320,1536]{2,1,0:T(8,128)(2,1)} %weight_ref.2) | copy-start | bytes 5898244
  129.3 1.9 copy-start
  131.2 7.3 %copy-start.4 = (bf16[256,320]{0,1:T(8,128)(2,1)S(1)}, bf16[256,320]{0,1:T(8,128)(2,1)}, u32[]{:S(2)}) copy-start(bf16[256,320]{0,1:T(8,128)(2,1)} %param.9) | copy-start | bytes 491524
  131.2 7.3 %copy-start.5 = (bf16[320,512]{1,0:T(8,128)(2,1)S(1)}, bf16[320,512]{1,0:T(8,128)(2,1)}, u32[]{:S(2)}) copy-start(bf16[320,512]{1,0:T(8,128)(2,1)} %weight_ref.3) | copy-start | bytes 983044
  131.2 7.3 %copy-start.10 = (s32[1,16]{1,0:T(1,128)S(1)}, s32[1,16]{1,0:T(1,128)}, u32[]{:S(2)}) copy-start(s32[1,16]{1,0:T(1,128)} %lengths_ref.1) | copy-start | bytes 196
  131.2 7.3 %copy-start.11 = (s32[1,16]{1,0:T(1,128)S(1)}, s32[1,16]{1,0:T(1,128)}, u32[]{:S(2)}) copy-start(s32[1,16]{1,0:T(1,128)} %placement_ref.1) | copy-start | bytes 196
  131.2 121.9 %all-to-all-start.1 = ((bf16[16,80,1536]{2,1,0:T(8,128)(2,1)}), bf16[16,80,1536]{2,1,0:T(8,128)(2,1)}, u32[]{:S(2)}, u32[]{:S(2)}) async-start(bf16[16,80,1536]{2,1,0:T(8,128)(2,1)} %bitcast.9), calls=%async_computation.1 | async-start | bytes 7864320 | tf_op jit(solution)/shard_map/up/all_to_all | solution.py:170
  138.4 114.6 %reduce-scatter.2.cloned.1.call-start = ((), (), s32[]{:S(2)}) async-start(), calls=%async_computation.5 | async-start | bytes 557056 | tf_op jit(solution)/shard_map/latent/reduce_scatter | solution.py:224
  255.7 29.7 %copy-start.2 = (bf16[2,768,320]{1,2,0:T(8,128)(2,1)S(1)}, bf16[2,768,320]{1,2,0:T(8,128)(2,1)}, u32[]{:S(2)}) copy-start(bf16[2,768,320]{1,2,0:T(8,128)(2,1)} %param.13) | copy-start | bytes 2949124
  286.7 24.6 %copy-start.8 = (s32[256,4]{0,1:T(4,128)S(1)}, s32[256,4]{0,1:T(4,128)}, u32[]{:S(2)}) copy-start(s32[256,4]{0,1:T(4,128)} %param.10) | copy-start | bytes 12292
  286.7 24.6 %copy-start.12 = (f32[256,4]{0,1:T(4,128)S(1)}, f32[256,4]{0,1:T(4,128)}, u32[]{:S(2)}) copy-start(f32[256,4]{0,1:T(4,128)} %param.11) | copy-start | bytes 12292
  286.7 25.3 %copy-start.6 = (bf16[32,512]{1,0:T(8,128)(2,1)S(1)}, bf16[32,512]{1,0:T(8,128)(2,1)}, u32[]{:S(2)}) copy-start(bf16[32,512]{1,0:T(8,128)(2,1)} %reduce-scatter.2.cloned.1.call-done.sum_ref) | copy-start | bytes 98308
  286.7 25.3 %copy-start.9 = (f32[512]{0:T(512)S(1)}, f32[512]{0:T(512)}, u32[]{:S(2)}) copy-start(f32[512]{0:T(512)} %param.15) | copy-start | bytes 6148
  287.9 109.7 %all-to-all-start.3 = ((bf16[64,2,3200]{2,1,0:T(2,128)(2,1)}), bf16[64,2,3200]{2,1,0:T(2,128)(2,1)S(1)}, u32[]{:S(2)}, u32[]{:S(2)}) async-start(bf16[64,2,3200]{2,1,0:T(2,128)(2,1)} %reshape.32), calls=%async_computation.4 | async-start | bytes 1638400 | tf_op jit(solution)/shard_map/down/all_to_all | solution.py:170
Sparse Core Ops, SparseCore 0:
  144.5 108.5 reduce-scatter.1

commit v2 on v1

v2 whole, which is shorter than its diff:
```python
import functools

import jax
import jax.numpy as jnp
from jax import lax
from jax.experimental import pallas as pl
from jax.experimental.pallas import tpu as pltpu
from jax.sharding import PartitionSpec as P

SE = ("section", "expert")
NT = (((1,), (1,)), ((), ()))
TN = (((0,), (0,)), ((), ()))
BF = jnp.bfloat16
F32 = jnp.float32


def call(kernel, out_shape, *args, in_specs=None, scratch=(), flops=0, moved=0):
    kwargs = {}
    if in_specs is not None:
        kwargs["in_specs"] = in_specs
        kwargs["grid"] = (1,)
    return pl.pallas_call(
        kernel,
        out_shape=out_shape,
        scratch_shapes=list(scratch),
        cost_estimate=pl.CostEstimate(flops=flops, bytes_accessed=moved, transcendentals=0),
        compiler_params=pltpu.CompilerParams(vmem_limit_bytes=24 * 1024 * 1024),
        **kwargs,
    )(*args)


def iota(shape, dim):
    return lax.broadcasted_iota(jnp.int32, shape, dim)


def slot_rows(routes, ids, half):
    named, rank = [], []
    for g, routes_t in enumerate(routes):
        tops, rows = routes_t.shape
        hits = jnp.zeros((ids.shape[0], rows), F32)
        for k in range(tops):
            hits = hits + jnp.where(routes_t[k : k + 1, :] == ids, 1.0, 0.0)
        hits = jnp.where(half == g, hits, 0.0)
        earlier = (iota((rows, rows), 0) < iota((rows, rows), 1)).astype(F32).astype(BF)
        named.append(hits)
        rank.append(jnp.dot(hits.astype(BF), earlier, preferred_element_type=F32))
    return jnp.concatenate(named, axis=1), jnp.concatenate(rank, axis=1)


def slot_masks(named, rank, lanes):
    base = ((iota(named.shape, 0) & 1) * lanes).astype(F32)
    return [(named > 0.5) & (rank == base + float(i)) for i in range(lanes)]


def half_of(slot_rows_count):
    return (iota((slot_rows_count, 1), 0) >> 2) & 1


def dispatch_kernel(lanes, ids_ref, own_ref, other_ref, own_tokens, other_tokens, *outs):
    width = own_tokens.shape[0]
    ids = ids_ref[...]
    named, rank = slot_rows((own_ref[...], other_ref[...]), ids, half_of(ids.shape[0]))
    both = jnp.concatenate([own_tokens[...], other_tokens[...]], axis=1)
    for i, mask in enumerate(slot_masks(named, rank, lanes)):
        rows = lax.dot_general(mask.astype(F32).astype(BF), both, NT, preferred_element_type=F32)
        for d, out in enumerate(outs):
            out[:, i * width : (i + 1) * width] = rows[d * 8 : d * 8 + 8, :].astype(BF)


def weights_kernel(lanes, ids_ref, own_ref, other_ref, own_gates, other_gates, high_ref, low_ref):
    ids = ids_ref[...]
    routes = (own_ref[...], other_ref[...])
    named, rank = slot_rows(routes, ids, half_of(ids.shape[0]))
    gates = []
    for routes_t, weights_t in zip(routes, (own_gates[...], other_gates[...])):
        total = jnp.zeros((ids.shape[0], routes_t.shape[1]), F32)
        for k in range(routes_t.shape[0]):
            hit = routes_t[k : k + 1, :] == ids
            total = total + jnp.where(hit, weights_t[k : k + 1, :], 0.0)
        gates.append(total)
    gates = jnp.concatenate(gates, axis=1)
    high = gates.astype(BF).astype(F32)
    low = gates - high
    for i, mask in enumerate(slot_masks(named, rank, lanes)):
        high_ref[i] = jnp.where(mask, high, 0.0).astype(BF)
        low_ref[i] = jnp.where(mask, low, 0.0).astype(BF)


def by_expert(count):
    a = iota((count, count), 1)
    to = ((a >> 1) & 1) * (count // 2) + (a >> 3) * 4 + ((a >> 2) & 1) * 2 + (a & 1)
    return (iota((count, count), 0) == to).astype(F32).astype(BF)


def up_kernel(lanes, *refs):
    blocks, (weight_ref, out, gathered, packed) = refs[:-4], refs[-4:]
    count = gathered.shape[0]
    residents, width, columns = weight_ref.shape
    each, half = out.shape[0] // residents, count // residents
    step = 512 if columns % 512 == 0 else columns
    for d, block in enumerate(blocks):
        gathered[d * 8 : d * 8 + 8, :] = block[...].astype(F32)
    rows = jnp.dot(by_expert(count), gathered[...].astype(BF), preferred_element_type=F32)
    rows = rows.astype(BF)
    for r in range(residents):
        for i in range(lanes):
            piece = rows[r * half : (r + 1) * half, i * width : (i + 1) * width]
            packed[i * half : (i + 1) * half, :] = piece
        for c in range(0, columns, step):
            part = jnp.dot(
                packed[...], weight_ref[r, :, c : c + step], preferred_element_type=F32
            )
            out[r * each : (r + 1) * each, c : c + step] = part.astype(BF)


def hidden_kernel(parts_ref, out):
    blocks = parts_ref.shape[0]
    half = out.shape[2]
    total = parts_ref[0].astype(F32)
    for b in range(1, blocks):
        total = total + parts_ref[b].astype(F32)
    gate, up = total[:, :half], total[:, half:]
    hidden = (gate / (1.0 + jnp.exp(-gate)) * up).astype(BF)
    for b in range(blocks):
        out[b] = hidden


def down_kernel(lanes, hidden_ref, weight_ref, *refs):
    outs, packed = refs[:-1], refs[-1]
    count = packed.shape[0]
    residents, width, _ = weight_ref.shape
    each, half = hidden_ref.shape[0] // residents, count // residents
    for r in range(residents):
        part = lax.dot_general(
            hidden_ref[r * each : (r + 1) * each, :],
            weight_ref[r],
            NT,
            preferred_element_type=F32,
        ).astype(BF)
        for i in range(lanes):
            piece = part[i * half : (i + 1) * half, :]
            packed[r * half : (r + 1) * half, i * width : (i + 1) * width] = piece
    rows = lax.dot_general(by_expert(count), packed[...], TN, preferred_element_type=F32)
    for d, out in enumerate(outs):
        out[...] = rows[d * 8 : d * 8 + 8, :].astype(BF)


def mix_kernel(lanes, last, *refs):
    if last:
        blocks, (high_ref, low_ref, before_ref, own_ref, other_ref, gathered) = refs[:-6], refs[-6:]
        total = before_ref[...]
    else:
        blocks, (high_ref, low_ref, out, gathered) = refs[:-4], refs[-4:]
        total = jnp.zeros(out.shape, F32)
    width = total.shape[0]
    for d, block in enumerate(blocks):
        gathered[d * 8 : d * 8 + 8, :] = block[...].astype(F32)
    for i in range(lanes):
        rows = gathered[:, i * width : (i + 1) * width].astype(BF)
        total = total + lax.dot_general(rows, high_ref[i], TN, preferred_element_type=F32)
        total = total + lax.dot_general(rows, low_ref[i], TN, preferred_element_type=F32)
    if last:
        tokens = own_ref.shape[1]
        own_ref[...] = total[:, :tokens]
        other_ref[...] = total[:, tokens:].astype(BF)
    else:
        out[...] = total


def join_kernel(own_ref, other_ref, out):
    out[...] = (own_ref[...] + other_ref[...].astype(F32)).astype(BF)


def latent_kernel(longest, lengths_ref, placement_ref, tokens_ref, weight_ref, out, select, offset):
    requests = lengths_ref.shape[1]
    rows = tokens_ref.shape[1]
    partial = lax.dot_general(tokens_ref[...], weight_ref[...], TN, preferred_element_type=F32)
    run = jnp.int32(0)
    for j in range(requests):
        offset[j] = run
        run = run + lengths_ref[0, j]
    place, position = iota((longest, rows), 0), iota((longest, rows), 1)
    for q in range(requests):
        request = placement_ref[0, q]
        hit = (position == place + offset[request]) & (place < lengths_ref[0, request])
        select[q * longest : (q + 1) * longest, :] = hit.astype(F32).astype(BF)
    picked = jnp.dot(select[...], partial.astype(BF), preferred_element_type=F32)
    out[...] = picked.astype(BF)


def norm_kernel(parts_ref, gain_ref, out):
    total = parts_ref[0].astype(F32)
    for b in range(1, parts_ref.shape[0]):
        total = total + parts_ref[b].astype(F32)
    scale = lax.rsqrt(jnp.mean(total * total, axis=1, keepdims=True) + 1e-06)
    out[...] = (total * scale * gain_ref[...]).astype(BF)


def exchange(x, axes):
    return lax.all_to_all(x, axes, split_axis=0, concat_axis=0, tiled=True)


def swap(x):
    return lax.ppermute(x, "section", [(0, 1), (1, 0)])


def shift(x, distance, size):
    if distance % size == 0:
        return x
    return lax.ppermute(x, "expert", [(i, (i + distance) % size) for i in range(size)])


def distances(size):
    order = sorted(range(-((size - 1) // 2), size // 2 + 1), key=lambda d: (-abs(d), -d))
    return [d for d in order if d % 2 == 0], [d for d in order if d % 2]


def body(
    tokens, routes, route_weights, w_gate_up, w_down, w_latent, latent_gain, lengths, placement
):
    sections, ring = lax.axis_size("section"), lax.axis_size("expert")
    groups = sections * ring
    blocks = lax.axis_size("dp")
    rows, width = tokens.shape
    tops = routes.shape[1]
    residents = w_gate_up.shape[0]
    hidden_units = w_down.shape[1]
    latent_width = w_latent.shape[1]
    experts = residents * groups
    capacity = 5 * rows * tops // (4 * experts)
    lanes = capacity // 2
    longest = 2 * rows // blocks
    row = lanes * width
    shape = jax.ShapeDtypeStruct
    tokens_t, routes_t, gates_t = tokens.T, routes.T, route_weights.T
    down_t = w_down.transpose(0, 2, 1)
    vmem = pl.BlockSpec(memory_space=pltpu.VMEM)
    smem = pl.BlockSpec(memory_space=pltpu.SMEM)
    chunks = distances(ring)
    slots = 4 * residents * len(chunks[0])
    total_slots = slots * lanes
    share = total_slots // blocks

    with jax.named_scope("swap"):
        other_tokens, other_routes, other_gates = swap(tokens_t), swap(routes_t), swap(gates_t)

    with jax.named_scope("dispatch"):
        here = lax.axis_index("expert")
        first = lax.axis_index("section") * (experts // sections)
        local = experts // sections
        ids, sent = [], []
        for chunk in chunks:
            relative = [residents * d + r for d in chunk for h in range(2) for r in (0, 1) for j in (0, 1)]
            relative = jnp.asarray(relative, jnp.int32)[:, None]
            ids.append(first + (relative + residents * here + local) % local)
        for chunk, of_rows in zip(chunks, ids):
            sent.append(
                call(
                    functools.partial(dispatch_kernel, lanes),
                    [shape((8, row), BF)] * len(chunk),
                    of_rows,
                    routes_t,
                    other_routes,
                    tokens_t,
                    other_tokens,
                    flops=4 * rows * width * total_slots,
                    moved=2 * total_slots * width,
                )
            )
        arrived = [
            [shift(x, d, ring) for x, d in zip(of_chunk, chunk)]
            for of_chunk, chunk in zip(sent, chunks)
        ]

    with jax.named_scope("gates"):
        gates = [
            call(
                functools.partial(weights_kernel, lanes),
                [shape((lanes, slots, 2 * rows), BF)] * 2,
                of_rows,
                routes_t,
                other_routes,
                gates_t,
                other_gates,
                flops=4 * slots * rows * rows,
                moved=8 * total_slots * rows,
            )
            for of_rows in ids
        ]

    def up(c):
        with jax.named_scope("up"):
            return call(
                functools.partial(up_kernel, lanes),
                shape((total_slots, 2 * hidden_units), BF),
                *arrived[c],
                w_gate_up,
                scratch=[
                    pltpu.VMEM((slots, row), F32),
                    pltpu.VMEM((total_slots // residents, width), BF),
                ],
                flops=4 * total_slots * width * hidden_units,
                moved=4 * hidden_units * (residents * width + total_slots),
            )

    def middle(partial, beside):
        cut = 5 * len(beside) // 8
        with jax.named_scope("hidden"):
            shares = exchange(partial.reshape(blocks, share, 2 * hidden_units), "dp")
            shares, beside[:cut] = lax.optimization_barrier((shares, beside[:cut]))
            hidden = call(
                hidden_kernel,
                shape((blocks, share, hidden_units), BF),
                shares,
                flops=2 * total_slots * hidden_units,
                moved=6 * total_slots * hidden_units,
            )
            gathered = exchange(hidden, "dp")
            gathered, beside[cut:] = lax.optimization_barrier((gathered, beside[cut:]))
        return gathered

    def down(c, gathered):
        with jax.named_scope("down"):
            produced = call(
                functools.partial(down_kernel, lanes),
                [shape((8, row), BF)] * len(chunks[c]),
                gathered.reshape(total_slots, hidden_units),
                down_t,
                scratch=[pltpu.VMEM((slots, row), BF)],
                flops=2 * total_slots * width * hidden_units,
                moved=2 * hidden_units * (residents * width + total_slots),
            )
            return [shift(x, -d, ring) for x, d in zip(produced, chunks[c])]

    def mix(c, back, before):
        last = before is not None
        whole = shape((width, 2 * rows), F32)
        ends = [shape((width, rows), F32), shape((width, rows), BF)]
        with jax.named_scope("mix"):
            return call(
                functools.partial(mix_kernel, lanes, last),
                ends if last else whole,
                *back,
                *gates[c],
                *([before] if last else []),
                scratch=[pltpu.VMEM((slots, row), F32)],
                flops=8 * total_slots * width * rows,
                moved=4 * total_slots * (width + 2 * rows),
            )

    gathered = middle(up(0), arrived[1])
    partial, gathered = lax.optimization_barrier((up(1), gathered))
    back = down(0, gathered)
    gathered = middle(partial, back)
    gathered, late_tokens = lax.optimization_barrier((gathered, tokens_t))

    with jax.named_scope("latent"):
        picked = call(
            functools.partial(latent_kernel, longest),
            shape((blocks * longest, latent_width), BF),
            lengths,
            placement,
            late_tokens,
            w_latent,
            in_specs=[smem, smem, vmem, vmem],
            scratch=[
                pltpu.VMEM((blocks * longest, rows), BF),
                pltpu.SMEM((blocks,), jnp.int32),
            ],
            flops=2 * rows * latent_width * (width + blocks * longest),
            moved=2 * latent_width * (width + blocks * longest),
        )
        received = exchange(picked.reshape(blocks, longest, latent_width), "dp")
        latent_cache = call(
            norm_kernel,
            shape((longest, latent_width), BF),
            received,
            latent_gain.reshape(1, latent_width),
            flops=blocks * longest * latent_width,
            moved=2 * blocks * longest * latent_width,
        )

    total = mix(0, back, None)
    total = mix(1, down(1, gathered), total)
    with jax.named_scope("join"):
        own, other = total
        mixed = call(
            join_kernel,
            shape((width, rows), BF),
            own,
            swap(other),
            flops=width * rows,
            moved=8 * width * rows,
        )
    return (mixed.T, latent_cache.reshape(1, 1, longest, latent_width))


def solution(mesh):
    return jax.shard_map(
        body,
        mesh=mesh,
        in_specs=(
            P(SE, "dp"),
            P(SE, None),
            P(SE, None),
            P(SE, "dp", None),
            P(SE, None, "dp"),
            P("dp", None),
            P(),
            P(SE, None),
            P(SE, None),
        ),
        out_specs=(P(SE, "dp"), P("dp", SE, None, None)),
        check_vma=False,
    )
```

time: 407 us -> 604 us (1.48)
  the two profiles are of different devices: /device:TPU:96 before, /device:TPU:1 now
where the time goes in v2:
time: 604 us; the launch traced here: 601 us
  starting transfers between devices  543 us (90%)
  local copies, waits for them, and re-layouts  24.6 us (4%)
  Pallas kernels  17.2 us (3%)
  waiting for transfers between devices  13.5 us (2%)
    ppermute x62, starting transfers between devices, shift(): lax.ppermute(x, 'expert', [(i, (i + distance) % size) for i in range(size)])  464 us
    ppermute x4, starting transfers between devices, swap(): return lax.ppermute(x, 'section', [(0, 1), (1, 0)])  45.3 us
    all_to_all x5, starting transfers between devices, exchange(): return lax.all_to_all(x, axes, split_axis=0, concat_axis=0, tiled=True)  33.8 us
    unnamed x132, local copies, waits for them, and re-layouts  24.4 us
    pallas_call x15, Pallas kernels, call(): pl.pallas_call(kernel, out_shape=out_shape, scratch_shapes=list(scratch),...  17.2 us
  transfers between devices with their start and end apart: 71, of which 7 were waited for; matrix products, arithmetic and copies ran while one was open for 0% of the time, Pallas kernels for 1%

profile of v2, /device:TPU:1, one launch (start us, length us, event | category | flops | bytes accessed | tf_op | source)
XLA Modules:
  0.0 601.3 jit_solution(17837354528200400907)
XLA Ops:
  0.6 16.1 %collective-permute-start = (s32[4,256]{1,0:T(4,128)}, s32[4,256]{1,0:T(4,128)S(1)}, u32[]{:S(2)}, u32[]{:S(2)}) collective-permute-start(s32[4,256]{1,0:T(4,128)} %bitcast.26), channel_id=1, source_target_pairs={{0,512},{512,0},{1,513},{513,1},{2,514},{514,2},{3,515},{515,3},{4... | collective-permute-start | bytes 12296 | tf_op jit(solution)/shard_map/swap/ppermute | solution.py:204
  22.7 10.1 %collective-permute-start.10 = (bf16[8,1600]{1,0:T(8,128)(2,1)S(1)}, bf16[8,1600]{1,0:T(8,128)(2,1)S(1)}, u32[]{:S(2)}, u32[]{:S(2)}) collective-permute-start(bf16[8,1600]{1,0:T(8,128)(2,1)S(1)} %get-tuple-element.120), channel_id=1, source_target_pairs={{0,24},{1,25},{2,26},{3,27},{4,28},{5,29},{6,30},{7,31},{8,0},{9,1... | collective-permute-start | bytes 76808 | tf_op jit(solution)/shard_map/dispatch/ppermute | solution.py:210
  37.8 7.3 %collective-permute-start.12 = (bf16[8,1600]{1,0:T(8,128)(2,1)S(1)}, bf16[8,1600]{1,0:T(8,128)(2,1)S(1)}, u32[]{:S(2)}, u32[]{:S(2)}) collective-permute-start(bf16[8,1600]{1,0:T(8,128)(2,1)S(1)} %get-tuple-element.122), channel_id=1, source_target_pairs={{0,26},{1,27},{2,28},{3,29},{4,30},{5,31},{6,0},{7,1},{8,2},{9,3},... | collective-permute-start | bytes 76808 | tf_op jit(solution)/shard_map/dispatch/ppermute | solution.py:210
  61.7 7.9 %collective-permute-start.2 = (bf16[8,1600]{1,0:T(8,128)(2,1)S(1)}, bf16[8,1600]{1,0:T(8,128)(2,1)S(1)}, u32[]{:S(2)}, u32[]{:S(2)}) collective-permute-start(bf16[8,1600]{1,0:T(8,128)(2,1)S(1)} %get-tuple-element.112), channel_id=1, source_target_pairs={{0,16},{1,17},{2,18},{3,19},{4,20},{5,21},{6,22},{7,23},{8,24},{9,... | collective-permute-start | bytes 76808 | tf_op jit(solution)/shard_map/dispatch/ppermute | solution.py:210
  69.6 12.4 %collective-permute-start.3 = (bf16[8,1600]{1,0:T(8,128)(2,1)S(1)}, bf16[8,1600]{1,0:T(8,128)(2,1)S(1)}, u32[]{:S(2)}, u32[]{:S(2)}) collective-permute-start(bf16[8,1600]{1,0:T(8,128)(2,1)S(1)} %get-tuple-element.113), channel_id=1, source_target_pairs={{0,14},{1,15},{2,16},{3,17},{4,18},{5,19},{6,20},{7,21},{8,22},{9,... | collective-permute-start | bytes 76808 | tf_op jit(solution)/shard_map/dispatch/ppermute | solution.py:210
  82.0 9.4 %collective-permute-start.4 = (bf16[8,1600]{1,0:T(8,128)(2,1)S(1)}, bf16[8,1600]{1,0:T(8,128)(2,1)S(1)}, u32[]{:S(2)}, u32[]{:S(2)}) collective-permute-start(bf16[8,1600]{1,0:T(8,128)(2,1)S(1)} %get-tuple-element.114), channel_id=1, source_target_pairs={{0,18},{1,19},{2,20},{3,21},{4,22},{5,23},{6,24},{7,25},{8,26},{9,... | collective-permute-start | bytes 76808 | tf_op jit(solution)/shard_map/dispatch/ppermute | solution.py:210
  91.4 13.9 %collective-permute-start.5 = (bf16[8,1600]{1,0:T(8,128)(2,1)S(1)}, bf16[8,1600]{1,0:T(8,128)(2,1)S(1)}, u32[]{:S(2)}, u32[]{:S(2)}) collective-permute-start(bf16[8,1600]{1,0:T(8,128)(2,1)S(1)} %get-tuple-element.115), channel_id=1, source_target_pairs={{0,12},{1,13},{2,14},{3,15},{4,16},{5,17},{6,18},{7,19},{8,20},{9,... | collective-permute-start | bytes 76808 | tf_op jit(solution)/shard_map/dispatch/ppermute | solution.py:210
  110.3 9.4 %collective-permute-start.7 = (bf16[8,1600]{1,0:T(8,128)(2,1)S(1)}, bf16[8,1600]{1,0:T(8,128)(2,1)S(1)}, u32[]{:S(2)}, u32[]{:S(2)}) collective-permute-start(bf16[8,1600]{1,0:T(8,128)(2,1)S(1)} %get-tuple-element.117), channel_id=1, source_target_pairs={{0,10},{1,11},{2,12},{3,13},{4,14},{5,15},{6,16},{7,17},{8,18},{9,... | collective-permute-start | bytes 76808 | tf_op jit(solution)/shard_map/dispatch/ppermute | solution.py:210
  119.7 7.6 %collective-permute-start.8 = (bf16[8,1600]{1,0:T(8,128)(2,1)S(1)}, bf16[8,1600]{1,0:T(8,128)(2,1)S(1)}, u32[]{:S(2)}, u32[]{:S(2)}) collective-permute-start(bf16[8,1600]{1,0:T(8,128)(2,1)S(1)} %get-tuple-element.118), channel_id=1, source_target_pairs={{0,22},{1,23},{2,24},{3,25},{4,26},{5,27},{6,28},{7,29},{8,30},{9,... | collective-permute-start | bytes 76808 | tf_op jit(solution)/shard_map/dispatch/ppermute | solution.py:210
  127.3 12.1 %collective-permute-start.9 = (bf16[8,1600]{1,0:T(8,128)(2,1)S(1)}, bf16[8,1600]{1,0:T(8,128)(2,1)S(1)}, u32[]{:S(2)}, u32[]{:S(2)}) collective-permute-start(bf16[8,1600]{1,0:T(8,128)(2,1)S(1)} %get-tuple-element.119), channel_id=1, source_target_pairs={{0,8},{1,9},{2,10},{3,11},{4,12},{5,13},{6,14},{7,15},{8,16},{9,17... | collective-permute-start | bytes 76808 | tf_op jit(solution)/shard_map/dispatch/ppermute | solution.py:210
  157.2 9.5 %collective-permute-start.17 = (bf16[8,1600]{1,0:T(8,128)(2,1)S(1)}, bf16[8,1600]{1,0:T(8,128)(2,1)S(1)}, u32[]{:S(2)}, u32[]{:S(2)}) collective-permute-start(bf16[8,1600]{1,0:T(8,128)(2,1)S(1)} %get-tuple-element.128), channel_id=1, source_target_pairs={{0,15},{1,16},{2,17},{3,18},{4,19},{5,20},{6,21},{7,22},{8,23},{9,... | collective-permute-start | bytes 76808 | tf_op jit(solution)/shard_map/dispatch/ppermute | solution.py:210
  166.7 13.2 %collective-permute-start.18 = (bf16[8,1600]{1,0:T(8,128)(2,1)S(1)}, bf16[8,1600]{1,0:T(8,128)(2,1)S(1)}, u32[]{:S(2)}, u32[]{:S(2)}) collective-permute-start(bf16[8,1600]{1,0:T(8,128)(2,1)S(1)} %get-tuple-element.129), channel_id=1, source_target_pairs={{0,17},{1,18},{2,19},{3,20},{4,21},{5,22},{6,23},{7,24},{8,25},{9,... | collective-permute-start | bytes 76808 | tf_op jit(solution)/shard_map/dispatch/ppermute | solution.py:210
  179.9 13.1 %collective-permute-start.19 = (bf16[8,1600]{1,0:T(8,128)(2,1)S(1)}, bf16[8,1600]{1,0:T(8,128)(2,1)S(1)}, u32[]{:S(2)}, u32[]{:S(2)}) collective-permute-start(bf16[8,1600]{1,0:T(8,128)(2,1)S(1)} %get-tuple-element.130), channel_id=1, source_target_pairs={{0,13},{1,14},{2,15},{3,16},{4,17},{5,18},{6,19},{7,20},{8,21},{9,... | collective-permute-start | bytes 76808 | tf_op jit(solution)/shard_map/dispatch/ppermute | solution.py:210
  193.0 7.8 %collective-permute-start.20 = (bf16[8,1600]{1,0:T(8,128)(2,1)S(1)}, bf16[8,1600]{1,0:T(8,128)(2,1)S(1)}, u32[]{:S(2)}, u32[]{:S(2)}) collective-permute-start(bf16[8,1600]{1,0:T(8,128)(2,1)S(1)} %get-tuple-element.131), channel_id=1, source_target_pairs={{0,19},{1,20},{2,21},{3,22},{4,23},{5,24},{6,25},{7,26},{8,27},{9,... | collective-permute-start | bytes 76808 | tf_op jit(solution)/shard_map/dispatch/ppermute | solution.py:210
  205.8 12.9 %collective-permute-start.22 = (bf16[8,1600]{1,0:T(8,128)(2,1)S(1)}, bf16[8,1600]{1,0:T(8,128)(2,1)S(1)}, u32[]{:S(2)}, u32[]{:S(2)}) collective-permute-start(bf16[8,1600]{1,0:T(8,128)(2,1)S(1)} %get-tuple-element.133), channel_id=1, source_target_pairs={{0,21},{1,22},{2,23},{3,24},{4,25},{5,26},{6,27},{7,28},{8,29},{9,... | collective-permute-start | bytes 76808 | tf_op jit(solution)/shard_map/dispatch/ppermute | solution.py:210
  218.7 10.1 %collective-permute-start.23 = (bf16[8,1600]{1,0:T(8,128)(2,1)S(1)}, bf16[8,1600]{1,0:T(8,128)(2,1)S(1)}, u32[]{:S(2)}, u32[]{:S(2)}) collective-permute-start(bf16[8,1600]{1,0:T(8,128)(2,1)S(1)} %get-tuple-element.134), channel_id=1, source_target_pairs={{0,9},{1,10},{2,11},{3,12},{4,13},{5,14},{6,15},{7,16},{8,17},{9,1... | collective-permute-start | bytes 76808 | tf_op jit(solution)/shard_map/dispatch/ppermute | solution.py:210
  237.8 10.3 %collective-permute-start.26 = (bf16[8,1600]{1,0:T(8,128)(2,1)S(1)}, bf16[8,1600]{1,0:T(8,128)(2,1)S(1)}, u32[]{:S(2)}, u32[]{:S(2)}) collective-permute-start(bf16[8,1600]{1,0:T(8,128)(2,1)S(1)} %get-tuple-element.137), channel_id=1, source_target_pairs={{0,25},{1,26},{2,27},{3,28},{4,29},{5,30},{6,31},{7,0},{8,1},{9,2}... | collective-permute-start | bytes 76808 | tf_op jit(solution)/shard_map/dispatch/ppermute | solution.py:210
  258.6 13.3 %collective-permute-start.27 = (bf16[8,1600]{1,0:T(8,128)(2,1)}, bf16[8,1600]{1,0:T(8,128)(2,1)S(1)}, u32[]{:S(2)}, u32[]{:S(2)}) collective-permute-start(bf16[8,1600]{1,0:T(8,128)(2,1)} %get-tuple-element.149), channel_id=1, source_target_pairs={{0,5},{1,6},{2,7},{3,8},{4,9},{5,10},{6,11},{7,12},{8,13},{9,14},{... | collective-permute-start | bytes 76808 | tf_op jit(solution)/shard_map/dispatch/ppermute | solution.py:210
  311.9 8.6 %collective-permute-start.33 = (bf16[8,1600]{1,0:T(8,128)(2,1)S(1)}, bf16[8,1600]{1,0:T(8,128)(2,1)S(1)}, u32[]{:S(2)}, u32[]{:S(2)}) collective-permute-start(bf16[8,1600]{1,0:T(8,128)(2,1)S(1)} %get-tuple-element.164), channel_id=1, source_target_pairs={{0,16},{1,17},{2,18},{3,19},{4,20},{5,21},{6,22},{7,23},{8,24},{9,... | collective-permute-start | bytes 76808 | tf_op jit(solution)/shard_map/down/ppermute | solution.py:210
  320.5 13.1 %collective-permute-start.34 = (bf16[8,1600]{1,0:T(8,128)(2,1)S(1)}, bf16[8,1600]{1,0:T(8,128)(2,1)S(1)}, u32[]{:S(2)}, u32[]{:S(2)}) collective-permute-start(bf16[8,1600]{1,0:T(8,128)(2,1)S(1)} %get-tuple-element.165), channel_id=1, source_target_pairs={{0,18},{1,19},{2,20},{3,21},{4,22},{5,23},{6,24},{7,25},{8,26},{9,... | collective-permute-start | bytes 76808 | tf_op jit(solution)/shard_map/down/ppermute | solution.py:210
  333.6 7.5 %collective-permute-start.35 = (bf16[8,1600]{1,0:T(8,128)(2,1)S(1)}, bf16[8,1600]{1,0:T(8,128)(2,1)S(1)}, u32[]{:S(2)}, u32[]{:S(2)}) collective-permute-start(bf16[8,1600]{1,0:T(8,128)(2,1)S(1)} %get-tuple-element.166), channel_id=1, source_target_pairs={{0,14},{1,15},{2,16},{3,17},{4,18},{5,19},{6,20},{7,21},{8,22},{9,... | collective-permute-start | bytes 76808 | tf_op jit(solution)/shard_map/down/ppermute | solution.py:210
  341.1 11.6 %collective-permute-start.36 = (bf16[8,1600]{1,0:T(8,128)(2,1)S(1)}, bf16[8,1600]{1,0:T(8,128)(2,1)S(1)}, u32[]{:S(2)}, u32[]{:S(2)}) collective-permute-start(bf16[8,1600]{1,0:T(8,128)(2,1)S(1)} %get-tuple-element.167), channel_id=1, source_target_pairs={{0,20},{1,21},{2,22},{3,23},{4,24},{5,25},{6,26},{7,27},{8,28},{9,... | collective-permute-start | bytes 76808 | tf_op jit(solution)/shard_map/down/ppermute | solution.py:210
  360.6 10.8 %collective-permute-start.38 = (bf16[8,1600]{1,0:T(8,128)(2,1)S(1)}, bf16[8,1600]{1,0:T(8,128)(2,1)S(1)}, u32[]{:S(2)}, u32[]{:S(2)}) collective-permute-start(bf16[8,1600]{1,0:T(8,128)(2,1)S(1)} %get-tuple-element.169), channel_id=1, source_target_pairs={{0,22},{1,23},{2,24},{3,25},{4,26},{5,27},{6,28},{7,29},{8,30},{9,... | collective-permute-start | bytes 76808 | tf_op jit(solution)/shard_map/down/ppermute | solution.py:210
  377.6 9.4 %collective-permute-start.40 = (bf16[8,1600]{1,0:T(8,128)(2,1)S(1)}, bf16[8,1600]{1,0:T(8,128)(2,1)S(1)}, u32[]{:S(2)}, u32[]{:S(2)}) collective-permute-start(bf16[8,1600]{1,0:T(8,128)(2,1)S(1)} %get-tuple-element.171), channel_id=1, source_target_pairs={{0,24},{1,25},{2,26},{3,27},{4,28},{5,29},{6,30},{7,31},{8,0},{9,1... | collective-permute-start | bytes 76808 | tf_op jit(solution)/shard_map/down/ppermute | solution.py:210
  392.8 9.8 %collective-permute-start.42 = (bf16[8,1600]{1,0:T(8,128)(2,1)S(1)}, bf16[8,1600]{1,0:T(8,128)(2,1)S(1)}, u32[]{:S(2)}, u32[]{:S(2)}) collective-permute-start(bf16[8,1600]{1,0:T(8,128)(2,1)S(1)} %get-tuple-element.173), channel_id=1, source_target_pairs={{0,26},{1,27},{2,28},{3,29},{4,30},{5,31},{6,0},{7,1},{8,2},{9,3},... | collective-permute-start | bytes 76808 | tf_op jit(solution)/shard_map/down/ppermute | solution.py:210
  448.9 14.7 %collective-permute-start.48 = (bf16[8,1600]{1,0:T(8,128)(2,1)S(1)}, bf16[8,1600]{1,0:T(8,128)(2,1)S(1)}, u32[]{:S(2)}, u32[]{:S(2)}) collective-permute-start(bf16[8,1600]{1,0:T(8,128)(2,1)S(1)} %get-tuple-element.183), channel_id=1, source_target_pairs={{0,17},{1,18},{2,19},{3,20},{4,21},{5,22},{6,23},{7,24},{8,25},{9,... | collective-permute-start | bytes 76808 | tf_op jit(solution)/shard_map/down/ppermute | solution.py:210
  463.6 20.3 %collective-permute-start.64 = (f32[4,256]{1,0:T(4,128)S(1)}, f32[4,256]{1,0:T(4,128)S(1)}, u32[]{:S(2)}, u32[]{:S(2)}) collective-permute-start(f32[4,256]{1,0:T(4,128)S(1)} %bitcast.31), channel_id=1, source_target_pairs={{0,512},{512,0},{1,513},{513,1},{2,514},{514,2},{3,515},{515,3},{4... | collective-permute-start | bytes 12296 | tf_op jit(solution)/shard_map/swap/ppermute | solution.py:204
  489.9 16.0 %collective-permute-start.50 = (bf16[8,1600]{1,0:T(8,128)(2,1)S(1)}, bf16[8,1600]{1,0:T(8,128)(2,1)S(1)}, u32[]{:S(2)}, u32[]{:S(2)}) collective-permute-start(bf16[8,1600]{1,0:T(8,128)(2,1)S(1)} %get-tuple-element.185), channel_id=1, source_target_pairs={{0,19},{1,20},{2,21},{3,22},{4,23},{5,24},{6,25},{7,26},{8,27},{9,... | collective-permute-start | bytes 76808 | tf_op jit(solution)/shard_map/down/ppermute | solution.py:210
  509.6 13.9 %collective-permute-start.52 = (bf16[8,1600]{1,0:T(8,128)(2,1)S(1)}, bf16[8,1600]{1,0:T(8,128)(2,1)S(1)}, u32[]{:S(2)}, u32[]{:S(2)}) collective-permute-start(bf16[8,1600]{1,0:T(8,128)(2,1)S(1)} %get-tuple-element.187), channel_id=1, source_target_pairs={{0,21},{1,22},{2,23},{3,24},{4,25},{5,26},{6,27},{7,28},{8,29},{9,... | collective-permute-start | bytes 76808 | tf_op jit(solution)/shard_map/down/ppermute | solution.py:210
  527.7 14.0 %collective-permute-start.54 = (bf16[8,1600]{1,0:T(8,128)(2,1)S(1)}, bf16[8,1600]{1,0:T(8,128)(2,1)S(1)}, u32[]{:S(2)}, u32[]{:S(2)}) collective-permute-start(bf16[8,1600]{1,0:T(8,128)(2,1)S(1)} %get-tuple-element.189), channel_id=1, source_target_pairs={{0,23},{1,24},{2,25},{3,26},{4,27},{5,28},{6,29},{7,30},{8,31},{9,... | collective-permute-start | bytes 76808 | tf_op jit(solution)/shard_map/down/ppermute | solution.py:210
  543.6 9.4 %collective-permute-start.56 = (bf16[8,1600]{1,0:T(8,128)(2,1)S(1)}, bf16[8,1600]{1,0:T(8,128)(2,1)S(1)}, u32[]{:S(2)}, u32[]{:S(2)}) collective-permute-start(bf16[8,1600]{1,0:T(8,128)(2,1)S(1)} %get-tuple-element.191), channel_id=1, source_target_pairs={{0,25},{1,26},{2,27},{3,28},{4,29},{5,30},{6,31},{7,0},{8,1},{9,2}... | collective-permute-start | bytes 76808 | tf_op jit(solution)/shard_map/down/ppermute | solution.py:210
  557.9 10.1 %collective-permute-start.58 = (bf16[8,1600]{1,0:T(8,128)(2,1)S(1)}, bf16[8,1600]{1,0:T(8,128)(2,1)S(1)}, u32[]{:S(2)}, u32[]{:S(2)}) collective-permute-start(bf16[8,1600]{1,0:T(8,128)(2,1)S(1)} %get-tuple-element.193), channel_id=1, source_target_pairs={{0,27},{1,28},{2,29},{3,30},{4,31},{5,0},{6,1},{7,2},{8,3},{9,4},{... | collective-permute-start | bytes 76808 | tf_op jit(solution)/shard_map/down/ppermute | solution.py:210
  (260 shorter events, 233.5 us)
Async XLA Ops:
  49.1 33.0 %collective-permute-start.14 = (bf16[8,1600]{1,0:T(8,128)(2,1)S(1)}, bf16[8,1600]{1,0:T(8,128)(2,1)S(1)}, u32[]{:S(2)}, u32[]{:S(2)}) collective-permute-start(bf16[8,1600]{1,0:T(8,128)(2,1)S(1)} %get-tuple-element.124), channel_id=1, source_target_pairs={{0,28},{1,29},{2,30},{3,31},{4,0},{5,1},{6,2},{7,3},{8,4},{9,5},{1... | collective-permute-start | bytes 76808 | tf_op jit(solution)/shard_map/dispatch/ppermute | solution.py:210
  54.3 37.2 %collective-permute-start.15 = (bf16[8,1600]{1,0:T(8,128)(2,1)S(1)}, bf16[8,1600]{1,0:T(8,128)(2,1)S(1)}, u32[]{:S(2)}, u32[]{:S(2)}) collective-permute-start(bf16[8,1600]{1,0:T(8,128)(2,1)S(1)} %get-tuple-element.125), channel_id=1, source_target_pairs={{0,2},{1,3},{2,4},{3,5},{4,6},{5,7},{6,8},{7,9},{8,10},{9,11},{10,... | collective-permute-start | bytes 76808 | tf_op jit(solution)/shard_map/dispatch/ppermute | solution.py:210
  56.2 49.2 %collective-permute-start.16 = (bf16[8,1600]{1,0:T(8,128)(2,1)S(1)}, bf16[8,1600]{1,0:T(8,128)(2,1)S(1)}, u32[]{:S(2)}, u32[]{:S(2)}) collective-permute-start(bf16[8,1600]{1,0:T(8,128)(2,1)S(1)} %get-tuple-element.126), channel_id=1, source_target_pairs={{0,30},{1,31},{2,0},{3,1},{4,2},{5,3},{6,4},{7,5},{8,6},{9,7},{10,... | collective-permute-start | bytes 76808 | tf_op jit(solution)/shard_map/dispatch/ppermute | solution.py:210
  61.7 48.6 %collective-permute-start.2 = (bf16[8,1600]{1,0:T(8,128)(2,1)S(1)}, bf16[8,1600]{1,0:T(8,128)(2,1)S(1)}, u32[]{:S(2)}, u32[]{:S(2)}) collective-permute-start(bf16[8,1600]{1,0:T(8,128)(2,1)S(1)} %get-tuple-element.112), channel_id=1, source_target_pairs={{0,16},{1,17},{2,18},{3,19},{4,20},{5,21},{6,22},{7,23},{8,24},{9,... | collective-permute-start | bytes 76808 | tf_op jit(solution)/shard_map/dispatch/ppermute | solution.py:210
  69.6 50.1 %collective-permute-start.3 = (bf16[8,1600]{1,0:T(8,128)(2,1)S(1)}, bf16[8,1600]{1,0:T(8,128)(2,1)S(1)}, u32[]{:S(2)}, u32[]{:S(2)}) collective-permute-start(bf16[8,1600]{1,0:T(8,128)(2,1)S(1)} %get-tuple-element.113), channel_id=1, source_target_pairs={{0,14},{1,15},{2,16},{3,17},{4,18},{5,19},{6,20},{7,21},{8,22},{9,... | collective-permute-start | bytes 76808 | tf_op jit(solution)/shard_map/dispatch/ppermute | solution.py:210
  82.0 45.3 %collective-permute-start.4 = (bf16[8,1600]{1,0:T(8,128)(2,1)S(1)}, bf16[8,1600]{1,0:T(8,128)(2,1)S(1)}, u32[]{:S(2)}, u32[]{:S(2)}) collective-permute-start(bf16[8,1600]{1,0:T(8,128)(2,1)S(1)} %get-tuple-element.114), channel_id=1, source_target_pairs={{0,18},{1,19},{2,20},{3,21},{4,22},{5,23},{6,24},{7,25},{8,26},{9,... | collective-permute-start | bytes 76808 | tf_op jit(solution)/shard_map/dispatch/ppermute | solution.py:210
  91.4 48.0 %collective-permute-start.5 = (bf16[8,1600]{1,0:T(8,128)(2,1)S(1)}, bf16[8,1600]{1,0:T(8,128)(2,1)S(1)}, u32[]{:S(2)}, u32[]{:S(2)}) collective-permute-start(bf16[8,1600]{1,0:T(8,128)(2,1)S(1)} %get-tuple-element.115), channel_id=1, source_target_pairs={{0,12},{1,13},{2,14},{3,15},{4,16},{5,17},{6,18},{7,19},{8,20},{9,... | collective-permute-start | bytes 76808 | tf_op jit(solution)/shard_map/dispatch/ppermute | solution.py:210
  105.4 34.1 %collective-permute-start.6 = (bf16[8,1600]{1,0:T(8,128)(2,1)S(1)}, bf16[8,1600]{1,0:T(8,128)(2,1)S(1)}, u32[]{:S(2)}, u32[]{:S(2)}) collective-permute-start(bf16[8,1600]{1,0:T(8,128)(2,1)S(1)} %get-tuple-element.116), channel_id=1, source_target_pairs={{0,20},{1,21},{2,22},{3,23},{4,24},{5,25},{6,26},{7,27},{8,28},{9,... | collective-permute-start | bytes 76808 | tf_op jit(solution)/shard_map/dispatch/ppermute | solution.py:210
  146.1 103.0 %all-to-all-start = ((bf16[16,40,1536]{2,1,0:T(8,128)(2,1)}), bf16[16,40,1536]{2,1,0:T(8,128)(2,1)}, u32[]{:S(2)}, u32[]{:S(2)}) async-start(bf16[16,40,1536]{2,1,0:T(8,128)(2,1)} %bitcast.3), calls=%async_computation | async-start | bytes 3932160 | tf_op jit(solution)/shard_map/hidden/all_to_all | solution.py:200
  157.2 48.6 %collective-permute-start.17 = (bf16[8,1600]{1,0:T(8,128)(2,1)S(1)}, bf16[8,1600]{1,0:T(8,128)(2,1)S(1)}, u32[]{:S(2)}, u32[]{:S(2)}) collective-permute-start(bf16[8,1600]{1,0:T(8,128)(2,1)S(1)} %get-tuple-element.128), channel_id=1, source_target_pairs={{0,15},{1,16},{2,17},{3,18},{4,19},{5,20},{6,21},{7,22},{8,23},{9,... | collective-permute-start | bytes 76808 | tf_op jit(solution)/shard_map/dispatch/ppermute | solution.py:210
  166.7 52.1 %collective-permute-start.18 = (bf16[8,1600]{1,0:T(8,128)(2,1)S(1)}, bf16[8,1600]{1,0:T(8,128)(2,1)S(1)}, u32[]{:S(2)}, u32[]{:S(2)}) collective-permute-start(bf16[8,1600]{1,0:T(8,128)(2,1)S(1)} %get-tuple-element.129), channel_id=1, source_target_pairs={{0,17},{1,18},{2,19},{3,20},{4,21},{5,22},{6,23},{7,24},{8,25},{9,... | collective-permute-start | bytes 76808 | tf_op jit(solution)/shard_map/dispatch/ppermute | solution.py:210
  179.9 49.0 %collective-permute-start.19 = (bf16[8,1600]{1,0:T(8,128)(2,1)S(1)}, bf16[8,1600]{1,0:T(8,128)(2,1)S(1)}, u32[]{:S(2)}, u32[]{:S(2)}) collective-permute-start(bf16[8,1600]{1,0:T(8,128)(2,1)S(1)} %get-tuple-element.130), channel_id=1, source_target_pairs={{0,13},{1,14},{2,15},{3,16},{4,17},{5,18},{6,19},{7,20},{8,21},{9,... | collective-permute-start | bytes 76808 | tf_op jit(solution)/shard_map/dispatch/ppermute | solution.py:210
  193.0 41.9 %collective-permute-start.20 = (bf16[8,1600]{1,0:T(8,128)(2,1)S(1)}, bf16[8,1600]{1,0:T(8,128)(2,1)S(1)}, u32[]{:S(2)}, u32[]{:S(2)}) collective-permute-start(bf16[8,1600]{1,0:T(8,128)(2,1)S(1)} %get-tuple-element.131), channel_id=1, source_target_pairs={{0,19},{1,20},{2,21},{3,22},{4,23},{5,24},{6,25},{7,26},{8,27},{9,... | collective-permute-start | bytes 76808 | tf_op jit(solution)/shard_map/dispatch/ppermute | solution.py:210
  200.8 37.0 %collective-permute-start.21 = (bf16[8,1600]{1,0:T(8,128)(2,1)S(1)}, bf16[8,1600]{1,0:T(8,128)(2,1)S(1)}, u32[]{:S(2)}, u32[]{:S(2)}) collective-permute-start(bf16[8,1600]{1,0:T(8,128)(2,1)S(1)} %get-tuple-element.132), channel_id=1, source_target_pairs={{0,11},{1,12},{2,13},{3,14},{4,15},{5,16},{6,17},{7,18},{8,19},{9,... | collective-permute-start | bytes 76808 | tf_op jit(solution)/shard_map/dispatch/ppermute | solution.py:210
  205.8 42.4 %collective-permute-start.22 = (bf16[8,1600]{1,0:T(8,128)(2,1)S(1)}, bf16[8,1600]{1,0:T(8,128)(2,1)S(1)}, u32[]{:S(2)}, u32[]{:S(2)}) collective-permute-start(bf16[8,1600]{1,0:T(8,128)(2,1)S(1)} %get-tuple-element.133), channel_id=1, source_target_pairs={{0,21},{1,22},{2,23},{3,24},{4,25},{5,26},{6,27},{7,28},{8,29},{9,... | collective-permute-start | bytes 76808 | tf_op jit(solution)/shard_map/dispatch/ppermute | solution.py:210
  251.9 42.4 %all-to-all-start.1 = ((bf16[16,40,768]{2,1,0:T(8,128)(2,1)}), bf16[16,40,768]{2,1,0:T(8,128)(2,1)S(1)}, u32[]{:S(2)}, u32[]{:S(2)}) async-start(bf16[16,40,768]{2,1,0:T(8,128)(2,1)} %copy-done.6), calls=%async_computation.1 | async-start | bytes 1966080 | tf_op jit(solution)/shard_map/hidden/all_to_all | solution.py:200
  300.0 105.6 %all-to-all-start.2 = ((bf16[16,40,1536]{2,1,0:T(8,128)(2,1)}), bf16[16,40,1536]{2,1,0:T(8,128)(2,1)S(1)}, u32[]{:S(2)}, u32[]{:S(2)}) async-start(bf16[16,40,1536]{2,1,0:T(8,128)(2,1)} %bitcast.16), calls=%async_computation.2 | async-start | bytes 3932160 | tf_op jit(solution)/shard_map/hidden/all_to_all | solution.py:200
  311.9 48.0 %collective-permute-start.33 = (bf16[8,1600]{1,0:T(8,128)(2,1)S(1)}, bf16[8,1600]{1,0:T(8,128)(2,1)S(1)}, u32[]{:S(2)}, u32[]{:S(2)}) collective-permute-start(bf16[8,1600]{1,0:T(8,128)(2,1)S(1)} %get-tuple-element.164), channel_id=1, source_target_pairs={{0,16},{1,17},{2,18},{3,19},{4,20},{5,21},{6,22},{7,23},{8,24},{9,... | collective-permute-start | bytes 76808 | tf_op jit(solution)/shard_map/down/ppermute | solution.py:210
  320.5 50.9 %collective-permute-start.34 = (bf16[8,1600]{1,0:T(8,128)(2,1)S(1)}, bf16[8,1600]{1,0:T(8,128)(2,1)S(1)}, u32[]{:S(2)}, u32[]{:S(2)}) collective-permute-start(bf16[8,1600]{1,0:T(8,128)(2,1)S(1)} %get-tuple-element.165), channel_id=1, source_target_pairs={{0,18},{1,19},{2,20},{3,21},{4,22},{5,23},{6,24},{7,25},{8,26},{9,... | collective-permute-start | bytes 76808 | tf_op jit(solution)/shard_map/down/ppermute | solution.py:210
  333.6 43.3 %collective-permute-start.35 = (bf16[8,1600]{1,0:T(8,128)(2,1)S(1)}, bf16[8,1600]{1,0:T(8,128)(2,1)S(1)}, u32[]{:S(2)}, u32[]{:S(2)}) collective-permute-start(bf16[8,1600]{1,0:T(8,128)(2,1)S(1)} %get-tuple-element.166), channel_id=1, source_target_pairs={{0,14},{1,15},{2,16},{3,17},{4,18},{5,19},{6,20},{7,21},{8,22},{9,... | collective-permute-start | bytes 76808 | tf_op jit(solution)/shard_map/down/ppermute | solution.py:210
  341.1 45.9 %collective-permute-start.36 = (bf16[8,1600]{1,0:T(8,128)(2,1)S(1)}, bf16[8,1600]{1,0:T(8,128)(2,1)S(1)}, u32[]{:S(2)}, u32[]{:S(2)}) collective-permute-start(bf16[8,1600]{1,0:T(8,128)(2,1)S(1)} %get-tuple-element.167), channel_id=1, source_target_pairs={{0,20},{1,21},{2,22},{3,23},{4,24},{5,25},{6,26},{7,27},{8,28},{9,... | collective-permute-start | bytes 76808 | tf_op jit(solution)/shard_map/down/ppermute | solution.py:210
  352.7 39.5 %collective-permute-start.37 = (bf16[8,1600]{1,0:T(8,128)(2,1)S(1)}, bf16[8,1600]{1,0:T(8,128)(2,1)S(1)}, u32[]{:S(2)}, u32[]{:S(2)}) collective-permute-start(bf16[8,1600]{1,0:T(8,128)(2,1)S(1)} %get-tuple-element.168), channel_id=1, source_target_pairs={{0,12},{1,13},{2,14},{3,15},{4,16},{5,17},{6,18},{7,19},{8,20},{9,... | collective-permute-start | bytes 76808 | tf_op jit(solution)/shard_map/down/ppermute | solution.py:210
  360.6 42.0 %collective-permute-start.38 = (bf16[8,1600]{1,0:T(8,128)(2,1)S(1)}, bf16[8,1600]{1,0:T(8,128)(2,1)S(1)}, u32[]{:S(2)}, u32[]{:S(2)}) collective-permute-start(bf16[8,1600]{1,0:T(8,128)(2,1)S(1)} %get-tuple-element.169), channel_id=1, source_target_pairs={{0,22},{1,23},{2,24},{3,25},{4,26},{5,27},{6,28},{7,29},{8,30},{9,... | collective-permute-start | bytes 76808 | tf_op jit(solution)/shard_map/down/ppermute | solution.py:210
  441.3 159.2 %all-to-all-start.4 = ((bf16[16,32,512]{2,1,0:T(8,128)(2,1)}), bf16[16,32,512]{2,1,0:T(8,128)(2,1)S(1)}, u32[]{:S(2)}, u32[]{:S(2)}) async-start(bf16[16,32,512]{2,1,0:T(8,128)(2,1)} %bitcast.11), calls=%async_computation.4 | async-start | bytes 1048576 | tf_op jit(solution)/shard_map/latent/all_to_all | solution.py:200
  448.9 74.6 %collective-permute-start.48 = (bf16[8,1600]{1,0:T(8,128)(2,1)S(1)}, bf16[8,1600]{1,0:T(8,128)(2,1)S(1)}, u32[]{:S(2)}, u32[]{:S(2)}) collective-permute-start(bf16[8,1600]{1,0:T(8,128)(2,1)S(1)} %get-tuple-element.183), channel_id=1, source_target_pairs={{0,17},{1,18},{2,19},{3,20},{4,21},{5,22},{6,23},{7,24},{8,25},{9,... | collective-permute-start | bytes 76808 | tf_op jit(solution)/shard_map/down/ppermute | solution.py:210
  463.6 46.0 %collective-permute-start.64 = (f32[4,256]{1,0:T(4,128)S(1)}, f32[4,256]{1,0:T(4,128)S(1)}, u32[]{:S(2)}, u32[]{:S(2)}) collective-permute-start(f32[4,256]{1,0:T(4,128)S(1)} %bitcast.31), channel_id=1, source_target_pairs={{0,512},{512,0},{1,513},{513,1},{2,514},{514,2},{3,515},{515,3},{4... | collective-permute-start | bytes 12296 | tf_op jit(solution)/shard_map/swap/ppermute | solution.py:204
  484.0 43.7 %collective-permute-start.49 = (bf16[8,1600]{1,0:T(8,128)(2,1)S(1)}, bf16[8,1600]{1,0:T(8,128)(2,1)S(1)}, u32[]{:S(2)}, u32[]{:S(2)}) collective-permute-start(bf16[8,1600]{1,0:T(8,128)(2,1)S(1)} %get-tuple-element.184), channel_id=1, source_target_pairs={{0,15},{1,16},{2,17},{3,18},{4,19},{5,20},{6,21},{7,22},{8,23},{9,... | collective-permute-start | bytes 76808 | tf_op jit(solution)/shard_map/down/ppermute | solution.py:210
  489.9 51.8 %collective-permute-start.50 = (bf16[8,1600]{1,0:T(8,128)(2,1)S(1)}, bf16[8,1600]{1,0:T(8,128)(2,1)S(1)}, u32[]{:S(2)}, u32[]{:S(2)}) collective-permute-start(bf16[8,1600]{1,0:T(8,128)(2,1)S(1)} %get-tuple-element.185), channel_id=1, source_target_pairs={{0,19},{1,20},{2,21},{3,22},{4,23},{5,24},{6,25},{7,26},{8,27},{9,... | collective-permute-start | bytes 76808 | tf_op jit(solution)/shard_map/down/ppermute | solution.py:210
  505.9 37.8 %collective-permute-start.51 = (bf16[8,1600]{1,0:T(8,128)(2,1)S(1)}, bf16[8,1600]{1,0:T(8,128)(2,1)S(1)}, u32[]{:S(2)}, u32[]{:S(2)}) collective-permute-start(bf16[8,1600]{1,0:T(8,128)(2,1)S(1)} %get-tuple-element.186), channel_id=1, source_target_pairs={{0,13},{1,14},{2,15},{3,16},{4,17},{5,18},{6,19},{7,20},{8,21},{9,... | collective-permute-start | bytes 76808 | tf_op jit(solution)/shard_map/down/ppermute | solution.py:210
  509.6 43.4 %collective-permute-start.52 = (bf16[8,1600]{1,0:T(8,128)(2,1)S(1)}, bf16[8,1600]{1,0:T(8,128)(2,1)S(1)}, u32[]{:S(2)}, u32[]{:S(2)}) collective-permute-start(bf16[8,1600]{1,0:T(8,128)(2,1)S(1)} %get-tuple-element.187), channel_id=1, source_target_pairs={{0,21},{1,22},{2,23},{3,24},{4,25},{5,26},{6,27},{7,28},{8,29},{9,... | collective-permute-start | bytes 76808 | tf_op jit(solution)/shard_map/down/ppermute | solution.py:210
  523.5 34.4 %collective-permute-start.53 = (bf16[8,1600]{1,0:T(8,128)(2,1)S(1)}, bf16[8,1600]{1,0:T(8,128)(2,1)S(1)}, u32[]{:S(2)}, u32[]{:S(2)}) collective-permute-start(bf16[8,1600]{1,0:T(8,128)(2,1)S(1)} %get-tuple-element.188), channel_id=1, source_target_pairs={{0,11},{1,12},{2,13},{3,14},{4,15},{5,16},{6,17},{7,18},{8,19},{9,... | collective-permute-start | bytes 76808 | tf_op jit(solution)/shard_map/down/ppermute | solution.py:210
  527.7 41.4 %collective-permute-start.54 = (bf16[8,1600]{1,0:T(8,128)(2,1)S(1)}, bf16[8,1600]{1,0:T(8,128)(2,1)S(1)}, u32[]{:S(2)}, u32[]{:S(2)}) collective-permute-start(bf16[8,1600]{1,0:T(8,128)(2,1)S(1)} %get-tuple-element.189), channel_id=1, source_target_pairs={{0,23},{1,24},{2,25},{3,26},{4,27},{5,28},{6,29},{7,30},{8,31},{9,... | collective-permute-start | bytes 76808 | tf_op jit(solution)/shard_map/down/ppermute | solution.py:210
  (105 other events, 3154.0 us)

commit v3 on v1

v3 whole, which is shorter than its diff:
```python
import functools

import jax
import jax.numpy as jnp
from jax import lax
from jax.experimental import pallas as pl
from jax.experimental.pallas import tpu as pltpu
from jax.sharding import PartitionSpec as P

SE = ("section", "expert")
NT = (((1,), (1,)), ((), ()))
TN = (((0,), (0,)), ((), ()))
BF = jnp.bfloat16
F32 = jnp.float32


def call(kernel, out_shape, *args, in_specs=None, scratch=(), flops=0, moved=0):
    kwargs = {}
    if in_specs is not None:
        kwargs["in_specs"] = in_specs
        kwargs["grid"] = (1,)
    return pl.pallas_call(
        kernel,
        out_shape=out_shape,
        scratch_shapes=list(scratch),
        cost_estimate=pl.CostEstimate(flops=flops, bytes_accessed=moved, transcendentals=0),
        compiler_params=pltpu.CompilerParams(vmem_limit_bytes=24 * 1024 * 1024),
        **kwargs,
    )(*args)


def iota(shape, dim):
    return lax.broadcasted_iota(jnp.int32, shape, dim)


def slot_masks(pick_ref, routes_t, lanes, slot_count):
    tops, rows = routes_t.shape
    resident, part = pick_ref[0], pick_ref[1]
    ids = (iota((slot_count, rows), 0) >> 1) * 2 + resident
    named = jnp.zeros((slot_count, rows), F32)
    for k in range(tops):
        named = named + jnp.where(routes_t[k : k + 1, :] == ids, 1.0, 0.0)
    earlier = (iota((rows, rows), 0) < iota((rows, rows), 1)).astype(F32).astype(BF)
    rank = jnp.dot(named.astype(BF), earlier, preferred_element_type=F32)
    base = (part * lanes).astype(F32)
    return ids, [(named > 0.5) & (rank == base + float(i)) for i in range(lanes)]


def by_half(x):
    half = iota(x.shape, 0) & 1
    return jnp.concatenate([jnp.where(half == 0, x, 0.0), jnp.where(half == 1, x, 0.0)], axis=1)


def dispatch_kernel(lanes, pick_ref, routes_ref, t0, t1, t2, t3, out):
    span = 2 * t0.shape[0]
    _, masks = slot_masks(pick_ref, routes_ref[...], lanes, out.shape[0])
    left = jnp.concatenate([t0[...], t1[...]], axis=0)
    right = jnp.concatenate([t2[...], t3[...]], axis=0)
    both = jnp.concatenate([left, right], axis=1)
    for i, mask in enumerate(masks):
        hot = by_half(mask.astype(F32)).astype(BF)
        rows = lax.dot_general(hot, both, NT, preferred_element_type=F32)
        out[:, i * span : (i + 1) * span] = rows.astype(BF)


def weights_kernel(lanes, pick_ref, routes_ref, weights_ref, high_ref, low_ref):
    routes_t, weights_t = routes_ref[...], weights_ref[...]
    ids, masks = slot_masks(pick_ref, routes_t, lanes, high_ref.shape[1])
    gates = jnp.zeros(ids.shape, F32)
    for k in range(routes_t.shape[0]):
        gates = gates + jnp.where(routes_t[k : k + 1, :] == ids, weights_t[k : k + 1, :], 0.0)
    high = gates.astype(BF).astype(F32)
    low = gates - high
    for i, mask in enumerate(masks):
        high_ref[i] = by_half(jnp.where(mask, high, 0.0)).astype(BF)
        low_ref[i] = by_half(jnp.where(mask, low, 0.0)).astype(BF)


def halves_first(count):
    a = iota((count, count), 1)
    return (iota((count, count), 0) == (a & 1) * (count // 2) + (a >> 1)).astype(F32).astype(BF)


def up_kernel(lanes, rows_ref, w0, w1, w2, w3, out, packed):
    count = rows_ref.shape[0]
    groups = count // 2
    width, columns = w0.shape
    span = 2 * width
    step = 512 if columns % 512 == 0 else columns
    rows = jnp.dot(halves_first(count), rows_ref[...], preferred_element_type=F32).astype(BF)
    for i in range(lanes):
        for p in range(2):
            piece = rows[p * groups : (p + 1) * groups, i * span : (i + 1) * span]
            packed[i * groups : (i + 1) * groups, p * span : (p + 1) * span] = piece
    for c in range(0, columns, step):
        total = None
        for k, weight in enumerate((w0, w1, w2, w3)):
            part = jnp.dot(
                packed[:, k * width : (k + 1) * width],
                weight[:, c : c + step],
                preferred_element_type=F32,
            )
            total = part if total is None else total + part
        out[:, c : c + step] = total.astype(BF)


def hidden_kernel(parts_ref, out):
    blocks = parts_ref.shape[0]
    half = out.shape[2]
    total = parts_ref[0].astype(F32)
    for b in range(1, blocks):
        total = total + parts_ref[b].astype(F32)
    gate, up = total[:, :half], total[:, half:]
    hidden = (gate / (1.0 + jnp.exp(-gate)) * up).astype(BF)
    for b in range(blocks):
        out[b] = hidden


def down_kernel(lanes, hidden_ref, w0, w1, w2, w3, out, packed):
    count = out.shape[0]
    groups = count // 2
    width = w0.shape[0]
    span = 2 * width
    for k, weight in enumerate((w0, w1, w2, w3)):
        part = lax.dot_general(hidden_ref[...], weight[...], NT, preferred_element_type=F32)
        part = part.astype(BF)
        p, skip = k // 2, (k % 2) * width
        for i in range(lanes):
            at = i * span + skip
            piece = part[i * groups : (i + 1) * groups, :]
            packed[p * groups : (p + 1) * groups, at : at + width] = piece
    rows = lax.dot_general(halves_first(count), packed[...], TN, preferred_element_type=F32)
    out[...] = rows.astype(BF)


def mix_kernel(lanes, back_ref, high_ref, low_ref, own_ref, o1, o2, o3):
    width, tokens = own_ref.shape
    span = 2 * width
    total = jnp.zeros((span, 2 * tokens), F32)
    for i in range(lanes):
        rows = back_ref[:, i * span : (i + 1) * span]
        total = total + lax.dot_general(rows, high_ref[i], TN, preferred_element_type=F32)
        total = total + lax.dot_general(rows, low_ref[i], TN, preferred_element_type=F32)
    own_ref[...] = total[:width, :tokens]
    o1[...] = total[width:, :tokens].astype(BF)
    o2[...] = total[:width, tokens:].astype(BF)
    o3[...] = total[width:, tokens:].astype(BF)


def join_kernel(own_ref, a_ref, b_ref, c_ref, out):
    total = own_ref[...] + a_ref[...].astype(F32) + b_ref[...].astype(F32)
    out[...] = (total + c_ref[...].astype(F32)).astype(BF)


def latent_kernel(longest, lengths_ref, placement_ref, tokens_ref, weight_ref, out, select, offset):
    requests = lengths_ref.shape[1]
    rows = tokens_ref.shape[1]
    partial = lax.dot_general(tokens_ref[...], weight_ref[...], TN, preferred_element_type=F32)
    run = jnp.int32(0)
    for j in range(requests):
        offset[j] = run
        run = run + lengths_ref[0, j]
    place, position = iota((longest, rows), 0), iota((longest, rows), 1)
    for q in range(requests):
        request = placement_ref[0, q]
        hit = (position == place + offset[request]) & (place < lengths_ref[0, request])
        select[q * longest : (q + 1) * longest, :] = hit.astype(F32).astype(BF)
    picked = jnp.dot(select[...], partial.astype(BF), preferred_element_type=F32)
    out[...] = picked.astype(BF)


def norm_kernel(sum_ref, gain_ref, out):
    total = sum_ref[...]
    scale = lax.rsqrt(jnp.mean(total * total, axis=1, keepdims=True) + 1e-06)
    out[...] = (total * scale * gain_ref[...]).astype(BF)


def exchange(x, axes, groups=None):
    return lax.all_to_all(x, axes, split_axis=0, concat_axis=0, axis_index_groups=groups, tiled=True)


def flip(x, bits):
    return lax.ppermute(x, "dp", [(i, i ^ bits) for i in range(lax.axis_size("dp"))])


def gather_expert(array, resident):
    own = lax.dynamic_index_in_dim(array, resident, 0, keepdims=False)
    cross = lax.dynamic_index_in_dim(array, 1 - resident, 0, keepdims=False)
    second, third = flip(own, 1), flip(cross, 3)
    return own, second, third, flip(third, 1)


def sum_to_owner(parts):
    me = lax.axis_index("dp")
    bit = parts.shape[0] // 2
    while bit:
        high = (me & bit) != 0
        keep = jnp.where(high, parts[bit:], parts[:bit])
        send = jnp.where(high, parts[:bit], parts[bit:])
        parts = keep.astype(F32) + flip(send, bit).astype(F32)
        bit //= 2
        if bit:
            parts = parts.astype(BF)
    return parts[0]


def body(
    tokens, routes, route_weights, w_gate_up, w_down, w_latent, latent_gain, lengths, placement
):
    groups = lax.axis_size(SE)
    blocks = lax.axis_size("dp")
    along_y = 4
    along_x = blocks // along_y
    columns = [[y + along_y * x for x in range(along_x)] for y in range(along_y)]
    rows, width = tokens.shape
    tops = routes.shape[1]
    residents = w_gate_up.shape[0]
    hidden_units = w_down.shape[1]
    latent_width = w_latent.shape[1]
    experts = residents * groups
    capacity = 5 * rows * tops // (4 * experts)
    lanes = capacity // 2
    longest = 2 * rows // blocks
    slots = 2 * groups
    row = 2 * lanes * width
    taken = lanes * groups
    share = taken // along_x
    shape = jax.ShapeDtypeStruct
    tokens_t, routes_t, gates_t = tokens.T, routes.T, route_weights.T
    vmem = pl.BlockSpec(memory_space=pltpu.VMEM)
    smem = pl.BlockSpec(memory_space=pltpu.SMEM)

    at_y = lax.axis_index("dp") % along_y
    resident = at_y // 2
    pick = jnp.stack([resident, at_y % 2])

    with jax.named_scope("tokens"):
        pieces = [tokens_t, flip(tokens_t, 1), flip(tokens_t, 3), flip(tokens_t, 2)]

    with jax.named_scope("dispatch"):
        outgoing = call(
            functools.partial(dispatch_kernel, lanes),
            shape((slots, row), BF),
            pick,
            routes_t,
            *pieces,
            in_specs=[smem] + [vmem] * 5,
            flops=8 * slots * rows * width * lanes,
            moved=2 * slots * row,
        )
        outgoing, w_gate_up, w_down = lax.optimization_barrier((outgoing, w_gate_up, w_down))
        arrived = exchange(outgoing.reshape(groups, 2, row), SE)

    with jax.named_scope("gather"):
        up_blocks = gather_expert(w_gate_up, resident)
        down_blocks = gather_expert(w_down.transpose(0, 2, 1), resident)
        arrived, up_blocks, down_blocks = lax.optimization_barrier(
            (arrived, up_blocks, down_blocks)
        )

    with jax.named_scope("up"):
        partial = call(
            functools.partial(up_kernel, lanes),
            shape((taken, 2 * hidden_units), BF),
            arrived.reshape(slots, row),
            *up_blocks,
            scratch=[pltpu.VMEM((taken, 4 * width), BF)],
            flops=16 * taken * width * hidden_units,
            moved=4 * hidden_units * (4 * width + taken),
        )
        shares = exchange(partial.reshape(along_x, share, 2 * hidden_units), "dp", columns)

    with jax.named_scope("hidden"):
        hidden = call(
            hidden_kernel,
            shape((along_x, share, hidden_units), BF),
            shares,
            flops=2 * taken * hidden_units,
            moved=6 * taken * hidden_units,
        )
        gathered = exchange(hidden, "dp", columns)

    with jax.named_scope("down"):
        produced = call(
            functools.partial(down_kernel, lanes),
            shape((slots, row), BF),
            gathered.reshape(taken, hidden_units),
            *down_blocks,
            scratch=[pltpu.VMEM((slots, row), BF)],
            flops=8 * taken * width * hidden_units,
            moved=2 * hidden_units * (4 * width + taken),
        )
        produced, tokens_t, gates_t = lax.optimization_barrier((produced, tokens_t, gates_t))
        back = exchange(produced.reshape(groups, 2, row), SE).reshape(slots, row)

    with jax.named_scope("gates"):
        gates = call(
            functools.partial(weights_kernel, lanes),
            [shape((lanes, slots, 2 * rows), BF)] * 2,
            pick,
            routes_t,
            gates_t,
            in_specs=[smem, vmem, vmem],
            flops=4 * slots * rows * rows,
            moved=8 * lanes * slots * rows,
        )

    with jax.named_scope("latent"):
        picked = call(
            functools.partial(latent_kernel, longest),
            shape((blocks * longest, latent_width), BF),
            lengths,
            placement,
            tokens_t,
            w_latent,
            in_specs=[smem, smem, vmem, vmem],
            scratch=[
                pltpu.VMEM((blocks * longest, rows), BF),
                pltpu.SMEM((blocks,), jnp.int32),
            ],
            flops=2 * rows * latent_width * (width + blocks * longest),
            moved=2 * latent_width * (width + blocks * longest),
        )
        latent = sum_to_owner(picked.reshape(blocks, longest, latent_width))
        latent_cache = call(
            norm_kernel,
            shape((longest, latent_width), BF),
            latent,
            latent_gain.reshape(1, latent_width),
            flops=8 * longest * latent_width,
            moved=4 * longest * latent_width,
        )
        back, latent_cache = lax.optimization_barrier((back, latent_cache))

    with jax.named_scope("mix"):
        own, *others = call(
            functools.partial(mix_kernel, lanes),
            [shape((width, rows), F32)] + [shape((width, rows), BF)] * 3,
            back,
            *gates,
            flops=32 * taken * width * rows,
            moved=2 * slots * row + 8 * lanes * slots * rows,
        )
        mixed = call(
            join_kernel,
            shape((width, rows), BF),
            own,
            *[flip(x, bits) for x, bits in zip(others, (1, 3, 2))],
            flops=3 * width * rows,
            moved=12 * width * rows,
        )
    return (mixed.T, latent_cache.reshape(1, 1, longest, latent_width))


def solution(mesh):
    return jax.shard_map(
        body,
        mesh=mesh,
        in_specs=(
            P(SE, "dp"),
            P(SE, None),
            P(SE, None),
            P(SE, "dp", None),
            P(SE, None, "dp"),
            P("dp", None),
            P(),
            P(SE, None),
            P(SE, None),
        ),
        out_specs=(P(SE, "dp"), P("dp", SE, None, None)),
        check_vma=False,
    )
```

time: 407 us -> 291 us (0.71)
  blocking collectives: 144 us -> 29.9 us
  starting transfers between devices: 30.7 us -> 85.1 us
  waiting for transfers between devices: 197 us -> 148 us
  between operations: 14.2 us -> 1.17 us
  local copies, waits for them, and re-layouts: 7.64 us -> 13.6 us
    all_to_all x2, blocking collectives: 144 us -> 29.9 us  [exchange(): lax.all_to_all(x, axes, split_axis=0, concat_axis=0, axis_index_groups=gr...]
    reduce_scatter x1 -> x0, waiting for transfers between devices: 113 us -> none  [body(): summed = lax.psum_scatter(picked, 'dp', scatter_dimension=0, tiled=True)]
    ppermute x0 -> x16, waiting for transfers between devices: none -> 85 us  [flip(): lax.ppermute(x, 'dp', [(i, i ^ bits) for i in range(lax.axis_size('dp'))])]
    ppermute x0 -> x16, starting transfers between devices: none -> 48.2 us  [flip(): lax.ppermute(x, 'dp', [(i, i ^ bits) for i in range(lax.axis_size('dp'))])]
    all_to_all x2, waiting for transfers between devices: 84.9 us -> 62.9 us  [exchange(): lax.all_to_all(x, axes, split_axis=0, concat_axis=0, axis_index_groups=gr...]
    all_to_all x2, starting transfers between devices: 30.6 us -> 36.9 us  [exchange(): lax.all_to_all(x, axes, split_axis=0, concat_axis=0, axis_index_groups=gr...]
    unnamed x26 -> x42, local copies, waits for them, and re-layouts: 3.51 us -> 8.37 us
    pallas_call x8 -> x9, Pallas kernels: 12.4 us -> 11.5 us  [call(): pl.pallas_call(kernel, out_shape=out_shape, scratch_shapes=list(scratch),...]
  transfers between devices with their start and end apart: 3 -> 18, of which waited for: 2 -> 14; matrix products, arithmetic and copies ran while one was open for 0% -> 0% of each run, Pallas kernels for 1% -> 1%
where the time goes in v3:
time: 291 us; the launch traced here: 290 us
  waiting for transfers between devices  148 us (51%)
  starting transfers between devices  85.1 us (29%)
  blocking collectives  29.9 us (10%)
  local copies, waits for them, and re-layouts  13.6 us (5%)
  Pallas kernels  11.5 us (4%)
    ppermute x16, waiting for transfers between devices, flip(): lax.ppermute(x, 'dp', [(i, i ^ bits) for i in range(lax.axis_size('dp'))])  85 us
    all_to_all x2, waiting for transfers between devices, exchange(): lax.all_to_all(x, axes, split_axis=0, concat_axis=0, axis_index_groups=gr...  62.9 us
    ppermute x16, starting transfers between devices, flip(): lax.ppermute(x, 'dp', [(i, i ^ bits) for i in range(lax.axis_size('dp'))])  48.2 us
    all_to_all x2, starting transfers between devices, exchange(): lax.all_to_all(x, axes, split_axis=0, concat_axis=0, axis_index_groups=gr...  36.9 us
    all_to_all x2, blocking collectives, exchange(): lax.all_to_all(x, axes, split_axis=0, concat_axis=0, axis_index_groups=gr...  29.9 us
    pallas_call x9, Pallas kernels, call(): pl.pallas_call(kernel, out_shape=out_shape, scratch_shapes=list(scratch),...  11.5 us
    unnamed x42, local copies, waits for them, and re-layouts  8.37 us
  transfers between devices with their start and end apart: 18, of which 14 were waited for; matrix products, arithmetic and copies ran while one was open for 0% of the time, Pallas kernels for 1%

profile of v3, /device:TPU:96, one launch (start us, length us, event | category | flops | bytes accessed | tf_op | source)
XLA Modules:
  0.0 289.5 jit_solution(16039807054572244310)
XLA Ops:
  0.6 3.5 %collective-permute-start = (bf16[320,256]{1,0:T(8,128)(2,1)}, bf16[320,256]{1,0:T(8,128)(2,1)S(1)}, u32[]{:S(2)}, u32[]{:S(2)}) collective-permute-start(bf16[320,256]{1,0:T(8,128)(2,1)} %bitcast.29), channel_id=1, source_target_pairs={{0,32},{32,0},{64,96},{96,64},{128,160},{160,128},{192,224},{224,1... | collective-permute-start | bytes 491528 | tf_op jit(solution)/shard_map/tokens/ppermute | solution.py:183
  4.1 4.1 %collective-permute-start.1 = (bf16[320,256]{1,0:T(8,128)(2,1)}, bf16[320,256]{1,0:T(8,128)(2,1)S(1)}, u32[]{:S(2)}, u32[]{:S(2)}) collective-permute-start(bf16[320,256]{1,0:T(8,128)(2,1)} %bitcast.30), channel_id=1, source_target_pairs={{0,96},{32,64},{64,32},{96,0},{128,224},{160,192},{192,160},{224,1... | collective-permute-start | bytes 491528 | tf_op jit(solution)/shard_map/tokens/ppermute | solution.py:183
  8.2 2.6 collective-permute-start.2
  11.0 4.2 %collective-permute-done.1.t2 = bf16[320,256]{1,0:T(8,128)(2,1)S(1)} collective-permute-done((bf16[320,256]{1,0:T(8,128)(2,1)}, bf16[320,256]{1,0:T(8,128)(2,1)S(1)}, u32[]{:S(2)}, u32[]{:S(2)}) %collective-permute-start.1) | collective-permute-done | bytes 163872 | tf_op jit(solution)/shard_map/tokens/ppermute | solution.py:183
  15.2 2.0 collective-permute-done.2.t3
  21.8 28.3 %all-to-all-start = ((bf16[64,2,3200]{2,1,0:T(2,128)(2,1)}), bf16[64,2,3200]{2,1,0:T(2,128)(2,1)}, u32[]{:S(2)}, u32[]{:S(2)}) async-start(bf16[64,2,3200]{2,1,0:T(2,128)(2,1)} %reshape.37), calls=%async_computation | async-start | bytes 1638400 | tf_op jit(solution)/shard_map/dispatch/all_to_all | solution.py:179
  50.3 3.6 %collective-permute-start.4 = (bf16[320,1536]{1,0:T(8,128)(2,1)S(1)}, bf16[320,1536]{1,0:T(8,128)(2,1)S(1)}, u32[]{:S(2)}, u32[]{:S(2)}) collective-permute-start(bf16[320,1536]{1,0:T(8,128)(2,1)S(1)} %get-tuple-element.48), channel_id=1, source_target_pairs={{0,96},{32,64},{64,32},{96,0},{128,224},{160,192},{192,160},{224,1... | collective-permute-start | bytes 2949128 | tf_op jit(solution)/shard_map/gather/ppermute | solution.py:183
  55.9 3.6 %collective-permute-start.7 = (bf16[320,768]{1,0:T(8,128)(2,1)S(1)}, bf16[320,768]{1,0:T(8,128)(2,1)S(1)}, u32[]{:S(2)}, u32[]{:S(2)}) collective-permute-start(bf16[320,768]{1,0:T(8,128)(2,1)S(1)} %get-tuple-element.50), channel_id=1, source_target_pairs={{0,96},{32,64},{64,32},{96,0},{128,224},{160,192},{192,160},{224,1... | collective-permute-start | bytes 1474568 | tf_op jit(solution)/shard_map/gather/ppermute | solution.py:183
  59.6 18.6 %collective-permute-done.4.w2 = bf16[320,1536]{1,0:T(8,128)(2,1)S(1)} collective-permute-done((bf16[320,1536]{1,0:T(8,128)(2,1)S(1)}, bf16[320,1536]{1,0:T(8,128)(2,1)S(1)}, u32[]{:S(2)}, u32[]{:S(2)}) %collective-permute-start.4) | collective-permute-done | bytes 983072 | tf_op jit(solution)/shard_map/gather/ppermute | solution.py:183
  80.0 3.9 %collective-permute-start.6 = (bf16[320,768]{1,0:T(8,128)(2,1)S(1)}, bf16[320,768]{1,0:T(8,128)(2,1)S(1)}, u32[]{:S(2)}, u32[]{:S(2)}) collective-permute-start(bf16[320,768]{1,0:T(8,128)(2,1)S(1)} %get-tuple-element.33.w0), channel_id=1, source_target_pairs={{0,32},{32,0},{64,96},{96,64},{128,160},{160,128},{192,224},{224,1... | collective-permute-start | bytes 1474568 | tf_op jit(solution)/shard_map/gather/ppermute | solution.py:183
  84.0 4.0 %collective-permute-done.7.w2 = bf16[320,768]{1,0:T(8,128)(2,1)S(1)} collective-permute-done((bf16[320,768]{1,0:T(8,128)(2,1)S(1)}, bf16[320,768]{1,0:T(8,128)(2,1)S(1)}, u32[]{:S(2)}, u32[]{:S(2)}) %collective-permute-start.7) | collective-permute-done | bytes 491552 | tf_op jit(solution)/shard_map/gather/ppermute | solution.py:183
  90.7 24.6 %collective-permute-done.6.w1 = bf16[320,768]{1,0:T(8,128)(2,1)S(1)} collective-permute-done((bf16[320,768]{1,0:T(8,128)(2,1)S(1)}, bf16[320,768]{1,0:T(8,128)(2,1)S(1)}, u32[]{:S(2)}, u32[]{:S(2)}) %collective-permute-start.6) | collective-permute-done | bytes 491552 | tf_op jit(solution)/shard_map/gather/ppermute | solution.py:183
  117.0 6.6 %collective-permute-done.8.w3 = bf16[320,768]{1,0:T(8,128)(2,1)S(1)} collective-permute-done((bf16[320,768]{1,0:T(8,128)(2,1)S(1)}, bf16[320,768]{1,0:T(8,128)(2,1)S(1)}, u32[]{:S(2)}, u32[]{:S(2)}) %collective-permute-start.8) | collective-permute-done | bytes 491552 | tf_op jit(solution)/shard_map/gather/ppermute | solution.py:183
  125.3 11.0 %all-to-all-done = bf16[64,2,3200]{2,1,0:T(2,128)(2,1)} async-done(((bf16[64,2,3200]{2,1,0:T(2,128)(2,1)}), bf16[64,2,3200]{2,1,0:T(2,128)(2,1)}, u32[]{:S(2)}, u32[]{:S(2)}) %all-to-all-start) | async-done | bytes 819232 | tf_op jit(solution)/shard_map/dispatch/all_to_all | solution.py:179
  136.3 2.3 reshape.38.rows_ref
  141.1 2.6 up.1
  143.7 18.9 %all_to_all.20.parts_ref = bf16[4,80,1536]{2,1,0:T(8,128)(2,1)S(1)} all-to-all(bf16[4,80,1536]{2,1,0:T(8,128)(2,1)S(1)} %bitcast.27), channel_id=1, replica_groups={{0,128,256,384},{32,160,288,416},{64,192,320,448},{96,224,352,480},{1,1..., dimensions={0} | all-to-all | bytes 1966080 | tf_op jit(solution)/shard_map/up/all_to_all | solution.py:179
  162.8 11.0 %all_to_all.21 = bf16[4,80,768]{2,1,0:T(8,128)(2,1)S(1)} all-to-all(bf16[4,80,768]{2,1,0:T(8,128)(2,1)S(1)} %hidden.1), channel_id=1, replica_groups={{0,128,256,384},{32,160,288,416},{64,192,320,448},{96,224,352,480},{1,1..., dimensions={0} | all-to-all | bytes 983040 | tf_op jit(solution)/shard_map/hidden/all_to_all | solution.py:179
  176.6 8.6 %all-to-all-start.3 = ((bf16[64,2,3200]{2,1,0:T(2,128)(2,1)}), bf16[64,2,3200]{2,1,0:T(2,128)(2,1)S(1)}, u32[]{:S(2)}, u32[]{:S(2)}) async-start(bf16[64,2,3200]{2,1,0:T(2,128)(2,1)} %reshape.41), calls=%async_computation.3 | async-start | bytes 1638400 | tf_op jit(solution)/shard_map/down/all_to_all | solution.py:179
  186.5 2.8 collective-permute-start.9
  189.3 9.0 %collective-permute-done.9 = bf16[8,32,512]{2,1,0:T(8,128)(2,1)S(1)} collective-permute-done((bf16[8,32,512]{2,1,0:T(8,128)(2,1)S(1)}, bf16[8,32,512]{2,1,0:T(8,128)(2,1)S(1)}, u32[]{:S(2)}, u32[]{:S(2)}) %collective-permute-start.9) | collective-permute-done | bytes 262176 | tf_op jit(solution)/shard_map/latent/ppermute | solution.py:183
  198.4 2.5 collective-permute-start.10
  200.9 4.4 %collective-permute-done.10 = bf16[4,32,512]{2,1,0:T(8,128)(2,1)S(1)} collective-permute-done((bf16[4,32,512]{2,1,0:T(8,128)(2,1)S(1)}, bf16[4,32,512]{2,1,0:T(8,128)(2,1)S(1)}, u32[]{:S(2)}, u32[]{:S(2)}) %collective-permute-start.10) | collective-permute-done | bytes 131104 | tf_op jit(solution)/shard_map/latent/ppermute | solution.py:183
  205.4 3.5 %collective-permute-start.11 = (bf16[2,32,512]{2,1,0:T(8,128)(2,1)S(1)}, bf16[2,32,512]{2,1,0:T(8,128)(2,1)S(1)}, u32[]{:S(2)}, u32[]{:S(2)}) collective-permute-start(bf16[2,32,512]{2,1,0:T(8,128)(2,1)S(1)} %broadcast_select_fusion.3), channel_id=1, source_target_pairs={{0,64},{32,96},{64,0},{96,32},{128,192},{160,224},{192,128},{224,1... | collective-permute-start | bytes 196616 | tf_op jit(solution)/shard_map/latent/ppermute | solution.py:183
  208.9 4.2 %collective-permute-done.11 = bf16[2,32,512]{2,1,0:T(8,128)(2,1)S(1)} collective-permute-done((bf16[2,32,512]{2,1,0:T(8,128)(2,1)S(1)}, bf16[2,32,512]{2,1,0:T(8,128)(2,1)S(1)}, u32[]{:S(2)}, u32[]{:S(2)}) %collective-permute-start.11) | collective-permute-done | bytes 65568 | tf_op jit(solution)/shard_map/latent/ppermute | solution.py:183
  213.1 2.5 collective-permute-start.12
  216.5 2.3 collective-permute-done.12
  219.6 51.9 %all-to-all-done.3 = bf16[64,2,3200]{2,1,0:T(2,128)(2,1)S(1)} async-done(((bf16[64,2,3200]{2,1,0:T(2,128)(2,1)}), bf16[64,2,3200]{2,1,0:T(2,128)(2,1)S(1)}, u32[]{:S(2)}, u32[]{:S(2)}) %all-to-all-start.3) | async-done | bytes 819232 | tf_op jit(solution)/shard_map/down/all_to_all | solution.py:179
  273.7 2.5 collective-permute-start.13
  276.2 3.5 %collective-permute-start.14 = (bf16[320,256]{1,0:T(8,128)(2,1)S(1)}, bf16[320,256]{1,0:T(8,128)(2,1)S(1)}, u32[]{:S(2)}, u32[]{:S(2)}) collective-permute-start(bf16[320,256]{1,0:T(8,128)(2,1)S(1)} %get-tuple-element.45), channel_id=1, source_target_pairs={{0,96},{32,64},{64,32},{96,0},{128,224},{160,192},{192,160},{224,1... | collective-permute-start | bytes 491528 | tf_op jit(solution)/shard_map/mix/ppermute | solution.py:183
  279.7 3.8 %collective-permute-start.15 = (bf16[320,256]{1,0:T(8,128)(2,1)S(1)}, bf16[320,256]{1,0:T(8,128)(2,1)S(1)}, u32[]{:S(2)}, u32[]{:S(2)}) collective-permute-start(bf16[320,256]{1,0:T(8,128)(2,1)S(1)} %get-tuple-element.46), channel_id=1, source_target_pairs={{0,64},{32,96},{64,0},{96,32},{128,192},{160,224},{192,128},{224,1... | collective-permute-start | bytes 491528 | tf_op jit(solution)/shard_map/mix/ppermute | solution.py:183
  285.3 3.5 %collective-permute-done.15.c_ref = bf16[320,256]{1,0:T(8,128)(2,1)S(1)} collective-permute-done((bf16[320,256]{1,0:T(8,128)(2,1)S(1)}, bf16[320,256]{1,0:T(8,128)(2,1)S(1)}, u32[]{:S(2)}, u32[]{:S(2)}) %collective-permute-start.15) | collective-permute-done | bytes 163872 | tf_op jit(solution)/shard_map/mix/ppermute | solution.py:183
  (72 shorter events, 28.1 us)
Async XLA Ops:
  0.6 10.4 %collective-permute-start = (bf16[320,256]{1,0:T(8,128)(2,1)}, bf16[320,256]{1,0:T(8,128)(2,1)S(1)}, u32[]{:S(2)}, u32[]{:S(2)}) collective-permute-start(bf16[320,256]{1,0:T(8,128)(2,1)} %bitcast.29), channel_id=1, source_target_pairs={{0,32},{32,0},{64,96},{96,64},{128,160},{160,128},{192,224},{224,1... | collective-permute-start | bytes 491528 | tf_op jit(solution)/shard_map/tokens/ppermute | solution.py:183
  4.1 11.1 %collective-permute-start.1 = (bf16[320,256]{1,0:T(8,128)(2,1)}, bf16[320,256]{1,0:T(8,128)(2,1)S(1)}, u32[]{:S(2)}, u32[]{:S(2)}) collective-permute-start(bf16[320,256]{1,0:T(8,128)(2,1)} %bitcast.30), channel_id=1, source_target_pairs={{0,96},{32,64},{64,32},{96,0},{128,224},{160,192},{192,160},{224,1... | collective-permute-start | bytes 491528 | tf_op jit(solution)/shard_map/tokens/ppermute | solution.py:183
  8.2 9.0 %collective-permute-start.2 = (bf16[320,256]{1,0:T(8,128)(2,1)}, bf16[320,256]{1,0:T(8,128)(2,1)S(1)}, u32[]{:S(2)}, u32[]{:S(2)}) collective-permute-start(bf16[320,256]{1,0:T(8,128)(2,1)} %bitcast.31), channel_id=1, source_target_pairs={{0,64},{32,96},{64,0},{96,32},{128,192},{160,224},{192,128},{224,1... | collective-permute-start | bytes 491528 | tf_op jit(solution)/shard_map/tokens/ppermute | solution.py:183
  20.6 29.5 %copy-start.19 = (bf16[2,320,1536]{2,1,0:T(8,128)(2,1)S(1)}, bf16[2,320,1536]{2,1,0:T(8,128)(2,1)}, u32[]{:S(2)}) copy-start(bf16[2,320,1536]{2,1,0:T(8,128)(2,1)} %param.12) | copy-start | bytes 5898244
  21.8 114.5 %all-to-all-start = ((bf16[64,2,3200]{2,1,0:T(2,128)(2,1)}), bf16[64,2,3200]{2,1,0:T(2,128)(2,1)}, u32[]{:S(2)}, u32[]{:S(2)}) async-start(bf16[64,2,3200]{2,1,0:T(2,128)(2,1)} %reshape.37), calls=%async_computation | async-start | bytes 1638400 | tf_op jit(solution)/shard_map/dispatch/all_to_all | solution.py:179
  50.1 5.7 %copy-start.20 = (bf16[2,768,320]{1,2,0:T(8,128)(2,1)S(1)}, bf16[2,768,320]{1,2,0:T(8,128)(2,1)}, u32[]{:S(2)}) copy-start(bf16[2,768,320]{1,2,0:T(8,128)(2,1)} %param.13) | copy-start | bytes 2949124
  50.3 27.8 %collective-permute-start.4 = (bf16[320,1536]{1,0:T(8,128)(2,1)S(1)}, bf16[320,1536]{1,0:T(8,128)(2,1)S(1)}, u32[]{:S(2)}, u32[]{:S(2)}) collective-permute-start(bf16[320,1536]{1,0:T(8,128)(2,1)S(1)} %get-tuple-element.48), channel_id=1, source_target_pairs={{0,96},{32,64},{64,32},{96,0},{128,224},{160,192},{192,160},{224,1... | collective-permute-start | bytes 2949128 | tf_op jit(solution)/shard_map/gather/ppermute | solution.py:183
  53.9 62.1 %collective-permute-start.3 = (bf16[320,1536]{1,0:T(8,128)(2,1)S(1)}, bf16[320,1536]{1,0:T(8,128)(2,1)S(1)}, u32[]{:S(2)}, u32[]{:S(2)}) collective-permute-start(bf16[320,1536]{1,0:T(8,128)(2,1)S(1)} %get-tuple-element.29.w0), channel_id=1, source_target_pairs={{0,32},{32,0},{64,96},{96,64},{128,160},{160,128},{192,224},{224,1... | collective-permute-start | bytes 2949128 | tf_op jit(solution)/shard_map/gather/ppermute | solution.py:183
  55.9 32.0 %collective-permute-start.7 = (bf16[320,768]{1,0:T(8,128)(2,1)S(1)}, bf16[320,768]{1,0:T(8,128)(2,1)S(1)}, u32[]{:S(2)}, u32[]{:S(2)}) collective-permute-start(bf16[320,768]{1,0:T(8,128)(2,1)S(1)} %get-tuple-element.50), channel_id=1, source_target_pairs={{0,96},{32,64},{64,32},{96,0},{128,224},{160,192},{192,160},{224,1... | collective-permute-start | bytes 1474568 | tf_op jit(solution)/shard_map/gather/ppermute | solution.py:183
  78.1 46.2 %collective-permute-start.5 = (bf16[320,1536]{1,0:T(8,128)(2,1)S(1)}, bf16[320,1536]{1,0:T(8,128)(2,1)S(1)}, u32[]{:S(2)}, u32[]{:S(2)}) collective-permute-start(bf16[320,1536]{1,0:T(8,128)(2,1)S(1)} %collective-permute-done.4.w2), channel_id=1, source_target_pairs={{0,32},{32,0},{64,96},{96,64},{128,160},{160,128},{192,224},{224,1... | collective-permute-start | bytes 2949128 | tf_op jit(solution)/shard_map/gather/ppermute | solution.py:183
  80.0 35.2 %collective-permute-start.6 = (bf16[320,768]{1,0:T(8,128)(2,1)S(1)}, bf16[320,768]{1,0:T(8,128)(2,1)S(1)}, u32[]{:S(2)}, u32[]{:S(2)}) collective-permute-start(bf16[320,768]{1,0:T(8,128)(2,1)S(1)} %get-tuple-element.33.w0), channel_id=1, source_target_pairs={{0,32},{32,0},{64,96},{96,64},{128,160},{160,128},{192,224},{224,1... | collective-permute-start | bytes 1474568 | tf_op jit(solution)/shard_map/gather/ppermute | solution.py:183
  88.0 35.6 %collective-permute-start.8 = (bf16[320,768]{1,0:T(8,128)(2,1)S(1)}, bf16[320,768]{1,0:T(8,128)(2,1)S(1)}, u32[]{:S(2)}, u32[]{:S(2)}) collective-permute-start(bf16[320,768]{1,0:T(8,128)(2,1)S(1)} %collective-permute-done.7.w2), channel_id=1, source_target_pairs={{0,32},{32,0},{64,96},{96,64},{128,160},{160,128},{192,224},{224,1... | collective-permute-start | bytes 1474568 | tf_op jit(solution)/shard_map/gather/ppermute | solution.py:183
  138.7 1.2 copy-start.1
  139.9 1.2 copy-start.3
  143.7 30.1 %copy-start.5 = (bf16[320,768]{1,0:T(8,128)(2,1)S(1)}, bf16[320,768]{1,0:T(8,128)(2,1)}, u32[]{:S(2)}) copy-start(bf16[320,768]{1,0:T(8,128)(2,1)} %copy-done.4) | copy-start | bytes 1474564
  143.7 30.1 %copy-start.7 = (bf16[320,768]{1,0:T(8,128)(2,1)S(1)}, bf16[320,768]{1,0:T(8,128)(2,1)}, u32[]{:S(2)}) copy-start(bf16[320,768]{1,0:T(8,128)(2,1)} %copy-done.6) | copy-start | bytes 1474564
  143.7 30.1 %copy-start.9 = (bf16[320,768]{1,0:T(8,128)(2,1)S(1)}, bf16[320,768]{1,0:T(8,128)(2,1)}, u32[]{:S(2)}) copy-start(bf16[320,768]{1,0:T(8,128)(2,1)} %copy-done.8) | copy-start | bytes 1474564
  175.3 9.9 %copy-start.10 = (bf16[320,512]{1,0:T(8,128)(2,1)S(1)}, bf16[320,512]{1,0:T(8,128)(2,1)}, u32[]{:S(2)}) copy-start(bf16[320,512]{1,0:T(8,128)(2,1)} %weight_ref.1) | copy-start | bytes 983044
  175.4 9.9 %copy-start.12 = (bf16[256,320]{0,1:T(8,128)(2,1)S(1)}, bf16[256,320]{0,1:T(8,128)(2,1)}, u32[]{:S(2)}) copy-start(bf16[256,320]{0,1:T(8,128)(2,1)} %param.9) | copy-start | bytes 491524
  175.4 9.9 %copy-start.14 = (s32[1,16]{1,0:T(1,128)S(1)}, s32[1,16]{1,0:T(1,128)}, u32[]{:S(2)}) copy-start(s32[1,16]{1,0:T(1,128)} %lengths_ref.1) | copy-start | bytes 196
  175.4 9.9 %copy-start.15 = (s32[1,16]{1,0:T(1,128)S(1)}, s32[1,16]{1,0:T(1,128)}, u32[]{:S(2)}) copy-start(s32[1,16]{1,0:T(1,128)} %placement_ref.1) | copy-start | bytes 196
  176.6 94.9 %all-to-all-start.3 = ((bf16[64,2,3200]{2,1,0:T(2,128)(2,1)}), bf16[64,2,3200]{2,1,0:T(2,128)(2,1)S(1)}, u32[]{:S(2)}, u32[]{:S(2)}) async-start(bf16[64,2,3200]{2,1,0:T(2,128)(2,1)} %reshape.41), calls=%async_computation.3 | async-start | bytes 1638400 | tf_op jit(solution)/shard_map/down/all_to_all | solution.py:179
  185.3 30.3 %copy-start.17 = (s32[256,4]{0,1:T(4,128)S(1)}, s32[256,4]{0,1:T(4,128)}, u32[]{:S(2)}) copy-start(s32[256,4]{0,1:T(4,128)} %param.10) | copy-start | bytes 12292
  185.3 30.3 %copy-start.18 = (f32[256,4]{0,1:T(4,128)S(1)}, f32[256,4]{0,1:T(4,128)}, u32[]{:S(2)}) copy-start(f32[256,4]{0,1:T(4,128)} %param.11) | copy-start | bytes 12292
  186.4 32.5 %copy-start.13 = (f32[512]{0:T(512)S(1)}, f32[512]{0:T(512)}, u32[]{:S(2)}) copy-start(f32[512]{0:T(512)} %param.15) | copy-start | bytes 6148
  186.5 11.8 %collective-permute-start.9 = (bf16[8,32,512]{2,1,0:T(8,128)(2,1)S(1)}, bf16[8,32,512]{2,1,0:T(8,128)(2,1)S(1)}, u32[]{:S(2)}, u32[]{:S(2)}) collective-permute-start(bf16[8,32,512]{2,1,0:T(8,128)(2,1)S(1)} %bitcast.39), channel_id=1, source_target_pairs={{0,256},{32,288},{64,320},{96,352},{128,384},{160,416},{192,448},{... | collective-permute-start | bytes 786440 | tf_op jit(solution)/shard_map/latent/ppermute | solution.py:183
  198.4 6.9 %collective-permute-start.10 = (bf16[4,32,512]{2,1,0:T(8,128)(2,1)S(1)}, bf16[4,32,512]{2,1,0:T(8,128)(2,1)S(1)}, u32[]{:S(2)}, u32[]{:S(2)}) collective-permute-start(bf16[4,32,512]{2,1,0:T(8,128)(2,1)S(1)} %broadcast_select_fusion.2), channel_id=1, source_target_pairs={{0,128},{32,160},{64,192},{96,224},{128,0},{160,32},{192,64},{224,... | collective-permute-start | bytes 393224 | tf_op jit(solution)/shard_map/latent/ppermute | solution.py:183
  205.4 7.7 %collective-permute-start.11 = (bf16[2,32,512]{2,1,0:T(8,128)(2,1)S(1)}, bf16[2,32,512]{2,1,0:T(8,128)(2,1)S(1)}, u32[]{:S(2)}, u32[]{:S(2)}) collective-permute-start(bf16[2,32,512]{2,1,0:T(8,128)(2,1)S(1)} %broadcast_select_fusion.3), channel_id=1, source_target_pairs={{0,64},{32,96},{64,0},{96,32},{128,192},{160,224},{192,128},{224,1... | collective-permute-start | bytes 196616 | tf_op jit(solution)/shard_map/latent/ppermute | solution.py:183
  213.1 5.8 %collective-permute-start.12 = (bf16[1,32,512]{2,1,0:T(8,128)(2,1)S(1)}, bf16[1,32,512]{2,1,0:T(8,128)(2,1)S(1)}, u32[]{:S(2)}, u32[]{:S(2)}) collective-permute-start(bf16[1,32,512]{2,1,0:T(8,128)(2,1)S(1)} %broadcast_select_fusion.4), channel_id=1, source_target_pairs={{0,32},{32,0},{64,96},{96,64},{128,160},{160,128},{192,224},{224,1... | collective-permute-start | bytes 98312 | tf_op jit(solution)/shard_map/latent/ppermute | solution.py:183
  273.7 9.8 %collective-permute-start.13 = (bf16[320,256]{1,0:T(8,128)(2,1)S(1)}, bf16[320,256]{1,0:T(8,128)(2,1)S(1)}, u32[]{:S(2)}, u32[]{:S(2)}) collective-permute-start(bf16[320,256]{1,0:T(8,128)(2,1)S(1)} %get-tuple-element.44), channel_id=1, source_target_pairs={{0,32},{32,0},{64,96},{96,64},{128,160},{160,128},{192,224},{224,1... | collective-permute-start | bytes 491528 | tf_op jit(solution)/shard_map/mix/ppermute | solution.py:183
  276.2 9.1 %collective-permute-start.14 = (bf16[320,256]{1,0:T(8,128)(2,1)S(1)}, bf16[320,256]{1,0:T(8,128)(2,1)S(1)}, u32[]{:S(2)}, u32[]{:S(2)}) collective-permute-start(bf16[320,256]{1,0:T(8,128)(2,1)S(1)} %get-tuple-element.45), channel_id=1, source_target_pairs={{0,96},{32,64},{64,32},{96,0},{128,224},{160,192},{192,160},{224,1... | collective-permute-start | bytes 491528 | tf_op jit(solution)/shard_map/mix/ppermute | solution.py:183
  279.7 9.1 %collective-permute-start.15 = (bf16[320,256]{1,0:T(8,128)(2,1)S(1)}, bf16[320,256]{1,0:T(8,128)(2,1)S(1)}, u32[]{:S(2)}, u32[]{:S(2)}) collective-permute-start(bf16[320,256]{1,0:T(8,128)(2,1)S(1)} %get-tuple-element.46), channel_id=1, source_target_pairs={{0,64},{32,96},{64,0},{96,32},{128,192},{160,224},{192,128},{224,1... | collective-permute-start | bytes 491528 | tf_op jit(solution)/shard_map/mix/ppermute | solution.py:183
  (7 other events, 5.9 us)

commit v4 on v3

--- a/solution.py
+++ b/solution.py
@@ -133,23 +133,25 @@
     out[...] = rows.astype(BF)
 
 
-def mix_kernel(lanes, back_ref, high_ref, low_ref, own_ref, o1, o2, o3):
-    width, tokens = own_ref.shape
+def mix_kernel(lanes, pick_ref, back_ref, high_ref, low_ref, out):
+    _, width, tokens = out.shape
     span = 2 * width
     total = jnp.zeros((span, 2 * tokens), F32)
     for i in range(lanes):
         rows = back_ref[:, i * span : (i + 1) * span]
         total = total + lax.dot_general(rows, high_ref[i], TN, preferred_element_type=F32)
         total = total + lax.dot_general(rows, low_ref[i], TN, preferred_element_type=F32)
-    own_ref[...] = total[:width, :tokens]
-    o1[...] = total[width:, :tokens].astype(BF)
-    o2[...] = total[:width, tokens:].astype(BF)
-    o3[...] = total[width:, tokens:].astype(BF)
-
-
-def join_kernel(own_ref, a_ref, b_ref, c_ref, out):
-    total = own_ref[...] + a_ref[...].astype(F32) + b_ref[...].astype(F32)
-    out[...] = (total + c_ref[...].astype(F32)).astype(BF)
+    place = pick_ref[2]
+    for k in range(4):
+        at, to = (k % 2) * width, (k // 2) * tokens
+        out[place ^ k] = total[at : at + width, to : to + tokens].astype(BF)
+
+
+def join_kernel(parts_ref, out):
+    total = parts_ref[0].astype(F32)
+    for k in range(1, parts_ref.shape[0]):
+        total = total + parts_ref[k].astype(F32)
+    out[...] = total.astype(BF)
 
 
 def latent_kernel(longest, lengths_ref, placement_ref, tokens_ref, weight_ref, out, select, offset):
@@ -183,10 +185,17 @@
     return lax.ppermute(x, "dp", [(i, i ^ bits) for i in range(lax.axis_size("dp"))])
 
 
+def cosets(size, *flips):
+    reach = [0]
+    for bits in flips:
+        reach += [i ^ bits for i in reach]
+    return sorted({tuple(sorted(i ^ j for j in reach)) for i in range(size)})
+
+
 def gather_expert(array, resident):
     own = lax.dynamic_index_in_dim(array, resident, 0, keepdims=False)
     cross = lax.dynamic_index_in_dim(array, 1 - resident, 0, keepdims=False)
-    second, third = flip(own, 1), flip(cross, 3)
+    second, third = flip(own, 1), flip(cross, 4)
     return own, second, third, flip(third, 1)
 
 
@@ -209,9 +218,8 @@
 ):
     groups = lax.axis_size(SE)
     blocks = lax.axis_size("dp")
-    along_y = 4
-    along_x = blocks // along_y
-    columns = [[y + along_y * x for x in range(along_x)] for y in range(along_y)]
+    near, far = cosets(blocks, 1, 4), cosets(blocks, 3, 12)
+    spread = len(far[0])
     rows, width = tokens.shape
     tops = routes.shape[1]
     residents = w_gate_up.shape[0]
@@ -224,18 +232,20 @@
     slots = 2 * groups
     row = 2 * lanes * width
     taken = lanes * groups
-    share = taken // along_x
+    share = taken // spread
     shape = jax.ShapeDtypeStruct
     tokens_t, routes_t, gates_t = tokens.T, routes.T, route_weights.T
     vmem = pl.BlockSpec(memory_space=pltpu.VMEM)
     smem = pl.BlockSpec(memory_space=pltpu.SMEM)
 
-    at_y = lax.axis_index("dp") % along_y
-    resident = at_y // 2
-    pick = jnp.stack([resident, at_y % 2])
+    here = lax.axis_index("dp")
+    resident = ((here >> 2) ^ (here >> 3)) & 1
+    place = ((here >> 1) & 2) + (here & 1)
+    pick = jnp.stack([resident, (here ^ (here >> 1)) & 1, place])
 
     with jax.named_scope("tokens"):
-        pieces = [tokens_t, flip(tokens_t, 1), flip(tokens_t, 3), flip(tokens_t, 2)]
+        both = flip(tokens_t, 5)
+        pieces = [tokens_t, flip(tokens_t, 1), flip(tokens_t, 4), both]
 
     with jax.named_scope("dispatch"):
         outgoing = call(
@@ -254,9 +264,7 @@
     with jax.named_scope("gather"):
         up_blocks = gather_expert(w_gate_up, resident)
         down_blocks = gather_expert(w_down.transpose(0, 2, 1), resident)
-        arrived, up_blocks, down_blocks = lax.optimization_barrier(
-            (arrived, up_blocks, down_blocks)
-        )
+        arrived, down_blocks = lax.optimization_barrier((arrived, down_blocks))
 
     with jax.named_scope("up"):
         partial = call(
@@ -268,17 +276,17 @@
             flops=16 * taken * width * hidden_units,
             moved=4 * hidden_units * (4 * width + taken),
         )
-        shares = exchange(partial.reshape(along_x, share, 2 * hidden_units), "dp", columns)
+        shares = exchange(partial.reshape(spread, share, 2 * hidden_units), "dp", far)
 
     with jax.named_scope("hidden"):
         hidden = call(
             hidden_kernel,
-            shape((along_x, share, hidden_units), BF),
+            shape((spread, share, hidden_units), BF),
             shares,
             flops=2 * taken * hidden_units,
             moved=6 * taken * hidden_units,
         )
-        gathered = exchange(hidden, "dp", columns)
+        gathered = exchange(hidden, "dp", far)
 
     with jax.named_scope("down"):
         produced = call(
@@ -333,21 +341,22 @@
         back, latent_cache = lax.optimization_barrier((back, latent_cache))
 
     with jax.named_scope("mix"):
-        own, *others = call(
+        parts = call(
             functools.partial(mix_kernel, lanes),
-            [shape((width, rows), F32)] + [shape((width, rows), BF)] * 3,
+            shape((4, width, rows), BF),
+            pick,
             back,
             *gates,
+            in_specs=[smem] + [vmem] * 3,
             flops=32 * taken * width * rows,
             moved=2 * slots * row + 8 * lanes * slots * rows,
         )
         mixed = call(
             join_kernel,
             shape((width, rows), BF),
-            own,
-            *[flip(x, bits) for x, bits in zip(others, (1, 3, 2))],
+            exchange(parts, "dp", near),
             flops=3 * width * rows,
-            moved=12 * width * rows,
+            moved=10 * width * rows,
         )
     return (mixed.T, latent_cache.reshape(1, 1, longest, latent_width))
 

time: 291 us -> 291 us (level)
  blocking collectives: 29.9 us -> 47.3 us
  starting transfers between devices: 85.1 us -> 71.5 us
  local copies, waits for them, and re-layouts: 13.6 us -> 9.29 us
    all_to_all x2 -> x3, blocking collectives: 29.9 us -> 47.3 us  [exchange(): lax.all_to_all(x, axes, split_axis=0, concat_axis=0, axis_index_groups=gr...]
    ppermute x16 -> x13, starting transfers between devices: 48.2 us -> 34.4 us  [flip(): lax.ppermute(x, 'dp', [(i, i ^ bits) for i in range(lax.axis_size('dp'))])]
    unnamed x42 -> x34, local copies, waits for them, and re-layouts: 8.37 us -> 4.03 us
    ppermute x16 -> x13, waiting for transfers between devices: 85 us -> 83.6 us  [flip(): lax.ppermute(x, 'dp', [(i, i ^ bits) for i in range(lax.axis_size('dp'))])]
  transfers between devices with their start and end apart: 18 -> 15, of which waited for: 14 -> 12; matrix products, arithmetic and copies ran while one was open for 0% -> 1% of each run, Pallas kernels for 1% -> 1%
where the time goes in v4:
time: 291 us; the launch traced here: 290 us
  waiting for transfers between devices  147 us (51%)
  starting transfers between devices  71.5 us (25%)
  blocking collectives  47.3 us (16%)
  Pallas kernels  13.6 us (5%)
  local copies, waits for them, and re-layouts  9.29 us (3%)
    ppermute x13, waiting for transfers between devices, flip(): lax.ppermute(x, 'dp', [(i, i ^ bits) for i in range(lax.axis_size('dp'))])  83.6 us
    all_to_all x2, waiting for transfers between devices, exchange(): lax.all_to_all(x, axes, split_axis=0, concat_axis=0, axis_index_groups=gr...  63.7 us
    all_to_all x3, blocking collectives, exchange(): lax.all_to_all(x, axes, split_axis=0, concat_axis=0, axis_index_groups=gr...  47.3 us
    all_to_all x2, starting transfers between devices, exchange(): lax.all_to_all(x, axes, split_axis=0, concat_axis=0, axis_index_groups=gr...  37.1 us
    ppermute x13, starting transfers between devices, flip(): lax.ppermute(x, 'dp', [(i, i ^ bits) for i in range(lax.axis_size('dp'))])  34.4 us
    pallas_call x9, Pallas kernels, call(): pl.pallas_call(kernel, out_shape=out_shape, scratch_shapes=list(scratch),...  13.6 us
  transfers between devices with their start and end apart: 15, of which 12 were waited for; matrix products, arithmetic and copies ran while one was open for 1% of the time, Pallas kernels for 1%

profile of v4, /device:TPU:96, one launch (start us, length us, event | category | flops | bytes accessed | tf_op | source)
XLA Modules:
  0.0 290.4 jit_solution(9298429377732781245)
XLA Ops:
  0.6 3.5 %collective-permute-start = (bf16[320,256]{1,0:T(8,128)(2,1)}, bf16[320,256]{1,0:T(8,128)(2,1)S(1)}, u32[]{:S(2)}, u32[]{:S(2)}) collective-permute-start(bf16[320,256]{1,0:T(8,128)(2,1)} %bitcast.30), channel_id=1, source_target_pairs={{0,32},{32,0},{64,96},{96,64},{128,160},{160,128},{192,224},{224,1... | collective-permute-start | bytes 491528 | tf_op jit(solution)/shard_map/tokens/ppermute | solution.py:185
  4.1 3.4 %collective-permute-start.1 = (bf16[320,256]{1,0:T(8,128)(2,1)}, bf16[320,256]{1,0:T(8,128)(2,1)S(1)}, u32[]{:S(2)}, u32[]{:S(2)}) collective-permute-start(bf16[320,256]{1,0:T(8,128)(2,1)} %bitcast.31), channel_id=1, source_target_pairs={{0,128},{32,160},{64,192},{96,224},{128,0},{160,32},{192,64},{224,... | collective-permute-start | bytes 491528 | tf_op jit(solution)/shard_map/tokens/ppermute | solution.py:185
  7.5 2.3 collective-permute-start.2
  10.0 2.5 collective-permute-done.1.t2
  12.5 3.5 %collective-permute-done.2.t3 = bf16[320,256]{1,0:T(8,128)(2,1)S(1)} collective-permute-done((bf16[320,256]{1,0:T(8,128)(2,1)}, bf16[320,256]{1,0:T(8,128)(2,1)S(1)}, u32[]{:S(2)}, u32[]{:S(2)}) %collective-permute-start.2) | collective-permute-done | bytes 163872 | tf_op jit(solution)/shard_map/tokens/ppermute | solution.py:185
  20.5 28.3 %all-to-all-start = ((bf16[64,2,3200]{2,1,0:T(2,128)(2,1)}), bf16[64,2,3200]{2,1,0:T(2,128)(2,1)}, u32[]{:S(2)}, u32[]{:S(2)}) async-start(bf16[64,2,3200]{2,1,0:T(2,128)(2,1)} %reshape.37), calls=%async_computation | async-start | bytes 1638400 | tf_op jit(solution)/shard_map/dispatch/all_to_all | solution.py:181
  49.0 2.9 collective-permute-start.7
  52.0 3.1 %collective-permute-start.4 = (bf16[320,768]{1,0:T(8,128)(2,1)S(1)}, bf16[320,768]{1,0:T(8,128)(2,1)S(1)}, u32[]{:S(2)}, u32[]{:S(2)}) collective-permute-start(bf16[320,768]{1,0:T(8,128)(2,1)S(1)} %get-tuple-element.34), channel_id=1, source_target_pairs={{0,128},{32,160},{64,192},{96,224},{128,0},{160,32},{192,64},{224,... | collective-permute-start | bytes 1474568 | tf_op jit(solution)/shard_map/gather/ppermute | solution.py:185
  55.1 2.9 collective-permute-start.6
  57.9 17.7 %collective-permute-done.7.w2 = bf16[320,1536]{1,0:T(8,128)(2,1)S(1)} collective-permute-done((bf16[320,1536]{1,0:T(8,128)(2,1)S(1)}, bf16[320,1536]{1,0:T(8,128)(2,1)S(1)}, u32[]{:S(2)}, u32[]{:S(2)}) %collective-permute-start.7) | collective-permute-done | bytes 983072 | tf_op jit(solution)/shard_map/gather/ppermute | solution.py:185
  75.6 2.9 collective-permute-start.8
  78.5 3.0 %collective-permute-start.3 = (bf16[320,768]{1,0:T(8,128)(2,1)S(1)}, bf16[320,768]{1,0:T(8,128)(2,1)S(1)}, u32[]{:S(2)}, u32[]{:S(2)}) collective-permute-start(bf16[320,768]{1,0:T(8,128)(2,1)S(1)} %get-tuple-element.21.w0), channel_id=1, source_target_pairs={{0,32},{32,0},{64,96},{96,64},{128,160},{160,128},{192,224},{224,1... | collective-permute-start | bytes 1474568 | tf_op jit(solution)/shard_map/gather/ppermute | solution.py:185
  81.4 4.0 %collective-permute-done.4.w2 = bf16[320,768]{1,0:T(8,128)(2,1)S(1)} collective-permute-done((bf16[320,768]{1,0:T(8,128)(2,1)S(1)}, bf16[320,768]{1,0:T(8,128)(2,1)S(1)}, u32[]{:S(2)}, u32[]{:S(2)}) %collective-permute-start.4) | collective-permute-done | bytes 491552 | tf_op jit(solution)/shard_map/gather/ppermute | solution.py:185
  85.4 2.9 collective-permute-start.5
  89.1 24.1 %collective-permute-done.3.w1 = bf16[320,768]{1,0:T(8,128)(2,1)S(1)} collective-permute-done((bf16[320,768]{1,0:T(8,128)(2,1)S(1)}, bf16[320,768]{1,0:T(8,128)(2,1)S(1)}, u32[]{:S(2)}, u32[]{:S(2)}) %collective-permute-start.3) | collective-permute-done | bytes 491552 | tf_op jit(solution)/shard_map/gather/ppermute | solution.py:185
  114.0 8.4 %collective-permute-done.5.w3 = bf16[320,768]{1,0:T(8,128)(2,1)S(1)} collective-permute-done((bf16[320,768]{1,0:T(8,128)(2,1)S(1)}, bf16[320,768]{1,0:T(8,128)(2,1)S(1)}, u32[]{:S(2)}, u32[]{:S(2)}) %collective-permute-start.5) | collective-permute-done | bytes 491552 | tf_op jit(solution)/shard_map/gather/ppermute | solution.py:185
  123.2 11.8 %all-to-all-done = bf16[64,2,3200]{2,1,0:T(2,128)(2,1)} async-done(((bf16[64,2,3200]{2,1,0:T(2,128)(2,1)}), bf16[64,2,3200]{2,1,0:T(2,128)(2,1)}, u32[]{:S(2)}, u32[]{:S(2)}) %all-to-all-start) | async-done | bytes 819232 | tf_op jit(solution)/shard_map/dispatch/all_to_all | solution.py:181
  135.0 2.3 reshape.38.rows_ref
  137.4 4.1 %up.1 = bf16[320,1536]{1,0:T(8,128)(2,1)S(1)} custom-call(bf16[128,3200]{1,0:T(8,128)(2,1)S(1)} %reshape.38.rows_ref, bf16[320,1536]{1,0:T(8,128)(2,1)S(1)} %get-tuple-element.33.w0, bf16[320,1536]{1,0:T(8,128)(2,1)} %collective-permute-done.6.w1, bf16[320,1536]{1,0:T(8,128)(2,1)S(1)} %collective-permute-done.7.w2, bf16[320,1536]{1,0:T(8,128)(2,1)} %collective-permute-done.8.w3), custom_call_target="tpu_custom_call" | custom-call | flops 1258291200 | bytes 4915200 | tf_op jit(solution)/shard_map/up/pallas_call | solution.py:22
  141.5 22.1 %all_to_all.25.parts_ref = bf16[4,80,1536]{2,1,0:T(8,128)(2,1)S(1)} all-to-all(bf16[4,80,1536]{2,1,0:T(8,128)(2,1)S(1)} %bitcast.28), channel_id=1, replica_groups={{0,96,384,480},{32,64,416,448},{128,224,256,352},{160,192,288,320},{1,9..., dimensions={0} | all-to-all | bytes 1966080 | tf_op jit(solution)/shard_map/up/all_to_all | solution.py:181
  163.8 12.2 %all_to_all.26 = bf16[4,80,768]{2,1,0:T(8,128)(2,1)S(1)} all-to-all(bf16[4,80,768]{2,1,0:T(8,128)(2,1)S(1)} %hidden.1), channel_id=1, replica_groups={{0,96,384,480},{32,64,416,448},{128,224,256,352},{160,192,288,320},{1,9..., dimensions={0} | all-to-all | bytes 983040 | tf_op jit(solution)/shard_map/hidden/all_to_all | solution.py:181
  178.8 8.8 %all-to-all-start.3 = ((bf16[64,2,3200]{2,1,0:T(2,128)(2,1)}), bf16[64,2,3200]{2,1,0:T(2,128)(2,1)S(1)}, u32[]{:S(2)}, u32[]{:S(2)}) async-start(bf16[64,2,3200]{2,1,0:T(2,128)(2,1)} %reshape.41), calls=%async_computation.3 | async-start | bytes 1638400 | tf_op jit(solution)/shard_map/down/all_to_all | solution.py:181
  188.9 1.9 collective-permute-start.9
  190.9 9.9 %collective-permute-done.9 = bf16[8,32,512]{2,1,0:T(8,128)(2,1)S(1)} collective-permute-done((bf16[8,32,512]{2,1,0:T(8,128)(2,1)S(1)}, bf16[8,32,512]{2,1,0:T(8,128)(2,1)S(1)}, u32[]{:S(2)}, u32[]{:S(2)}) %collective-permute-start.9) | collective-permute-done | bytes 262176 | tf_op jit(solution)/shard_map/latent/ppermute | solution.py:185
  200.9 1.9 collective-permute-start.10
  202.8 4.9 %collective-permute-done.10 = bf16[4,32,512]{2,1,0:T(8,128)(2,1)S(1)} collective-permute-done((bf16[4,32,512]{2,1,0:T(8,128)(2,1)S(1)}, bf16[4,32,512]{2,1,0:T(8,128)(2,1)S(1)}, u32[]{:S(2)}, u32[]{:S(2)}) %collective-permute-start.10) | collective-permute-done | bytes 131104 | tf_op jit(solution)/shard_map/latent/ppermute | solution.py:185
  209.8 5.7 %collective-permute-done.11 = bf16[2,32,512]{2,1,0:T(8,128)(2,1)S(1)} collective-permute-done((bf16[2,32,512]{2,1,0:T(8,128)(2,1)S(1)}, bf16[2,32,512]{2,1,0:T(8,128)(2,1)S(1)}, u32[]{:S(2)}, u32[]{:S(2)}) %collective-permute-start.11) | collective-permute-done | bytes 65568 | tf_op jit(solution)/shard_map/latent/ppermute | solution.py:185
  215.5 1.9 collective-permute-start.12
  218.4 2.9 collective-permute-done.12
  222.1 51.9 %all-to-all-done.3 = bf16[64,2,3200]{2,1,0:T(2,128)(2,1)S(1)} async-done(((bf16[64,2,3200]{2,1,0:T(2,128)(2,1)}), bf16[64,2,3200]{2,1,0:T(2,128)(2,1)S(1)}, u32[]{:S(2)}, u32[]{:S(2)}) %all-to-all-start.3) | async-done | bytes 819232 | tf_op jit(solution)/shard_map/down/all_to_all | solution.py:181
  274.3 2.4 mix.2
  276.7 12.9 %all_to_all.27.parts_ref = bf16[4,320,256]{2,1,0:T(8,128)(2,1)S(1)} all-to-all(bf16[4,320,256]{2,1,0:T(8,128)(2,1)S(1)} %mix.2), channel_id=1, replica_groups={{0,32,128,160},{64,96,192,224},{256,288,384,416},{320,352,448,480},{1,3..., dimensions={0} | all-to-all | bytes 1310720 | tf_op jit(solution)/shard_map/mix/all_to_all | solution.py:181
  (59 shorter events, 16.3 us)
Async XLA Ops:
  0.6 9.3 %collective-permute-start = (bf16[320,256]{1,0:T(8,128)(2,1)}, bf16[320,256]{1,0:T(8,128)(2,1)S(1)}, u32[]{:S(2)}, u32[]{:S(2)}) collective-permute-start(bf16[320,256]{1,0:T(8,128)(2,1)} %bitcast.30), channel_id=1, source_target_pairs={{0,32},{32,0},{64,96},{96,64},{128,160},{160,128},{192,224},{224,1... | collective-permute-start | bytes 491528 | tf_op jit(solution)/shard_map/tokens/ppermute | solution.py:185
  4.1 8.3 %collective-permute-start.1 = (bf16[320,256]{1,0:T(8,128)(2,1)}, bf16[320,256]{1,0:T(8,128)(2,1)S(1)}, u32[]{:S(2)}, u32[]{:S(2)}) collective-permute-start(bf16[320,256]{1,0:T(8,128)(2,1)} %bitcast.31), channel_id=1, source_target_pairs={{0,128},{32,160},{64,192},{96,224},{128,0},{160,32},{192,64},{224,... | collective-permute-start | bytes 491528 | tf_op jit(solution)/shard_map/tokens/ppermute | solution.py:185
  7.5 8.4 %collective-permute-start.2 = (bf16[320,256]{1,0:T(8,128)(2,1)}, bf16[320,256]{1,0:T(8,128)(2,1)S(1)}, u32[]{:S(2)}, u32[]{:S(2)}) collective-permute-start(bf16[320,256]{1,0:T(8,128)(2,1)} %bitcast.32), channel_id=1, source_target_pairs={{0,160},{32,128},{64,224},{96,192},{128,32},{160,0},{192,96},{224,... | collective-permute-start | bytes 491528 | tf_op jit(solution)/shard_map/tokens/ppermute | solution.py:185
  15.9 0.9 copy-start.7
  16.8 0.7 copy-start.12
  19.3 29.5 %copy-start.15 = (bf16[2,320,1536]{2,1,0:T(8,128)(2,1)S(1)}, bf16[2,320,1536]{2,1,0:T(8,128)(2,1)}, u32[]{:S(2)}) copy-start(bf16[2,320,1536]{2,1,0:T(8,128)(2,1)} %param.12) | copy-start | bytes 5898244
  20.5 114.5 %all-to-all-start = ((bf16[64,2,3200]{2,1,0:T(2,128)(2,1)}), bf16[64,2,3200]{2,1,0:T(2,128)(2,1)}, u32[]{:S(2)}, u32[]{:S(2)}) async-start(bf16[64,2,3200]{2,1,0:T(2,128)(2,1)} %reshape.37), calls=%async_computation | async-start | bytes 1638400 | tf_op jit(solution)/shard_map/dispatch/all_to_all | solution.py:181
  48.8 3.1 %copy-start.16 = (bf16[2,768,320]{1,2,0:T(8,128)(2,1)S(1)}, bf16[2,768,320]{1,2,0:T(8,128)(2,1)}, u32[]{:S(2)}) copy-start(bf16[2,768,320]{1,2,0:T(8,128)(2,1)} %param.13) | copy-start | bytes 2949124
  49.0 26.6 %collective-permute-start.7 = (bf16[320,1536]{1,0:T(8,128)(2,1)S(1)}, bf16[320,1536]{1,0:T(8,128)(2,1)S(1)}, u32[]{:S(2)}, u32[]{:S(2)}) collective-permute-start(bf16[320,1536]{1,0:T(8,128)(2,1)S(1)} %get-tuple-element.32), channel_id=1, source_target_pairs={{0,128},{32,160},{64,192},{96,224},{128,0},{160,32},{192,64},{224,... | collective-permute-start | bytes 2949128 | tf_op jit(solution)/shard_map/gather/ppermute | solution.py:185
  52.0 33.5 %collective-permute-start.4 = (bf16[320,768]{1,0:T(8,128)(2,1)S(1)}, bf16[320,768]{1,0:T(8,128)(2,1)S(1)}, u32[]{:S(2)}, u32[]{:S(2)}) collective-permute-start(bf16[320,768]{1,0:T(8,128)(2,1)S(1)} %get-tuple-element.34), channel_id=1, source_target_pairs={{0,128},{32,160},{64,192},{96,224},{128,0},{160,32},{192,64},{224,... | collective-permute-start | bytes 1474568 | tf_op jit(solution)/shard_map/gather/ppermute | solution.py:185
  55.1 82.3 %collective-permute-start.6 = (bf16[320,1536]{1,0:T(8,128)(2,1)S(1)}, bf16[320,1536]{1,0:T(8,128)(2,1)}, u32[]{:S(2)}, u32[]{:S(2)}) collective-permute-start(bf16[320,1536]{1,0:T(8,128)(2,1)S(1)} %get-tuple-element.33.w0), channel_id=1, source_target_pairs={{0,32},{32,0},{64,96},{96,64},{128,160},{160,128},{192,224},{224,1... | collective-permute-start | bytes 2949128 | tf_op jit(solution)/shard_map/gather/ppermute | solution.py:185
  75.6 61.8 %collective-permute-start.8 = (bf16[320,1536]{1,0:T(8,128)(2,1)S(1)}, bf16[320,1536]{1,0:T(8,128)(2,1)}, u32[]{:S(2)}, u32[]{:S(2)}) collective-permute-start(bf16[320,1536]{1,0:T(8,128)(2,1)S(1)} %collective-permute-done.7.w2), channel_id=1, source_target_pairs={{0,32},{32,0},{64,96},{96,64},{128,160},{160,128},{192,224},{224,1... | collective-permute-start | bytes 2949128 | tf_op jit(solution)/shard_map/gather/ppermute | solution.py:185
  78.5 34.8 %collective-permute-start.3 = (bf16[320,768]{1,0:T(8,128)(2,1)S(1)}, bf16[320,768]{1,0:T(8,128)(2,1)S(1)}, u32[]{:S(2)}, u32[]{:S(2)}) collective-permute-start(bf16[320,768]{1,0:T(8,128)(2,1)S(1)} %get-tuple-element.21.w0), channel_id=1, source_target_pairs={{0,32},{32,0},{64,96},{96,64},{128,160},{160,128},{192,224},{224,1... | collective-permute-start | bytes 1474568 | tf_op jit(solution)/shard_map/gather/ppermute | solution.py:185
  85.4 37.0 %collective-permute-start.5 = (bf16[320,768]{1,0:T(8,128)(2,1)S(1)}, bf16[320,768]{1,0:T(8,128)(2,1)S(1)}, u32[]{:S(2)}, u32[]{:S(2)}) collective-permute-start(bf16[320,768]{1,0:T(8,128)(2,1)S(1)} %collective-permute-done.4.w2), channel_id=1, source_target_pairs={{0,32},{32,0},{64,96},{96,64},{128,160},{160,128},{192,224},{224,1... | collective-permute-start | bytes 1474568 | tf_op jit(solution)/shard_map/gather/ppermute | solution.py:185
  88.3 0.8 copy-start
  113.2 0.8 copy-start.2
  122.4 0.8 copy-start.4
  141.5 34.5 %copy-start.1 = (bf16[320,768]{1,0:T(8,128)(2,1)S(1)}, bf16[320,768]{1,0:T(8,128)(2,1)}, u32[]{:S(2)}) copy-start(bf16[320,768]{1,0:T(8,128)(2,1)} %copy-done) | copy-start | bytes 1474564
  141.5 34.5 %copy-start.3 = (bf16[320,768]{1,0:T(8,128)(2,1)S(1)}, bf16[320,768]{1,0:T(8,128)(2,1)}, u32[]{:S(2)}) copy-start(bf16[320,768]{1,0:T(8,128)(2,1)} %copy-done.2) | copy-start | bytes 1474564
  141.5 34.5 %copy-start.5 = (bf16[320,768]{1,0:T(8,128)(2,1)S(1)}, bf16[320,768]{1,0:T(8,128)(2,1)}, u32[]{:S(2)}) copy-start(bf16[320,768]{1,0:T(8,128)(2,1)} %copy-done.4) | copy-start | bytes 1474564
  177.6 10.1 %copy-start.6 = (bf16[320,512]{1,0:T(8,128)(2,1)S(1)}, bf16[320,512]{1,0:T(8,128)(2,1)}, u32[]{:S(2)}) copy-start(bf16[320,512]{1,0:T(8,128)(2,1)} %weight_ref.1) | copy-start | bytes 983044
  177.6 10.1 %copy-start.8 = (bf16[256,320]{0,1:T(8,128)(2,1)S(1)}, bf16[256,320]{0,1:T(8,128)(2,1)}, u32[]{:S(2)}) copy-start(bf16[256,320]{0,1:T(8,128)(2,1)} %param.9) | copy-start | bytes 491524
  177.6 10.1 %copy-start.10 = (s32[1,16]{1,0:T(1,128)S(1)}, s32[1,16]{1,0:T(1,128)}, u32[]{:S(2)}) copy-start(s32[1,16]{1,0:T(1,128)} %lengths_ref.1) | copy-start | bytes 196
  177.6 10.1 %copy-start.11 = (s32[1,16]{1,0:T(1,128)S(1)}, s32[1,16]{1,0:T(1,128)}, u32[]{:S(2)}) copy-start(s32[1,16]{1,0:T(1,128)} %placement_ref.1) | copy-start | bytes 196
  178.8 95.1 %all-to-all-start.3 = ((bf16[64,2,3200]{2,1,0:T(2,128)(2,1)}), bf16[64,2,3200]{2,1,0:T(2,128)(2,1)S(1)}, u32[]{:S(2)}, u32[]{:S(2)}) async-start(bf16[64,2,3200]{2,1,0:T(2,128)(2,1)} %reshape.41), calls=%async_computation.3 | async-start | bytes 1638400 | tf_op jit(solution)/shard_map/down/all_to_all | solution.py:181
  187.7 29.7 %copy-start.13 = (s32[256,4]{0,1:T(4,128)S(1)}, s32[256,4]{0,1:T(4,128)}, u32[]{:S(2)}) copy-start(s32[256,4]{0,1:T(4,128)} %param.10) | copy-start | bytes 12292
  187.7 29.7 %copy-start.14 = (f32[256,4]{0,1:T(4,128)S(1)}, f32[256,4]{0,1:T(4,128)}, u32[]{:S(2)}) copy-start(f32[256,4]{0,1:T(4,128)} %param.11) | copy-start | bytes 12292
  188.9 32.5 %copy-start.9 = (f32[512]{0:T(512)S(1)}, f32[512]{0:T(512)}, u32[]{:S(2)}) copy-start(f32[512]{0:T(512)} %param.15) | copy-start | bytes 6148
  188.9 11.8 %collective-permute-start.9 = (bf16[8,32,512]{2,1,0:T(8,128)(2,1)S(1)}, bf16[8,32,512]{2,1,0:T(8,128)(2,1)S(1)}, u32[]{:S(2)}, u32[]{:S(2)}) collective-permute-start(bf16[8,32,512]{2,1,0:T(8,128)(2,1)S(1)} %bitcast.40), channel_id=1, source_target_pairs={{0,256},{32,288},{64,320},{96,352},{128,384},{160,416},{192,448},{... | collective-permute-start | bytes 786440 | tf_op jit(solution)/shard_map/latent/ppermute | solution.py:185
  200.9 6.9 %collective-permute-start.10 = (bf16[4,32,512]{2,1,0:T(8,128)(2,1)S(1)}, bf16[4,32,512]{2,1,0:T(8,128)(2,1)S(1)}, u32[]{:S(2)}, u32[]{:S(2)}) collective-permute-start(bf16[4,32,512]{2,1,0:T(8,128)(2,1)S(1)} %broadcast_select_fusion.2), channel_id=1, source_target_pairs={{0,128},{32,160},{64,192},{96,224},{128,0},{160,32},{192,64},{224,... | collective-permute-start | bytes 393224 | tf_op jit(solution)/shard_map/latent/ppermute | solution.py:185
  207.8 7.7 %collective-permute-start.11 = (bf16[2,32,512]{2,1,0:T(8,128)(2,1)S(1)}, bf16[2,32,512]{2,1,0:T(8,128)(2,1)S(1)}, u32[]{:S(2)}, u32[]{:S(2)}) collective-permute-start(bf16[2,32,512]{2,1,0:T(8,128)(2,1)S(1)} %broadcast_select_fusion.3), channel_id=1, source_target_pairs={{0,64},{32,96},{64,0},{96,32},{128,192},{160,224},{192,128},{224,1... | collective-permute-start | bytes 196616 | tf_op jit(solution)/shard_map/latent/ppermute | solution.py:185
  215.5 5.8 %collective-permute-start.12 = (bf16[1,32,512]{2,1,0:T(8,128)(2,1)S(1)}, bf16[1,32,512]{2,1,0:T(8,128)(2,1)S(1)}, u32[]{:S(2)}, u32[]{:S(2)}) collective-permute-start(bf16[1,32,512]{2,1,0:T(8,128)(2,1)S(1)} %broadcast_select_fusion.4), channel_id=1, source_target_pairs={{0,32},{32,0},{64,96},{96,64},{128,160},{160,128},{192,224},{224,1... | collective-permute-start | bytes 98312 | tf_op jit(solution)/shard_map/latent/ppermute | solution.py:185

commit v5 on v4

--- a/solution.py
+++ b/solution.py
@@ -51,15 +51,20 @@
     return jnp.concatenate([jnp.where(half == 0, x, 0.0), jnp.where(half == 1, x, 0.0)], axis=1)
 
 
-def dispatch_kernel(lanes, pick_ref, routes_ref, t0, t1, t2, t3, out):
+def hot_kernel(lanes, pick_ref, routes_ref, tokens_ref, out, tokens_out):
+    _, masks = slot_masks(pick_ref, routes_ref[...], lanes, out.shape[1])
+    for i, mask in enumerate(masks):
+        out[i] = by_half(mask.astype(F32)).astype(BF)
+    tokens_out[...] = tokens_ref[...]
+
+
+def dispatch_kernel(hot_ref, t0, t1, t2, t3, out):
     span = 2 * t0.shape[0]
-    _, masks = slot_masks(pick_ref, routes_ref[...], lanes, out.shape[0])
     left = jnp.concatenate([t0[...], t1[...]], axis=0)
     right = jnp.concatenate([t2[...], t3[...]], axis=0)
     both = jnp.concatenate([left, right], axis=1)
-    for i, mask in enumerate(masks):
-        hot = by_half(mask.astype(F32)).astype(BF)
-        rows = lax.dot_general(hot, both, NT, preferred_element_type=F32)
+    for i in range(hot_ref.shape[0]):
+        rows = lax.dot_general(hot_ref[i], both, NT, preferred_element_type=F32)
         out[:, i * span : (i + 1) * span] = rows.astype(BF)
 
 
@@ -84,24 +89,22 @@
 def up_kernel(lanes, rows_ref, w0, w1, w2, w3, out, packed):
     count = rows_ref.shape[0]
     groups = count // 2
-    width, columns = w0.shape
+    width = w0.shape[0]
     span = 2 * width
-    step = 512 if columns % 512 == 0 else columns
-    rows = jnp.dot(halves_first(count), rows_ref[...], preferred_element_type=F32).astype(BF)
-    for i in range(lanes):
-        for p in range(2):
-            piece = rows[p * groups : (p + 1) * groups, i * span : (i + 1) * span]
-            packed[i * groups : (i + 1) * groups, p * span : (p + 1) * span] = piece
-    for c in range(0, columns, step):
-        total = None
-        for k, weight in enumerate((w0, w1, w2, w3)):
-            part = jnp.dot(
-                packed[:, k * width : (k + 1) * width],
-                weight[:, c : c + step],
-                preferred_element_type=F32,
-            )
-            total = part if total is None else total + part
-        out[:, c : c + step] = total.astype(BF)
+
+    @pl.when(pl.program_id(0) == 0)
+    def _():
+        rows = jnp.dot(halves_first(count), rows_ref[...], preferred_element_type=F32).astype(BF)
+        for i in range(lanes):
+            for p in range(2):
+                piece = rows[p * groups : (p + 1) * groups, i * span : (i + 1) * span]
+                packed[i * groups : (i + 1) * groups, p * span : (p + 1) * span] = piece
+
+    total = jnp.zeros(out.shape, F32)
+    for k, weight in enumerate((w0, w1, w2, w3)):
+        rows = packed[:, k * width : (k + 1) * width]
+        total = total + jnp.dot(rows, weight[...], preferred_element_type=F32)
+    out[...] = total.astype(BF)
 
 
 def hidden_kernel(parts_ref, out):
@@ -144,7 +147,7 @@
     place = pick_ref[2]
     for k in range(4):
         at, to = (k % 2) * width, (k // 2) * tokens
-        out[place ^ k] = total[at : at + width, to : to + tokens].astype(BF)
+        out[place ^ (k ^ (k >> 1))] = total[at : at + width, to : to + tokens].astype(BF)
 
 
 def join_kernel(parts_ref, out):
@@ -185,17 +188,10 @@
     return lax.ppermute(x, "dp", [(i, i ^ bits) for i in range(lax.axis_size("dp"))])
 
 
-def cosets(size, *flips):
-    reach = [0]
-    for bits in flips:
-        reach += [i ^ bits for i in reach]
-    return sorted({tuple(sorted(i ^ j for j in reach)) for i in range(size)})
-
-
 def gather_expert(array, resident):
     own = lax.dynamic_index_in_dim(array, resident, 0, keepdims=False)
     cross = lax.dynamic_index_in_dim(array, 1 - resident, 0, keepdims=False)
-    second, third = flip(own, 1), flip(cross, 4)
+    second, third = flip(own, 1), flip(cross, 3)
     return own, second, third, flip(third, 1)
 
 
@@ -218,8 +214,10 @@
 ):
     groups = lax.axis_size(SE)
     blocks = lax.axis_size("dp")
-    near, far = cosets(blocks, 1, 4), cosets(blocks, 3, 12)
-    spread = len(far[0])
+    along_y = 4
+    spread = blocks // along_y
+    near = [[along_y * x + y for y in range(along_y)] for x in range(spread)]
+    far = [[along_y * x + y for x in range(spread)] for y in range(along_y)]
     rows, width = tokens.shape
     tops = routes.shape[1]
     residents = w_gate_up.shape[0]
@@ -238,23 +236,32 @@
     vmem = pl.BlockSpec(memory_space=pltpu.VMEM)
     smem = pl.BlockSpec(memory_space=pltpu.SMEM)
 
-    here = lax.axis_index("dp")
-    resident = ((here >> 2) ^ (here >> 3)) & 1
-    place = ((here >> 1) & 2) + (here & 1)
-    pick = jnp.stack([resident, (here ^ (here >> 1)) & 1, place])
+    at_y = lax.axis_index("dp") & (along_y - 1)
+    resident = at_y >> 1
+    pick = jnp.stack([resident, at_y & 1, at_y])
 
     with jax.named_scope("tokens"):
-        both = flip(tokens_t, 5)
-        pieces = [tokens_t, flip(tokens_t, 1), flip(tokens_t, 4), both]
+        flipped = [flip(tokens_t, bits) for bits in (2, 1, 3)]
+        hot, own_tokens = call(
+            functools.partial(hot_kernel, lanes),
+            [shape((lanes, slots, 2 * rows), BF), shape((width, rows), BF)],
+            pick,
+            routes_t,
+            tokens_t,
+            in_specs=[smem, vmem, vmem],
+            flops=2 * slots * rows * rows,
+            moved=4 * lanes * slots * rows,
+        )
 
     with jax.named_scope("dispatch"):
         outgoing = call(
-            functools.partial(dispatch_kernel, lanes),
+            dispatch_kernel,
             shape((slots, row), BF),
-            pick,
-            routes_t,
-            *pieces,
-            in_specs=[smem] + [vmem] * 5,
+            hot,
+            own_tokens,
+            flipped[1],
+            flipped[2],
+            flipped[0],
             flops=8 * slots * rows * width * lanes,
             moved=2 * slots * row,
         )
@@ -267,15 +274,23 @@
         arrived, down_blocks = lax.optimization_barrier((arrived, down_blocks))
 
     with jax.named_scope("up"):
-        partial = call(
+        columns = 2 * hidden_units
+        step = 512 if columns % 512 == 0 else columns
+        partial = pl.pallas_call(
             functools.partial(up_kernel, lanes),
-            shape((taken, 2 * hidden_units), BF),
-            arrived.reshape(slots, row),
-            *up_blocks,
-            scratch=[pltpu.VMEM((taken, 4 * width), BF)],
-            flops=16 * taken * width * hidden_units,
-            moved=4 * hidden_units * (4 * width + taken),
-        )
+            out_shape=shape((taken, columns), BF),
+            grid=(columns // step,),
+            in_specs=[pl.BlockSpec((slots, row), lambda c: (0, 0))]
+            + [pl.BlockSpec((width, step), lambda c: (0, c))] * 4,
+            out_specs=pl.BlockSpec((taken, step), lambda c: (0, c)),
+            scratch_shapes=[pltpu.VMEM((taken, 4 * width), BF)],
+            cost_estimate=pl.CostEstimate(
+                flops=16 * taken * width * hidden_units,
+                bytes_accessed=4 * hidden_units * (4 * width + taken),
+                transcendentals=0,
+            ),
+            compiler_params=pltpu.CompilerParams(vmem_limit_bytes=24 * 1024 * 1024),
+        )(arrived.reshape(slots, row), *up_blocks)
         shares = exchange(partial.reshape(spread, share, 2 * hidden_units), "dp", far)
 
     with jax.named_scope("hidden"):

time: 291 us -> 288 us (0.990)
  waiting for transfers between devices: 147 us -> 142 us
  starting transfers between devices: 71.5 us -> 76.4 us
  blocking collectives: 47.3 us -> 43.8 us
    pallas_call x0 -> x1, Pallas kernels: none -> 4.39 us  [body(): pl.pallas_call(functools.partial(up_kernel, lanes), out_shape=shape((take...]
    ppermute x13, starting transfers between devices: 34.4 us -> 38.4 us  [flip(): lax.ppermute(x, 'dp', [(i, i ^ bits) for i in range(lax.axis_size('dp'))])]
    ppermute x13, waiting for transfers between devices: 83.6 us -> 79.7 us  [flip(): lax.ppermute(x, 'dp', [(i, i ^ bits) for i in range(lax.axis_size('dp'))])]
    pallas_call x9, Pallas kernels: 13.6 us -> 9.67 us  [call(): pl.pallas_call(kernel, out_shape=out_shape, scratch_shapes=list(scratch),...]
    all_to_all x3, blocking collectives: 47.3 us -> 43.8 us  [exchange(): lax.all_to_all(x, axes, split_axis=0, concat_axis=0, axis_index_groups=gr...]
where the time goes in v5:
time: 288 us; the launch traced here: 287 us
  waiting for transfers between devices  142 us (49%)
  starting transfers between devices  76.4 us (27%)
  blocking collectives  43.8 us (15%)
  Pallas kernels  14.1 us (5%)
  local copies, waits for them, and re-layouts  9.3 us (3%)
    ppermute x13, waiting for transfers between devices, flip(): lax.ppermute(x, 'dp', [(i, i ^ bits) for i in range(lax.axis_size('dp'))])  79.7 us
    all_to_all x2, waiting for transfers between devices, exchange(): lax.all_to_all(x, axes, split_axis=0, concat_axis=0, axis_index_groups=gr...  62.5 us
    all_to_all x3, blocking collectives, exchange(): lax.all_to_all(x, axes, split_axis=0, concat_axis=0, axis_index_groups=gr...  43.8 us
    ppermute x13, starting transfers between devices, flip(): lax.ppermute(x, 'dp', [(i, i ^ bits) for i in range(lax.axis_size('dp'))])  38.4 us
    all_to_all x2, starting transfers between devices, exchange(): lax.all_to_all(x, axes, split_axis=0, concat_axis=0, axis_index_groups=gr...  38 us
    pallas_call x9, Pallas kernels, call(): pl.pallas_call(kernel, out_shape=out_shape, scratch_shapes=list(scratch),...  9.67 us
  transfers between devices with their start and end apart: 15, of which 12 were waited for; matrix products, arithmetic and copies ran while one was open for 1% of the time, Pallas kernels for 1%

profile of v5, /device:TPU:96, one launch (start us, length us, event | category | flops | bytes accessed | tf_op | source)
XLA Modules:
  0.0 287.2 jit_solution(13356719781787446517)
XLA Ops:
  0.6 3.5 %collective-permute-start = (bf16[320,256]{1,0:T(8,128)(2,1)}, bf16[320,256]{1,0:T(8,128)(2,1)S(1)}, u32[]{:S(2)}, u32[]{:S(2)}) collective-permute-start(bf16[320,256]{1,0:T(8,128)(2,1)} %bitcast.30), channel_id=1, source_target_pairs={{0,32},{32,0},{64,96},{96,64},{128,160},{160,128},{192,224},{224,1... | collective-permute-start | bytes 491528 | tf_op jit(solution)/shard_map/tokens/ppermute | solution.py:188
  4.1 4.1 %collective-permute-start.1 = (bf16[320,256]{1,0:T(8,128)(2,1)}, bf16[320,256]{1,0:T(8,128)(2,1)S(1)}, u32[]{:S(2)}, u32[]{:S(2)}) collective-permute-start(bf16[320,256]{1,0:T(8,128)(2,1)} %bitcast.31), channel_id=1, source_target_pairs={{0,96},{32,64},{64,32},{96,0},{128,224},{160,192},{192,160},{224,1... | collective-permute-start | bytes 491528 | tf_op jit(solution)/shard_map/tokens/ppermute | solution.py:188
  8.2 2.6 collective-permute-start.2
  15.2 2.0 collective-permute-done.2.t3
  19.6 28.3 %all-to-all-start = ((bf16[64,2,3200]{2,1,0:T(2,128)(2,1)}), bf16[64,2,3200]{2,1,0:T(2,128)(2,1)}, u32[]{:S(2)}, u32[]{:S(2)}) async-start(bf16[64,2,3200]{2,1,0:T(2,128)(2,1)} %reshape.37), calls=%async_computation | async-start | bytes 1638400 | tf_op jit(solution)/shard_map/dispatch/all_to_all | solution.py:184
  48.0 3.6 %collective-permute-start.7 = (bf16[320,1536]{1,0:T(8,128)(2,1)S(1)}, bf16[320,1536]{1,0:T(8,128)(2,1)S(1)}, u32[]{:S(2)}, u32[]{:S(2)}) collective-permute-start(bf16[320,1536]{1,0:T(8,128)(2,1)S(1)} %get-tuple-element.36), channel_id=1, source_target_pairs={{0,96},{32,64},{64,32},{96,0},{128,224},{160,192},{192,160},{224,1... | collective-permute-start | bytes 2949128 | tf_op jit(solution)/shard_map/gather/ppermute | solution.py:188
  51.7 3.6 %collective-permute-start.4 = (bf16[320,768]{1,0:T(8,128)(2,1)S(1)}, bf16[320,768]{1,0:T(8,128)(2,1)S(1)}, u32[]{:S(2)}, u32[]{:S(2)}) collective-permute-start(bf16[320,768]{1,0:T(8,128)(2,1)S(1)} %get-tuple-element.38), channel_id=1, source_target_pairs={{0,96},{32,64},{64,32},{96,0},{128,224},{160,192},{192,160},{224,1... | collective-permute-start | bytes 1474568 | tf_op jit(solution)/shard_map/gather/ppermute | solution.py:188
  55.3 1.9 collective-permute-start.6
  57.2 18.6 %collective-permute-done.7.w2 = bf16[320,1536]{1,0:T(8,128)(2,1)S(1)} collective-permute-done((bf16[320,1536]{1,0:T(8,128)(2,1)S(1)}, bf16[320,1536]{1,0:T(8,128)(2,1)S(1)}, u32[]{:S(2)}, u32[]{:S(2)}) %collective-permute-start.7) | collective-permute-done | bytes 983072 | tf_op jit(solution)/shard_map/gather/ppermute | solution.py:188
  75.8 1.9 collective-permute-start.8
  77.8 3.9 %collective-permute-start.3 = (bf16[320,768]{1,0:T(8,128)(2,1)S(1)}, bf16[320,768]{1,0:T(8,128)(2,1)S(1)}, u32[]{:S(2)}, u32[]{:S(2)}) collective-permute-start(bf16[320,768]{1,0:T(8,128)(2,1)S(1)} %get-tuple-element.25.w0), channel_id=1, source_target_pairs={{0,32},{32,0},{64,96},{96,64},{128,160},{160,128},{192,224},{224,1... | collective-permute-start | bytes 1474568 | tf_op jit(solution)/shard_map/gather/ppermute | solution.py:188
  81.7 4.0 %collective-permute-done.4.w2 = bf16[320,768]{1,0:T(8,128)(2,1)S(1)} collective-permute-done((bf16[320,768]{1,0:T(8,128)(2,1)S(1)}, bf16[320,768]{1,0:T(8,128)(2,1)S(1)}, u32[]{:S(2)}, u32[]{:S(2)}) %collective-permute-start.4) | collective-permute-done | bytes 491552 | tf_op jit(solution)/shard_map/gather/ppermute | solution.py:188
  85.7 1.9 collective-permute-start.5
  88.4 25.1 %collective-permute-done.3.w1 = bf16[320,768]{1,0:T(8,128)(2,1)S(1)} collective-permute-done((bf16[320,768]{1,0:T(8,128)(2,1)S(1)}, bf16[320,768]{1,0:T(8,128)(2,1)S(1)}, u32[]{:S(2)}, u32[]{:S(2)}) %collective-permute-start.3) | collective-permute-done | bytes 491552 | tf_op jit(solution)/shard_map/gather/ppermute | solution.py:188
  114.2 8.4 %collective-permute-done.5.w3 = bf16[320,768]{1,0:T(8,128)(2,1)S(1)} collective-permute-done((bf16[320,768]{1,0:T(8,128)(2,1)S(1)}, bf16[320,768]{1,0:T(8,128)(2,1)S(1)}, u32[]{:S(2)}, u32[]{:S(2)}) %collective-permute-start.5) | collective-permute-done | bytes 491552 | tf_op jit(solution)/shard_map/gather/ppermute | solution.py:188
  123.5 10.6 %all-to-all-done = bf16[64,2,3200]{2,1,0:T(2,128)(2,1)} async-done(((bf16[64,2,3200]{2,1,0:T(2,128)(2,1)}), bf16[64,2,3200]{2,1,0:T(2,128)(2,1)}, u32[]{:S(2)}, u32[]{:S(2)}) %all-to-all-start) | async-done | bytes 819232 | tf_op jit(solution)/shard_map/dispatch/all_to_all | solution.py:184
  134.1 2.3 reshape.38.rows_ref
  136.4 4.4 %up.1 = bf16[320,1536]{1,0:T(8,128)(2,1)S(1)} custom-call(bf16[128,3200]{1,0:T(8,128)(2,1)S(1)} %reshape.38.rows_ref, bf16[320,1536]{1,0:T(8,128)(2,1)S(1)} %get-tuple-element.37.w0, bf16[320,1536]{1,0:T(8,128)(2,1)} %collective-permute-done.6.w1, bf16[320,1536]{1,0:T(8,128)(2,1)S(1)} %collective-permute-done.7.w2, bf16[320,1536]{1,0:T(8,128)(2,1)} %collective-permute-done.8.w3), custom_call_target="tpu_custom_call" | custom-call | flops 1258291200 | bytes 4915200 | tf_op jit(solution)/shard_map/up/pallas_call | solution.py:279
  140.9 18.9 %all_to_all.25.parts_ref = bf16[4,80,1536]{2,1,0:T(8,128)(2,1)S(1)} all-to-all(bf16[4,80,1536]{2,1,0:T(8,128)(2,1)S(1)} %bitcast.28), channel_id=1, replica_groups={{0,128,256,384},{32,160,288,416},{64,192,320,448},{96,224,352,480},{1,1..., dimensions={0} | all-to-all | bytes 1966080 | tf_op jit(solution)/shard_map/up/all_to_all | solution.py:184
  160.0 11.0 %all_to_all.26 = bf16[4,80,768]{2,1,0:T(8,128)(2,1)S(1)} all-to-all(bf16[4,80,768]{2,1,0:T(8,128)(2,1)S(1)} %hidden.1), channel_id=1, replica_groups={{0,128,256,384},{32,160,288,416},{64,192,320,448},{96,224,352,480},{1,1..., dimensions={0} | all-to-all | bytes 983040 | tf_op jit(solution)/shard_map/hidden/all_to_all | solution.py:184
  173.8 9.7 %all-to-all-start.3 = ((bf16[64,2,3200]{2,1,0:T(2,128)(2,1)}), bf16[64,2,3200]{2,1,0:T(2,128)(2,1)S(1)}, u32[]{:S(2)}, u32[]{:S(2)}) async-start(bf16[64,2,3200]{2,1,0:T(2,128)(2,1)} %reshape.41), calls=%async_computation.3 | async-start | bytes 1638400 | tf_op jit(solution)/shard_map/down/all_to_all | solution.py:184
  184.7 2.8 collective-permute-start.9
  187.6 9.0 %collective-permute-done.9 = bf16[8,32,512]{2,1,0:T(8,128)(2,1)S(1)} collective-permute-done((bf16[8,32,512]{2,1,0:T(8,128)(2,1)S(1)}, bf16[8,32,512]{2,1,0:T(8,128)(2,1)S(1)}, u32[]{:S(2)}, u32[]{:S(2)}) %collective-permute-start.9) | collective-permute-done | bytes 262176 | tf_op jit(solution)/shard_map/latent/ppermute | solution.py:188
  196.7 2.5 collective-permute-start.10
  199.2 4.4 %collective-permute-done.10 = bf16[4,32,512]{2,1,0:T(8,128)(2,1)S(1)} collective-permute-done((bf16[4,32,512]{2,1,0:T(8,128)(2,1)S(1)}, bf16[4,32,512]{2,1,0:T(8,128)(2,1)S(1)}, u32[]{:S(2)}, u32[]{:S(2)}) %collective-permute-start.10) | collective-permute-done | bytes 131104 | tf_op jit(solution)/shard_map/latent/ppermute | solution.py:188
  203.6 3.5 %collective-permute-start.11 = (bf16[2,32,512]{2,1,0:T(8,128)(2,1)S(1)}, bf16[2,32,512]{2,1,0:T(8,128)(2,1)S(1)}, u32[]{:S(2)}, u32[]{:S(2)}) collective-permute-start(bf16[2,32,512]{2,1,0:T(8,128)(2,1)S(1)} %broadcast_select_fusion.3), channel_id=1, source_target_pairs={{0,64},{32,96},{64,0},{96,32},{128,192},{160,224},{192,128},{224,1... | collective-permute-start | bytes 196616 | tf_op jit(solution)/shard_map/latent/ppermute | solution.py:188
  207.2 4.1 %collective-permute-done.11 = bf16[2,32,512]{2,1,0:T(8,128)(2,1)S(1)} collective-permute-done((bf16[2,32,512]{2,1,0:T(8,128)(2,1)S(1)}, bf16[2,32,512]{2,1,0:T(8,128)(2,1)S(1)}, u32[]{:S(2)}, u32[]{:S(2)}) %collective-permute-start.11) | collective-permute-done | bytes 65568 | tf_op jit(solution)/shard_map/latent/ppermute | solution.py:188
  211.3 2.5 collective-permute-start.12
  214.8 2.3 collective-permute-done.12
  217.9 51.9 %all-to-all-done.3 = bf16[64,2,3200]{2,1,0:T(2,128)(2,1)S(1)} async-done(((bf16[64,2,3200]{2,1,0:T(2,128)(2,1)}), bf16[64,2,3200]{2,1,0:T(2,128)(2,1)S(1)}, u32[]{:S(2)}, u32[]{:S(2)}) %all-to-all-start.3) | async-done | bytes 819232 | tf_op jit(solution)/shard_map/down/all_to_all | solution.py:184
  270.1 2.4 mix.2
  272.5 13.9 %all_to_all.27.parts_ref = bf16[4,320,256]{2,1,0:T(8,128)(2,1)S(1)} all-to-all(bf16[4,320,256]{2,1,0:T(8,128)(2,1)S(1)} %mix.2), channel_id=1, replica_groups={{0,32,64,96},{128,160,192,224},{256,288,320,352},{384,416,448,480},{1,3..., dimensions={0} | all-to-all | bytes 1310720 | tf_op jit(solution)/shard_map/mix/all_to_all | solution.py:184
  (60 shorter events, 16.4 us)
Async XLA Ops:
  0.6 12.8 %collective-permute-start = (bf16[320,256]{1,0:T(8,128)(2,1)}, bf16[320,256]{1,0:T(8,128)(2,1)S(1)}, u32[]{:S(2)}, u32[]{:S(2)}) collective-permute-start(bf16[320,256]{1,0:T(8,128)(2,1)} %bitcast.30), channel_id=1, source_target_pairs={{0,32},{32,0},{64,96},{96,64},{128,160},{160,128},{192,224},{224,1... | collective-permute-start | bytes 491528 | tf_op jit(solution)/shard_map/tokens/ppermute | solution.py:188
  4.1 11.1 %collective-permute-start.1 = (bf16[320,256]{1,0:T(8,128)(2,1)}, bf16[320,256]{1,0:T(8,128)(2,1)S(1)}, u32[]{:S(2)}, u32[]{:S(2)}) collective-permute-start(bf16[320,256]{1,0:T(8,128)(2,1)} %bitcast.31), channel_id=1, source_target_pairs={{0,96},{32,64},{64,32},{96,0},{128,224},{160,192},{192,160},{224,1... | collective-permute-start | bytes 491528 | tf_op jit(solution)/shard_map/tokens/ppermute | solution.py:188
  8.2 9.0 %collective-permute-start.2 = (bf16[320,256]{1,0:T(8,128)(2,1)}, bf16[320,256]{1,0:T(8,128)(2,1)S(1)}, u32[]{:S(2)}, u32[]{:S(2)}) collective-permute-start(bf16[320,256]{1,0:T(8,128)(2,1)} %bitcast.32), channel_id=1, source_target_pairs={{0,64},{32,96},{64,0},{96,32},{128,192},{160,224},{192,128},{224,1... | collective-permute-start | bytes 491528 | tf_op jit(solution)/shard_map/tokens/ppermute | solution.py:188
  11.0 0.9 copy-start
  11.9 0.7 copy-start.9
  18.3 29.5 %copy-start.15 = (bf16[2,320,1536]{2,1,0:T(8,128)(2,1)S(1)}, bf16[2,320,1536]{2,1,0:T(8,128)(2,1)}, u32[]{:S(2)}) copy-start(bf16[2,320,1536]{2,1,0:T(8,128)(2,1)} %param.12) | copy-start | bytes 5898244
  19.6 114.5 %all-to-all-start = ((bf16[64,2,3200]{2,1,0:T(2,128)(2,1)}), bf16[64,2,3200]{2,1,0:T(2,128)(2,1)}, u32[]{:S(2)}, u32[]{:S(2)}) async-start(bf16[64,2,3200]{2,1,0:T(2,128)(2,1)} %reshape.37), calls=%async_computation | async-start | bytes 1638400 | tf_op jit(solution)/shard_map/dispatch/all_to_all | solution.py:184
  47.9 3.8 %copy-start.16 = (bf16[2,768,320]{1,2,0:T(8,128)(2,1)S(1)}, bf16[2,768,320]{1,2,0:T(8,128)(2,1)}, u32[]{:S(2)}) copy-start(bf16[2,768,320]{1,2,0:T(8,128)(2,1)} %param.13) | copy-start | bytes 2949124
  48.0 27.8 %collective-permute-start.7 = (bf16[320,1536]{1,0:T(8,128)(2,1)S(1)}, bf16[320,1536]{1,0:T(8,128)(2,1)S(1)}, u32[]{:S(2)}, u32[]{:S(2)}) collective-permute-start(bf16[320,1536]{1,0:T(8,128)(2,1)S(1)} %get-tuple-element.36), channel_id=1, source_target_pairs={{0,96},{32,64},{64,32},{96,0},{128,224},{160,192},{192,160},{224,1... | collective-permute-start | bytes 2949128 | tf_op jit(solution)/shard_map/gather/ppermute | solution.py:188
  51.7 33.9 %collective-permute-start.4 = (bf16[320,768]{1,0:T(8,128)(2,1)S(1)}, bf16[320,768]{1,0:T(8,128)(2,1)S(1)}, u32[]{:S(2)}, u32[]{:S(2)}) collective-permute-start(bf16[320,768]{1,0:T(8,128)(2,1)S(1)} %get-tuple-element.38), channel_id=1, source_target_pairs={{0,96},{32,64},{64,32},{96,0},{128,224},{160,192},{192,160},{224,1... | collective-permute-start | bytes 1474568 | tf_op jit(solution)/shard_map/gather/ppermute | solution.py:188
  55.3 81.1 %collective-permute-start.6 = (bf16[320,1536]{1,0:T(8,128)(2,1)S(1)}, bf16[320,1536]{1,0:T(8,128)(2,1)}, u32[]{:S(2)}, u32[]{:S(2)}) collective-permute-start(bf16[320,1536]{1,0:T(8,128)(2,1)S(1)} %get-tuple-element.37.w0), channel_id=1, source_target_pairs={{0,32},{32,0},{64,96},{96,64},{128,160},{160,128},{192,224},{224,1... | collective-permute-start | bytes 2949128 | tf_op jit(solution)/shard_map/gather/ppermute | solution.py:188
  75.8 60.6 %collective-permute-start.8 = (bf16[320,1536]{1,0:T(8,128)(2,1)S(1)}, bf16[320,1536]{1,0:T(8,128)(2,1)}, u32[]{:S(2)}, u32[]{:S(2)}) collective-permute-start(bf16[320,1536]{1,0:T(8,128)(2,1)S(1)} %collective-permute-done.7.w2), channel_id=1, source_target_pairs={{0,32},{32,0},{64,96},{96,64},{128,160},{160,128},{192,224},{224,1... | collective-permute-start | bytes 2949128 | tf_op jit(solution)/shard_map/gather/ppermute | solution.py:188
  77.8 35.7 %collective-permute-start.3 = (bf16[320,768]{1,0:T(8,128)(2,1)S(1)}, bf16[320,768]{1,0:T(8,128)(2,1)S(1)}, u32[]{:S(2)}, u32[]{:S(2)}) collective-permute-start(bf16[320,768]{1,0:T(8,128)(2,1)S(1)} %get-tuple-element.25.w0), channel_id=1, source_target_pairs={{0,32},{32,0},{64,96},{96,64},{128,160},{160,128},{192,224},{224,1... | collective-permute-start | bytes 1474568 | tf_op jit(solution)/shard_map/gather/ppermute | solution.py:188
  85.7 37.0 %collective-permute-start.5 = (bf16[320,768]{1,0:T(8,128)(2,1)S(1)}, bf16[320,768]{1,0:T(8,128)(2,1)S(1)}, u32[]{:S(2)}, u32[]{:S(2)}) collective-permute-start(bf16[320,768]{1,0:T(8,128)(2,1)S(1)} %collective-permute-done.4.w2), channel_id=1, source_target_pairs={{0,32},{32,0},{64,96},{96,64},{128,160},{160,128},{192,224},{224,1... | collective-permute-start | bytes 1474568 | tf_op jit(solution)/shard_map/gather/ppermute | solution.py:188
  87.6 0.8 copy-start.2
  113.5 0.8 copy-start.4
  122.7 0.8 copy-start.6
  140.8 30.1 %copy-start.3 = (bf16[320,768]{1,0:T(8,128)(2,1)S(1)}, bf16[320,768]{1,0:T(8,128)(2,1)}, u32[]{:S(2)}) copy-start(bf16[320,768]{1,0:T(8,128)(2,1)} %copy-done.2) | copy-start | bytes 1474564
  140.8 30.1 %copy-start.5 = (bf16[320,768]{1,0:T(8,128)(2,1)S(1)}, bf16[320,768]{1,0:T(8,128)(2,1)}, u32[]{:S(2)}) copy-start(bf16[320,768]{1,0:T(8,128)(2,1)} %copy-done.4) | copy-start | bytes 1474564
  140.8 30.1 %copy-start.7 = (bf16[320,768]{1,0:T(8,128)(2,1)S(1)}, bf16[320,768]{1,0:T(8,128)(2,1)}, u32[]{:S(2)}) copy-start(bf16[320,768]{1,0:T(8,128)(2,1)} %copy-done.6) | copy-start | bytes 1474564
  172.5 11.0 %copy-start.1 = (bf16[256,320]{0,1:T(8,128)(2,1)S(1)}, bf16[256,320]{0,1:T(8,128)(2,1)}, u32[]{:S(2)}) copy-start(bf16[256,320]{0,1:T(8,128)(2,1)} %param.9) | copy-start | bytes 491524
  172.5 11.0 %copy-start.8 = (bf16[320,512]{1,0:T(8,128)(2,1)S(1)}, bf16[320,512]{1,0:T(8,128)(2,1)}, u32[]{:S(2)}) copy-start(bf16[320,512]{1,0:T(8,128)(2,1)} %weight_ref.1) | copy-start | bytes 983044
  172.5 11.0 %copy-start.12 = (s32[1,16]{1,0:T(1,128)S(1)}, s32[1,16]{1,0:T(1,128)}, u32[]{:S(2)}) copy-start(s32[1,16]{1,0:T(1,128)} %lengths_ref.1) | copy-start | bytes 196
  172.5 11.0 %copy-start.13 = (s32[1,16]{1,0:T(1,128)S(1)}, s32[1,16]{1,0:T(1,128)}, u32[]{:S(2)}) copy-start(s32[1,16]{1,0:T(1,128)} %placement_ref.1) | copy-start | bytes 196
  173.8 96.0 %all-to-all-start.3 = ((bf16[64,2,3200]{2,1,0:T(2,128)(2,1)}), bf16[64,2,3200]{2,1,0:T(2,128)(2,1)S(1)}, u32[]{:S(2)}, u32[]{:S(2)}) async-start(bf16[64,2,3200]{2,1,0:T(2,128)(2,1)} %reshape.41), calls=%async_computation.3 | async-start | bytes 1638400 | tf_op jit(solution)/shard_map/down/all_to_all | solution.py:184
  183.5 30.3 %copy-start.10 = (s32[256,4]{0,1:T(4,128)S(1)}, s32[256,4]{0,1:T(4,128)}, u32[]{:S(2)}) copy-start(s32[256,4]{0,1:T(4,128)} %param.10) | copy-start | bytes 12292
  183.5 30.3 %copy-start.14 = (f32[256,4]{0,1:T(4,128)S(1)}, f32[256,4]{0,1:T(4,128)}, u32[]{:S(2)}) copy-start(f32[256,4]{0,1:T(4,128)} %param.11) | copy-start | bytes 12292
  184.7 32.5 %copy-start.11 = (f32[512]{0:T(512)S(1)}, f32[512]{0:T(512)}, u32[]{:S(2)}) copy-start(f32[512]{0:T(512)} %param.15) | copy-start | bytes 6148
  184.7 11.9 %collective-permute-start.9 = (bf16[8,32,512]{2,1,0:T(8,128)(2,1)S(1)}, bf16[8,32,512]{2,1,0:T(8,128)(2,1)S(1)}, u32[]{:S(2)}, u32[]{:S(2)}) collective-permute-start(bf16[8,32,512]{2,1,0:T(8,128)(2,1)S(1)} %bitcast.40), channel_id=1, source_target_pairs={{0,256},{32,288},{64,320},{96,352},{128,384},{160,416},{192,448},{... | collective-permute-start | bytes 786440 | tf_op jit(solution)/shard_map/latent/ppermute | solution.py:188
  196.7 6.9 %collective-permute-start.10 = (bf16[4,32,512]{2,1,0:T(8,128)(2,1)S(1)}, bf16[4,32,512]{2,1,0:T(8,128)(2,1)S(1)}, u32[]{:S(2)}, u32[]{:S(2)}) collective-permute-start(bf16[4,32,512]{2,1,0:T(8,128)(2,1)S(1)} %broadcast_select_fusion.2), channel_id=1, source_target_pairs={{0,128},{32,160},{64,192},{96,224},{128,0},{160,32},{192,64},{224,... | collective-permute-start | bytes 393224 | tf_op jit(solution)/shard_map/latent/ppermute | solution.py:188
  203.6 7.7 %collective-permute-start.11 = (bf16[2,32,512]{2,1,0:T(8,128)(2,1)S(1)}, bf16[2,32,512]{2,1,0:T(8,128)(2,1)S(1)}, u32[]{:S(2)}, u32[]{:S(2)}) collective-permute-start(bf16[2,32,512]{2,1,0:T(8,128)(2,1)S(1)} %broadcast_select_fusion.3), channel_id=1, source_target_pairs={{0,64},{32,96},{64,0},{96,32},{128,192},{160,224},{192,128},{224,1... | collective-permute-start | bytes 196616 | tf_op jit(solution)/shard_map/latent/ppermute | solution.py:188
  211.3 5.8 %collective-permute-start.12 = (bf16[1,32,512]{2,1,0:T(8,128)(2,1)S(1)}, bf16[1,32,512]{2,1,0:T(8,128)(2,1)S(1)}, u32[]{:S(2)}, u32[]{:S(2)}) collective-permute-start(bf16[1,32,512]{2,1,0:T(8,128)(2,1)S(1)} %broadcast_select_fusion.4), channel_id=1, source_target_pairs={{0,32},{32,0},{64,96},{96,64},{128,160},{160,128},{192,224},{224,1... | collective-permute-start | bytes 98312 | tf_op jit(solution)/shard_map/latent/ppermute | solution.py:188

commit v6 on v5

--- a/solution.py
+++ b/solution.py
@@ -33,11 +33,11 @@
     return lax.broadcasted_iota(jnp.int32, shape, dim)
 
 
-def slot_masks(pick_ref, routes_t, lanes, slot_count):
+def slot_masks(pick_ref, routes_t, lanes, groups):
     tops, rows = routes_t.shape
     resident, part = pick_ref[0], pick_ref[1]
-    ids = (iota((slot_count, rows), 0) >> 1) * 2 + resident
-    named = jnp.zeros((slot_count, rows), F32)
+    ids = iota((groups, rows), 0) * 2 + resident
+    named = jnp.zeros((groups, rows), F32)
     for k in range(tops):
         named = named + jnp.where(routes_t[k : k + 1, :] == ids, 1.0, 0.0)
     earlier = (iota((rows, rows), 0) < iota((rows, rows), 1)).astype(F32).astype(BF)
@@ -46,65 +46,51 @@
     return ids, [(named > 0.5) & (rank == base + float(i)) for i in range(lanes)]
 
 
-def by_half(x):
-    half = iota(x.shape, 0) & 1
-    return jnp.concatenate([jnp.where(half == 0, x, 0.0), jnp.where(half == 1, x, 0.0)], axis=1)
-
-
 def hot_kernel(lanes, pick_ref, routes_ref, tokens_ref, out, tokens_out):
-    _, masks = slot_masks(pick_ref, routes_ref[...], lanes, out.shape[1])
+    groups = out.shape[0] // lanes
+    _, masks = slot_masks(pick_ref, routes_ref[...], lanes, groups)
     for i, mask in enumerate(masks):
-        out[i] = by_half(mask.astype(F32)).astype(BF)
+        out[i * groups : (i + 1) * groups, :] = mask.astype(F32).astype(BF)
     tokens_out[...] = tokens_ref[...]
 
 
 def dispatch_kernel(hot_ref, t0, t1, t2, t3, out):
+    _, groups, row = out.shape
     span = 2 * t0.shape[0]
-    left = jnp.concatenate([t0[...], t1[...]], axis=0)
-    right = jnp.concatenate([t2[...], t3[...]], axis=0)
-    both = jnp.concatenate([left, right], axis=1)
-    for i in range(hot_ref.shape[0]):
-        rows = lax.dot_general(hot_ref[i], both, NT, preferred_element_type=F32)
-        out[:, i * span : (i + 1) * span] = rows.astype(BF)
-
-
-def weights_kernel(lanes, pick_ref, routes_ref, weights_ref, high_ref, low_ref):
+    for p, (left, right) in enumerate(((t0, t1), (t2, t3))):
+        both = jnp.concatenate([left[...], right[...]], axis=0)
+        rows = lax.dot_general(hot_ref[...], both, NT, preferred_element_type=F32).astype(BF)
+        for i in range(row // span):
+            out[p, :, i * span : (i + 1) * span] = rows[i * groups : (i + 1) * groups, :]
+
+
+def weights_kernel(lanes, pick_ref, routes_ref, weights_ref, out):
     routes_t, weights_t = routes_ref[...], weights_ref[...]
-    ids, masks = slot_masks(pick_ref, routes_t, lanes, high_ref.shape[1])
+    groups, rows = out.shape[0] // lanes, routes_t.shape[1]
+    ids, masks = slot_masks(pick_ref, routes_t, lanes, groups)
     gates = jnp.zeros(ids.shape, F32)
     for k in range(routes_t.shape[0]):
         gates = gates + jnp.where(routes_t[k : k + 1, :] == ids, weights_t[k : k + 1, :], 0.0)
     high = gates.astype(BF).astype(F32)
     low = gates - high
     for i, mask in enumerate(masks):
-        high_ref[i] = by_half(jnp.where(mask, high, 0.0)).astype(BF)
-        low_ref[i] = by_half(jnp.where(mask, low, 0.0)).astype(BF)
-
-
-def halves_first(count):
-    a = iota((count, count), 1)
-    return (iota((count, count), 0) == (a & 1) * (count // 2) + (a >> 1)).astype(F32).astype(BF)
-
-
-def up_kernel(lanes, rows_ref, w0, w1, w2, w3, out, packed):
-    count = rows_ref.shape[0]
-    groups = count // 2
-    width = w0.shape[0]
-    span = 2 * width
+        out[i * groups : (i + 1) * groups, :rows] = jnp.where(mask, high, 0.0).astype(BF)
+        out[i * groups : (i + 1) * groups, rows:] = jnp.where(mask, low, 0.0).astype(BF)
+
+
+def up_kernel(rows_ref, w0, w1, w2, w3, out, packed):
+    halves, groups, row = rows_ref.shape
+    span = packed.shape[1] // halves
 
     @pl.when(pl.program_id(0) == 0)
     def _():
-        rows = jnp.dot(halves_first(count), rows_ref[...], preferred_element_type=F32).astype(BF)
-        for i in range(lanes):
-            for p in range(2):
-                piece = rows[p * groups : (p + 1) * groups, i * span : (i + 1) * span]
+        for i in range(row // span):
+            for p in range(halves):
+                piece = rows_ref[p, :, i * span : (i + 1) * span]
                 packed[i * groups : (i + 1) * groups, p * span : (p + 1) * span] = piece
 
-    total = jnp.zeros(out.shape, F32)
-    for k, weight in enumerate((w0, w1, w2, w3)):
-        rows = packed[:, k * width : (k + 1) * width]
-        total = total + jnp.dot(rows, weight[...], preferred_element_type=F32)
-    out[...] = total.astype(BF)
+    weight = jnp.concatenate([w0[...], w1[...], w2[...], w3[...]], axis=0)
+    out[...] = jnp.dot(packed[...], weight, preferred_element_type=F32).astype(BF)
 
 
 def hidden_kernel(parts_ref, out):
@@ -119,35 +105,30 @@
         out[b] = hidden
 
 
-def down_kernel(lanes, hidden_ref, w0, w1, w2, w3, out, packed):
-    count = out.shape[0]
-    groups = count // 2
-    width = w0.shape[0]
-    span = 2 * width
-    for k, weight in enumerate((w0, w1, w2, w3)):
-        part = lax.dot_general(hidden_ref[...], weight[...], NT, preferred_element_type=F32)
-        part = part.astype(BF)
-        p, skip = k // 2, (k % 2) * width
-        for i in range(lanes):
-            at = i * span + skip
-            piece = part[i * groups : (i + 1) * groups, :]
-            packed[p * groups : (p + 1) * groups, at : at + width] = piece
-    rows = lax.dot_general(halves_first(count), packed[...], TN, preferred_element_type=F32)
-    out[...] = rows.astype(BF)
-
-
-def mix_kernel(lanes, pick_ref, back_ref, high_ref, low_ref, out):
+def down_kernel(hidden_ref, w0, w1, w2, w3, out):
+    _, groups, row = out.shape
+    span = 2 * w0.shape[0]
+    for p, (left, right) in enumerate(((w0, w1), (w2, w3))):
+        weight = jnp.concatenate([left[...], right[...]], axis=0)
+        part = lax.dot_general(hidden_ref[...], weight, NT, preferred_element_type=F32).astype(BF)
+        for i in range(row // span):
+            out[p, :, i * span : (i + 1) * span] = part[i * groups : (i + 1) * groups, :]
+
+
+def mix_kernel(pick_ref, back_ref, gates_ref, out):
     _, width, tokens = out.shape
     span = 2 * width
-    total = jnp.zeros((span, 2 * tokens), F32)
-    for i in range(lanes):
-        rows = back_ref[:, i * span : (i + 1) * span]
-        total = total + lax.dot_general(rows, high_ref[i], TN, preferred_element_type=F32)
-        total = total + lax.dot_general(rows, low_ref[i], TN, preferred_element_type=F32)
     place = pick_ref[2]
-    for k in range(4):
-        at, to = (k % 2) * width, (k // 2) * tokens
-        out[place ^ (k ^ (k >> 1))] = total[at : at + width, to : to + tokens].astype(BF)
+    for p in range(back_ref.shape[0]):
+        pieces = [
+            back_ref[p, :, at : at + span] for at in range(0, back_ref.shape[2], span)
+        ]
+        rows = jnp.concatenate(pieces, axis=0)
+        total = lax.dot_general(rows, gates_ref[...], TN, preferred_element_type=F32)
+        total = (total[:, :tokens] + total[:, tokens:]).astype(BF)
+        for half in range(2):
+            k = 2 * p + half
+            out[place ^ (k ^ (k >> 1))] = total[half * width : (half + 1) * width, :]
 
 
 def join_kernel(parts_ref, out):
@@ -244,7 +225,7 @@
         flipped = [flip(tokens_t, bits) for bits in (2, 1, 3)]
         hot, own_tokens = call(
             functools.partial(hot_kernel, lanes),
-            [shape((lanes, slots, 2 * rows), BF), shape((width, rows), BF)],
+            [shape((taken, rows), BF), shape((width, rows), BF)],
             pick,
             routes_t,
             tokens_t,
@@ -256,7 +237,7 @@
     with jax.named_scope("dispatch"):
         outgoing = call(
             dispatch_kernel,
-            shape((slots, row), BF),
+            shape((2, groups, row), BF),
             hot,
             own_tokens,
             flipped[1],
@@ -266,7 +247,7 @@
             moved=2 * slots * row,
         )
         outgoing, w_gate_up, w_down = lax.optimization_barrier((outgoing, w_gate_up, w_down))
-        arrived = exchange(outgoing.reshape(groups, 2, row), SE)
+        arrived = exchange(outgoing.transpose(1, 0, 2), SE).transpose(1, 0, 2)
 
     with jax.named_scope("gather"):
         up_blocks = gather_expert(w_gate_up, resident)
@@ -277,10 +258,10 @@
         columns = 2 * hidden_units
         step = 512 if columns % 512 == 0 else columns
         partial = pl.pallas_call(
-            functools.partial(up_kernel, lanes),
+            up_kernel,
             out_shape=shape((taken, columns), BF),
             grid=(columns // step,),
-            in_specs=[pl.BlockSpec((slots, row), lambda c: (0, 0))]
+            in_specs=[pl.BlockSpec((2, groups, row), lambda c: (0, 0, 0))]
             + [pl.BlockSpec((width, step), lambda c: (0, c))] * 4,
             out_specs=pl.BlockSpec((taken, step), lambda c: (0, c)),
             scratch_shapes=[pltpu.VMEM((taken, 4 * width), BF)],
@@ -290,7 +271,7 @@
                 transcendentals=0,
             ),
             compiler_params=pltpu.CompilerParams(vmem_limit_bytes=24 * 1024 * 1024),
-        )(arrived.reshape(slots, row), *up_blocks)
+        )(arrived, *up_blocks)
         shares = exchange(partial.reshape(spread, share, 2 * hidden_units), "dp", far)
 
     with jax.named_scope("hidden"):
@@ -305,21 +286,20 @@
 
     with jax.named_scope("down"):
         produced = call(
-            functools.partial(down_kernel, lanes),
-            shape((slots, row), BF),
+            down_kernel,
+            shape((2, groups, row), BF),
             gathered.reshape(taken, hidden_units),
             *down_blocks,
-            scratch=[pltpu.VMEM((slots, row), BF)],
             flops=8 * taken * width * hidden_units,
             moved=2 * hidden_units * (4 * width + taken),
         )
         produced, tokens_t, gates_t = lax.optimization_barrier((produced, tokens_t, gates_t))
-        back = exchange(produced.reshape(groups, 2, row), SE).reshape(slots, row)
+        back = exchange(produced.transpose(1, 0, 2), SE).transpose(1, 0, 2)
 
     with jax.named_scope("gates"):
         gates = call(
             functools.partial(weights_kernel, lanes),
-            [shape((lanes, slots, 2 * rows), BF)] * 2,
+            shape((taken, 2 * rows), BF),
             pick,
             routes_t,
             gates_t,
@@ -357,12 +337,12 @@
 
     with jax.named_scope("mix"):
         parts = call(
-            functools.partial(mix_kernel, lanes),
+            mix_kernel,
             shape((4, width, rows), BF),
             pick,
             back,
-            *gates,
-            in_specs=[smem] + [vmem] * 3,
+            gates,
+            in_specs=[smem] + [vmem] * 2,
             flops=32 * taken * width * rows,
             moved=2 * slots * row + 8 * lanes * slots * rows,
         )

time: 288 us -> 284 us (0.986)
  waiting for transfers between devices: 142 us -> 145 us
    all_to_all x2, waiting for transfers between devices: 62.5 us -> 98.3 us  [exchange(): lax.all_to_all(x, axes, split_axis=0, concat_axis=0, axis_index_groups=gr...]
    ppermute x13, waiting for transfers between devices: 79.7 us -> 47.1 us  [flip(): lax.ppermute(x, 'dp', [(i, i ^ bits) for i in range(lax.axis_size('dp'))])]
    reshape x4 -> x0, local copies, waits for them, and re-layouts: 5.05 us -> none  [the longest x1 2.32 us: body(): arrived.reshape(slots, row)]
    transpose x0 -> x2, local copies, waits for them, and re-layouts: none -> 3.51 us  [the longest x1 1.76 us: body(): back = exchange(produced.transpose(1, 0, 2), SE).transpose(1, 0, 2)]
  transfers between devices with their start and end apart: 15 -> 15, of which waited for: 12 -> 10; matrix products, arithmetic and copies ran while one was open for 1% -> 1% of each run, Pallas kernels for 1% -> 1%
where the time goes in v6:
time: 284 us; the launch traced here: 283 us
  waiting for transfers between devices  145 us (51%)
  starting transfers between devices  74.6 us (26%)
  blocking collectives  43.7 us (15%)
  Pallas kernels  11.8 us (4%)
  local copies, waits for them, and re-layouts  6.69 us (2%)
    all_to_all x2, waiting for transfers between devices, exchange(): lax.all_to_all(x, axes, split_axis=0, concat_axis=0, axis_index_groups=gr...  98.3 us
    ppermute x13, waiting for transfers between devices, flip(): lax.ppermute(x, 'dp', [(i, i ^ bits) for i in range(lax.axis_size('dp'))])  47.1 us
    all_to_all x3, blocking collectives, exchange(): lax.all_to_all(x, axes, split_axis=0, concat_axis=0, axis_index_groups=gr...  43.7 us
    ppermute x13, starting transfers between devices, flip(): lax.ppermute(x, 'dp', [(i, i ^ bits) for i in range(lax.axis_size('dp'))])  38 us
    all_to_all x2, starting transfers between devices, exchange(): lax.all_to_all(x, axes, split_axis=0, concat_axis=0, axis_index_groups=gr...  36.6 us
    pallas_call x9, Pallas kernels, call(): pl.pallas_call(kernel, out_shape=out_shape, scratch_shapes=list(scratch),...  8.43 us
  transfers between devices with their start and end apart: 15, of which 10 were waited for; matrix products, arithmetic and copies ran while one was open for 1% of the time, Pallas kernels for 1%

profile of v6, /device:TPU:96, one launch (start us, length us, event | category | flops | bytes accessed | tf_op | source)
XLA Modules:
  0.0 283.5 jit_solution(15350193118411136418)
XLA Ops:
  0.6 3.5 %collective-permute-start = (bf16[320,256]{1,0:T(8,128)(2,1)}, bf16[320,256]{1,0:T(8,128)(2,1)S(1)}, u32[]{:S(2)}, u32[]{:S(2)}) collective-permute-start(bf16[320,256]{1,0:T(8,128)(2,1)} %bitcast.42), channel_id=1, source_target_pairs={{0,32},{32,0},{64,96},{96,64},{128,160},{160,128},{192,224},{224,1... | collective-permute-start | bytes 491528 | tf_op jit(solution)/shard_map/tokens/ppermute | solution.py:169
  4.1 4.1 %collective-permute-start.1 = (bf16[320,256]{1,0:T(8,128)(2,1)}, bf16[320,256]{1,0:T(8,128)(2,1)S(1)}, u32[]{:S(2)}, u32[]{:S(2)}) collective-permute-start(bf16[320,256]{1,0:T(8,128)(2,1)} %bitcast.43), channel_id=1, source_target_pairs={{0,96},{32,64},{64,32},{96,0},{128,224},{160,192},{192,160},{224,1... | collective-permute-start | bytes 491528 | tf_op jit(solution)/shard_map/tokens/ppermute | solution.py:169
  8.2 2.6 collective-permute-start.2
  13.3 1.9 collective-permute-done.1.t2
  15.2 2.0 collective-permute-done.2.t3
  17.7 1.7 copy.11
  19.4 28.3 %all-to-all-start = ((bf16[64,2,3200]{2,1,0:T(2,128)(2,1)}), bf16[64,2,3200]{2,1,0:T(2,128)(2,1)}, u32[]{:S(2)}, u32[]{:S(2)}) async-start(bf16[64,2,3200]{2,1,0:T(2,128)(2,1)} %copy.11), calls=%async_computation | async-start | bytes 1638400 | tf_op jit(solution)/shard_map/dispatch/all_to_all | solution.py:165
  47.9 3.6 %collective-permute-start.7 = (bf16[320,1536]{1,0:T(8,128)(2,1)S(1)}, bf16[320,1536]{1,0:T(8,128)(2,1)S(1)}, u32[]{:S(2)}, u32[]{:S(2)}) collective-permute-start(bf16[320,1536]{1,0:T(8,128)(2,1)S(1)} %get-tuple-element.32), channel_id=1, source_target_pairs={{0,96},{32,64},{64,32},{96,0},{128,224},{160,192},{192,160},{224,1... | collective-permute-start | bytes 2949128 | tf_op jit(solution)/shard_map/gather/ppermute | solution.py:169
  51.6 3.6 %collective-permute-start.4 = (bf16[320,768]{1,0:T(8,128)(2,1)S(1)}, bf16[320,768]{1,0:T(8,128)(2,1)}, u32[]{:S(2)}, u32[]{:S(2)}) collective-permute-start(bf16[320,768]{1,0:T(8,128)(2,1)S(1)} %get-tuple-element.34), channel_id=1, source_target_pairs={{0,96},{32,64},{64,32},{96,0},{128,224},{160,192},{192,160},{224,1... | collective-permute-start | bytes 1474568 | tf_op jit(solution)/shard_map/gather/ppermute | solution.py:169
  55.2 1.9 collective-permute-start.6
  57.1 18.6 %collective-permute-done.7.w2 = bf16[320,1536]{1,0:T(8,128)(2,1)S(1)} collective-permute-done((bf16[320,1536]{1,0:T(8,128)(2,1)S(1)}, bf16[320,1536]{1,0:T(8,128)(2,1)S(1)}, u32[]{:S(2)}, u32[]{:S(2)}) %collective-permute-start.7) | collective-permute-done | bytes 983072 | tf_op jit(solution)/shard_map/gather/ppermute | solution.py:169
  75.7 1.9 collective-permute-start.8
  77.6 3.9 %collective-permute-start.3 = (bf16[320,768]{1,0:T(8,128)(2,1)S(1)}, bf16[320,768]{1,0:T(8,128)(2,1)}, u32[]{:S(2)}, u32[]{:S(2)}) collective-permute-start(bf16[320,768]{1,0:T(8,128)(2,1)S(1)} %get-tuple-element.23.w0), channel_id=1, source_target_pairs={{0,32},{32,0},{64,96},{96,64},{128,160},{160,128},{192,224},{224,1... | collective-permute-start | bytes 1474568 | tf_op jit(solution)/shard_map/gather/ppermute | solution.py:169
  81.5 4.1 %collective-permute-done.4.w2 = bf16[320,768]{1,0:T(8,128)(2,1)} collective-permute-done((bf16[320,768]{1,0:T(8,128)(2,1)S(1)}, bf16[320,768]{1,0:T(8,128)(2,1)}, u32[]{:S(2)}, u32[]{:S(2)}) %collective-permute-start.4) | collective-permute-done | bytes 491552 | tf_op jit(solution)/shard_map/gather/ppermute | solution.py:169
  85.6 1.9 collective-permute-start.5
  87.6 46.4 %all-to-all-done = bf16[64,2,3200]{2,1,0:T(2,128)(2,1)} async-done(((bf16[64,2,3200]{2,1,0:T(2,128)(2,1)}), bf16[64,2,3200]{2,1,0:T(2,128)(2,1)}, u32[]{:S(2)}, u32[]{:S(2)}) %all-to-all-start) | async-done | bytes 819232 | tf_op jit(solution)/shard_map/dispatch/all_to_all | solution.py:165
  135.2 3.4 %up.1 = bf16[320,1536]{1,0:T(8,128)(2,1)S(1)} custom-call(bf16[2,64,3200]{2,1,0:T(8,128)(2,1)S(1)} %bitcast.39, bf16[320,1536]{1,0:T(8,128)(2,1)S(1)} %get-tuple-element.33.w0, bf16[320,1536]{1,0:T(8,128)(2,1)S(1)} %collective-permute-done.6.w1, bf16[320,1536]{1,0:T(8,128)(2,1)S(1)} %collective-permute-done.7.w2, bf16[320,1536]{1,0:T(8,128)(2,1)} %collective-permute-done.8.w3), custom_call_target="tpu_custom_call" | custom-call | flops 1258291200 | bytes 4915200 | tf_op jit(solution)/shard_map/up/pallas_call | solution.py:260
  138.6 18.8 %all_to_all.25.parts_ref = bf16[4,80,1536]{2,1,0:T(8,128)(2,1)S(1)} all-to-all(bf16[4,80,1536]{2,1,0:T(8,128)(2,1)S(1)} %bitcast.36), channel_id=1, replica_groups={{0,128,256,384},{32,160,288,416},{64,192,320,448},{96,224,352,480},{1,1..., dimensions={0} | all-to-all | bytes 1966080 | tf_op jit(solution)/shard_map/up/all_to_all | solution.py:165
  157.6 11.0 %all_to_all.26 = bf16[4,80,768]{2,1,0:T(8,128)(2,1)S(1)} all-to-all(bf16[4,80,768]{2,1,0:T(8,128)(2,1)S(1)} %hidden.1), channel_id=1, replica_groups={{0,128,256,384},{32,160,288,416},{64,192,320,448},{96,224,352,480},{1,1..., dimensions={0} | all-to-all | bytes 983040 | tf_op jit(solution)/shard_map/hidden/all_to_all | solution.py:165
  168.5 2.3 down.1
  170.9 1.8 copy.13
  172.6 8.4 %all-to-all-start.3 = ((bf16[64,2,3200]{2,1,0:T(2,128)(2,1)}), bf16[64,2,3200]{2,1,0:T(2,128)(2,1)S(1)}, u32[]{:S(2)}, u32[]{:S(2)}) async-start(bf16[64,2,3200]{2,1,0:T(2,128)(2,1)} %copy.13), calls=%async_computation.3 | async-start | bytes 1638400 | tf_op jit(solution)/shard_map/down/all_to_all | solution.py:165
  182.3 2.8 collective-permute-start.9
  185.1 9.0 %collective-permute-done.9 = bf16[8,32,512]{2,1,0:T(8,128)(2,1)S(1)} collective-permute-done((bf16[8,32,512]{2,1,0:T(8,128)(2,1)S(1)}, bf16[8,32,512]{2,1,0:T(8,128)(2,1)S(1)}, u32[]{:S(2)}, u32[]{:S(2)}) %collective-permute-start.9) | collective-permute-done | bytes 262176 | tf_op jit(solution)/shard_map/latent/ppermute | solution.py:169
  194.2 2.5 collective-permute-start.10
  196.7 4.4 %collective-permute-done.10 = bf16[4,32,512]{2,1,0:T(8,128)(2,1)S(1)} collective-permute-done((bf16[4,32,512]{2,1,0:T(8,128)(2,1)S(1)}, bf16[4,32,512]{2,1,0:T(8,128)(2,1)S(1)}, u32[]{:S(2)}, u32[]{:S(2)}) %collective-permute-start.10) | collective-permute-done | bytes 131104 | tf_op jit(solution)/shard_map/latent/ppermute | solution.py:169
  201.2 3.0 %collective-permute-start.11 = (bf16[2,32,512]{2,1,0:T(8,128)(2,1)S(1)}, bf16[2,32,512]{2,1,0:T(8,128)(2,1)S(1)}, u32[]{:S(2)}, u32[]{:S(2)}) collective-permute-start(bf16[2,32,512]{2,1,0:T(8,128)(2,1)S(1)} %broadcast_select_fusion.3), channel_id=1, source_target_pairs={{0,64},{32,96},{64,0},{96,32},{128,192},{160,224},{192,128},{224,1... | collective-permute-start | bytes 196616 | tf_op jit(solution)/shard_map/latent/ppermute | solution.py:169
  204.2 4.7 %collective-permute-done.11 = bf16[2,32,512]{2,1,0:T(8,128)(2,1)S(1)} collective-permute-done((bf16[2,32,512]{2,1,0:T(8,128)(2,1)S(1)}, bf16[2,32,512]{2,1,0:T(8,128)(2,1)S(1)}, u32[]{:S(2)}, u32[]{:S(2)}) %collective-permute-start.11) | collective-permute-done | bytes 65568 | tf_op jit(solution)/shard_map/latent/ppermute | solution.py:169
  208.9 2.6 collective-permute-start.12
  212.2 2.4 collective-permute-done.12
  215.4 51.9 %all-to-all-done.3 = bf16[64,2,3200]{2,1,0:T(2,128)(2,1)S(1)} async-done(((bf16[64,2,3200]{2,1,0:T(2,128)(2,1)}), bf16[64,2,3200]{2,1,0:T(2,128)(2,1)S(1)}, u32[]{:S(2)}, u32[]{:S(2)}) %all-to-all-start.3) | async-done | bytes 819232 | tf_op jit(solution)/shard_map/down/all_to_all | solution.py:165
  268.8 13.9 %all_to_all.27.parts_ref = bf16[4,320,256]{2,1,0:T(8,128)(2,1)S(1)} all-to-all(bf16[4,320,256]{2,1,0:T(8,128)(2,1)S(1)} %mix.2), channel_id=1, replica_groups={{0,32,64,96},{128,160,192,224},{256,288,320,352},{384,416,448,480},{1,3..., dimensions={0} | all-to-all | bytes 1310720 | tf_op jit(solution)/shard_map/mix/all_to_all | solution.py:165
  (48 shorter events, 9.7 us)
Async XLA Ops:
  0.6 12.7 %collective-permute-start = (bf16[320,256]{1,0:T(8,128)(2,1)}, bf16[320,256]{1,0:T(8,128)(2,1)S(1)}, u32[]{:S(2)}, u32[]{:S(2)}) collective-permute-start(bf16[320,256]{1,0:T(8,128)(2,1)} %bitcast.42), channel_id=1, source_target_pairs={{0,32},{32,0},{64,96},{96,64},{128,160},{160,128},{192,224},{224,1... | collective-permute-start | bytes 491528 | tf_op jit(solution)/shard_map/tokens/ppermute | solution.py:169
  4.1 11.1 %collective-permute-start.1 = (bf16[320,256]{1,0:T(8,128)(2,1)}, bf16[320,256]{1,0:T(8,128)(2,1)S(1)}, u32[]{:S(2)}, u32[]{:S(2)}) collective-permute-start(bf16[320,256]{1,0:T(8,128)(2,1)} %bitcast.43), channel_id=1, source_target_pairs={{0,96},{32,64},{64,32},{96,0},{128,224},{160,192},{192,160},{224,1... | collective-permute-start | bytes 491528 | tf_op jit(solution)/shard_map/tokens/ppermute | solution.py:169
  8.2 9.0 %collective-permute-start.2 = (bf16[320,256]{1,0:T(8,128)(2,1)}, bf16[320,256]{1,0:T(8,128)(2,1)S(1)}, u32[]{:S(2)}, u32[]{:S(2)}) collective-permute-start(bf16[320,256]{1,0:T(8,128)(2,1)} %bitcast.44), channel_id=1, source_target_pairs={{0,64},{32,96},{64,0},{96,32},{128,192},{160,224},{192,128},{224,1... | collective-permute-start | bytes 491528 | tf_op jit(solution)/shard_map/tokens/ppermute | solution.py:169
  11.0 0.9 copy-start
  11.9 0.7 copy-start.3
  17.7 30.0 %copy-start.9 = (bf16[2,320,1536]{2,1,0:T(8,128)(2,1)S(1)}, bf16[2,320,1536]{2,1,0:T(8,128)(2,1)}, u32[]{:S(2)}) copy-start(bf16[2,320,1536]{2,1,0:T(8,128)(2,1)} %param.12) | copy-start | bytes 5898244
  19.4 114.5 %all-to-all-start = ((bf16[64,2,3200]{2,1,0:T(2,128)(2,1)}), bf16[64,2,3200]{2,1,0:T(2,128)(2,1)}, u32[]{:S(2)}, u32[]{:S(2)}) async-start(bf16[64,2,3200]{2,1,0:T(2,128)(2,1)} %copy.11), calls=%async_computation | async-start | bytes 1638400 | tf_op jit(solution)/shard_map/dispatch/all_to_all | solution.py:165
  47.7 3.8 %copy-start.10 = (bf16[2,768,320]{1,2,0:T(8,128)(2,1)S(1)}, bf16[2,768,320]{1,2,0:T(8,128)(2,1)}, u32[]{:S(2)}) copy-start(bf16[2,768,320]{1,2,0:T(8,128)(2,1)} %param.13) | copy-start | bytes 2949124
  47.9 27.8 %collective-permute-start.7 = (bf16[320,1536]{1,0:T(8,128)(2,1)S(1)}, bf16[320,1536]{1,0:T(8,128)(2,1)S(1)}, u32[]{:S(2)}, u32[]{:S(2)}) collective-permute-start(bf16[320,1536]{1,0:T(8,128)(2,1)S(1)} %get-tuple-element.32), channel_id=1, source_target_pairs={{0,96},{32,64},{64,32},{96,0},{128,224},{160,192},{192,160},{224,1... | collective-permute-start | bytes 2949128 | tf_op jit(solution)/shard_map/gather/ppermute | solution.py:169
  51.6 34.0 %collective-permute-start.4 = (bf16[320,768]{1,0:T(8,128)(2,1)S(1)}, bf16[320,768]{1,0:T(8,128)(2,1)}, u32[]{:S(2)}, u32[]{:S(2)}) collective-permute-start(bf16[320,768]{1,0:T(8,128)(2,1)S(1)} %get-tuple-element.34), channel_id=1, source_target_pairs={{0,96},{32,64},{64,32},{96,0},{128,224},{160,192},{192,160},{224,1... | collective-permute-start | bytes 1474568 | tf_op jit(solution)/shard_map/gather/ppermute | solution.py:169
  55.2 80.0 %collective-permute-start.6 = (bf16[320,1536]{1,0:T(8,128)(2,1)S(1)}, bf16[320,1536]{1,0:T(8,128)(2,1)S(1)}, u32[]{:S(2)}, u32[]{:S(2)}) collective-permute-start(bf16[320,1536]{1,0:T(8,128)(2,1)S(1)} %get-tuple-element.33.w0), channel_id=1, source_target_pairs={{0,32},{32,0},{64,96},{96,64},{128,160},{160,128},{192,224},{224,1... | collective-permute-start | bytes 2949128 | tf_op jit(solution)/shard_map/gather/ppermute | solution.py:169
  75.7 59.5 %collective-permute-start.8 = (bf16[320,1536]{1,0:T(8,128)(2,1)S(1)}, bf16[320,1536]{1,0:T(8,128)(2,1)}, u32[]{:S(2)}, u32[]{:S(2)}) collective-permute-start(bf16[320,1536]{1,0:T(8,128)(2,1)S(1)} %collective-permute-done.7.w2), channel_id=1, source_target_pairs={{0,32},{32,0},{64,96},{96,64},{128,160},{160,128},{192,224},{224,1... | collective-permute-start | bytes 2949128 | tf_op jit(solution)/shard_map/gather/ppermute | solution.py:169
  77.6 57.6 %collective-permute-start.3 = (bf16[320,768]{1,0:T(8,128)(2,1)S(1)}, bf16[320,768]{1,0:T(8,128)(2,1)}, u32[]{:S(2)}, u32[]{:S(2)}) collective-permute-start(bf16[320,768]{1,0:T(8,128)(2,1)S(1)} %get-tuple-element.23.w0), channel_id=1, source_target_pairs={{0,32},{32,0},{64,96},{96,64},{128,160},{160,128},{192,224},{224,1... | collective-permute-start | bytes 1474568 | tf_op jit(solution)/shard_map/gather/ppermute | solution.py:169
  85.6 49.5 %collective-permute-start.5 = (bf16[320,768]{1,0:T(8,128)(2,1)}, bf16[320,768]{1,0:T(8,128)(2,1)}, u32[]{:S(2)}, u32[]{:S(2)}) collective-permute-start(bf16[320,768]{1,0:T(8,128)(2,1)} %collective-permute-done.4.w2), channel_id=1, source_target_pairs={{0,32},{32,0},{64,96},{96,64},{128,160},{160,128},{192,224},{224,1... | collective-permute-start | bytes 1474568 | tf_op jit(solution)/shard_map/gather/ppermute | solution.py:169
  170.8 10.2 %copy-start.1 = (bf16[256,320]{0,1:T(8,128)(2,1)S(1)}, bf16[256,320]{0,1:T(8,128)(2,1)}, u32[]{:S(2)}) copy-start(bf16[256,320]{0,1:T(8,128)(2,1)} %param.9) | copy-start | bytes 491524
  170.8 10.2 %copy-start.2 = (bf16[320,512]{1,0:T(8,128)(2,1)S(1)}, bf16[320,512]{1,0:T(8,128)(2,1)}, u32[]{:S(2)}) copy-start(bf16[320,512]{1,0:T(8,128)(2,1)} %weight_ref.1) | copy-start | bytes 983044
  170.9 10.2 %copy-start.7 = (s32[1,16]{1,0:T(1,128)S(1)}, s32[1,16]{1,0:T(1,128)}, u32[]{:S(2)}) copy-start(s32[1,16]{1,0:T(1,128)} %lengths_ref.1) | copy-start | bytes 196
  170.9 10.2 %copy-start.8 = (s32[1,16]{1,0:T(1,128)S(1)}, s32[1,16]{1,0:T(1,128)}, u32[]{:S(2)}) copy-start(s32[1,16]{1,0:T(1,128)} %placement_ref.1) | copy-start | bytes 196
  172.6 94.6 %all-to-all-start.3 = ((bf16[64,2,3200]{2,1,0:T(2,128)(2,1)}), bf16[64,2,3200]{2,1,0:T(2,128)(2,1)S(1)}, u32[]{:S(2)}, u32[]{:S(2)}) async-start(bf16[64,2,3200]{2,1,0:T(2,128)(2,1)} %copy.13), calls=%async_computation.3 | async-start | bytes 1638400 | tf_op jit(solution)/shard_map/down/all_to_all | solution.py:165
  181.0 30.4 %copy-start.4 = (s32[256,4]{0,1:T(4,128)S(1)}, s32[256,4]{0,1:T(4,128)}, u32[]{:S(2)}) copy-start(s32[256,4]{0,1:T(4,128)} %param.10) | copy-start | bytes 12292
  181.1 30.4 %copy-start.5 = (f32[256,4]{0,1:T(4,128)S(1)}, f32[256,4]{0,1:T(4,128)}, u32[]{:S(2)}) copy-start(f32[256,4]{0,1:T(4,128)} %param.11) | copy-start | bytes 12292
  182.2 32.5 %copy-start.6 = (f32[512]{0:T(512)S(1)}, f32[512]{0:T(512)}, u32[]{:S(2)}) copy-start(f32[512]{0:T(512)} %param.15) | copy-start | bytes 6148
  182.3 11.8 %collective-permute-start.9 = (bf16[8,32,512]{2,1,0:T(8,128)(2,1)S(1)}, bf16[8,32,512]{2,1,0:T(8,128)(2,1)S(1)}, u32[]{:S(2)}, u32[]{:S(2)}) collective-permute-start(bf16[8,32,512]{2,1,0:T(8,128)(2,1)S(1)} %bitcast.52), channel_id=1, source_target_pairs={{0,256},{32,288},{64,320},{96,352},{128,384},{160,416},{192,448},{... | collective-permute-start | bytes 786440 | tf_op jit(solution)/shard_map/latent/ppermute | solution.py:169
  194.2 6.9 %collective-permute-start.10 = (bf16[4,32,512]{2,1,0:T(8,128)(2,1)S(1)}, bf16[4,32,512]{2,1,0:T(8,128)(2,1)S(1)}, u32[]{:S(2)}, u32[]{:S(2)}) collective-permute-start(bf16[4,32,512]{2,1,0:T(8,128)(2,1)S(1)} %broadcast_select_fusion.2), channel_id=1, source_target_pairs={{0,128},{32,160},{64,192},{96,224},{128,0},{160,32},{192,64},{224,... | collective-permute-start | bytes 393224 | tf_op jit(solution)/shard_map/latent/ppermute | solution.py:169
  201.2 7.7 %collective-permute-start.11 = (bf16[2,32,512]{2,1,0:T(8,128)(2,1)S(1)}, bf16[2,32,512]{2,1,0:T(8,128)(2,1)S(1)}, u32[]{:S(2)}, u32[]{:S(2)}) collective-permute-start(bf16[2,32,512]{2,1,0:T(8,128)(2,1)S(1)} %broadcast_select_fusion.3), channel_id=1, source_target_pairs={{0,64},{32,96},{64,0},{96,32},{128,192},{160,224},{192,128},{224,1... | collective-permute-start | bytes 196616 | tf_op jit(solution)/shard_map/latent/ppermute | solution.py:169
  208.9 5.8 %collective-permute-start.12 = (bf16[1,32,512]{2,1,0:T(8,128)(2,1)S(1)}, bf16[1,32,512]{2,1,0:T(8,128)(2,1)S(1)}, u32[]{:S(2)}, u32[]{:S(2)}) collective-permute-start(bf16[1,32,512]{2,1,0:T(8,128)(2,1)S(1)} %broadcast_select_fusion.4), channel_id=1, source_target_pairs={{0,32},{32,0},{64,96},{96,64},{128,160},{160,128},{192,224},{224,1... | collective-permute-start | bytes 98312 | tf_op jit(solution)/shard_map/latent/ppermute | solution.py:169

commit v7 on v6

--- a/solution.py
+++ b/solution.py
@@ -8,6 +8,7 @@
 from jax.sharding import PartitionSpec as P
 
 SE = ("section", "expert")
+CHIPS = ("expert", "section")
 NT = (((1,), (1,)), ((), ()))
 TN = (((0,), (0,)), ((), ()))
 BF = jnp.bfloat16
@@ -36,7 +37,8 @@
 def slot_masks(pick_ref, routes_t, lanes, groups):
     tops, rows = routes_t.shape
     resident, part = pick_ref[0], pick_ref[1]
-    ids = iota((groups, rows), 0) * 2 + resident
+    member = iota((groups, rows), 0)
+    ids = ((member & 1) * (groups // 2) + (member >> 1)) * 2 + resident
     named = jnp.zeros((groups, rows), F32)
     for k in range(tops):
         named = named + jnp.where(routes_t[k : k + 1, :] == ids, 1.0, 0.0)
@@ -105,14 +107,26 @@
         out[b] = hidden
 
 
-def down_kernel(hidden_ref, w0, w1, w2, w3, out):
-    _, groups, row = out.shape
-    span = 2 * w0.shape[0]
-    for p, (left, right) in enumerate(((w0, w1), (w2, w3))):
-        weight = jnp.concatenate([left[...], right[...]], axis=0)
-        part = lax.dot_general(hidden_ref[...], weight, NT, preferred_element_type=F32).astype(BF)
-        for i in range(row // span):
-            out[p, :, i * span : (i + 1) * span] = part[i * groups : (i + 1) * groups, :]
+def halves_first(count):
+    a = iota((count, count), 1)
+    return (iota((count, count), 0) == (a & 1) * (count // 2) + (a >> 1)).astype(F32).astype(BF)
+
+
+def down_kernel(lanes, hidden_ref, w0, w1, w2, w3, out, packed):
+    count = out.shape[0]
+    groups = count // 2
+    width = w0.shape[0]
+    span = 2 * width
+    for k, weight in enumerate((w0, w1, w2, w3)):
+        part = lax.dot_general(hidden_ref[...], weight[...], NT, preferred_element_type=F32)
+        part = part.astype(BF)
+        p, skip = k // 2, (k % 2) * width
+        for i in range(lanes):
+            at = i * span + skip
+            piece = part[i * groups : (i + 1) * groups, :]
+            packed[p * groups : (p + 1) * groups, at : at + width] = piece
+    rows = lax.dot_general(halves_first(count), packed[...], TN, preferred_element_type=F32)
+    out[...] = rows.astype(BF)
 
 
 def mix_kernel(pick_ref, back_ref, gates_ref, out):
@@ -247,7 +261,7 @@
             moved=2 * slots * row,
         )
         outgoing, w_gate_up, w_down = lax.optimization_barrier((outgoing, w_gate_up, w_down))
-        arrived = exchange(outgoing.transpose(1, 0, 2), SE).transpose(1, 0, 2)
+        arrived = exchange(outgoing.transpose(1, 0, 2), CHIPS).transpose(1, 0, 2)
 
     with jax.named_scope("gather"):
         up_blocks = gather_expert(w_gate_up, resident)
@@ -286,15 +300,16 @@
 
     with jax.named_scope("down"):
         produced = call(
-            down_kernel,
-            shape((2, groups, row), BF),
+            functools.partial(down_kernel, lanes),
+            shape((slots, row), BF),
             gathered.reshape(taken, hidden_units),
             *down_blocks,
+            scratch=[pltpu.VMEM((slots, row), BF)],
             flops=8 * taken * width * hidden_units,
             moved=2 * hidden_units * (4 * width + taken),
         )
         produced, tokens_t, gates_t = lax.optimization_barrier((produced, tokens_t, gates_t))
-        back = exchange(produced.transpose(1, 0, 2), SE).transpose(1, 0, 2)
+        back = exchange(produced.reshape(groups, 2, row), CHIPS).transpose(1, 0, 2)
 
     with jax.named_scope("gates"):
         gates = call(

time: 284 us -> 287 us (1.011)
  the two profiles are of different devices: /device:TPU:96 before, /device:TPU:2 now
where the time goes in v7:
time: 287 us; the launch traced here: 286 us
  waiting for transfers between devices  153 us (53%)
  starting transfers between devices  75 us (26%)
  blocking collectives  37.7 us (13%)
  Pallas kernels  12.4 us (4%)
  local copies, waits for them, and re-layouts  6.15 us (2%)
    all_to_all x2, waiting for transfers between devices, exchange(): lax.all_to_all(x, axes, split_axis=0, concat_axis=0, axis_index_groups=gr...  108 us
    ppermute x13, waiting for transfers between devices, flip(): lax.ppermute(x, 'dp', [(i, i ^ bits) for i in range(lax.axis_size('dp'))])  44.8 us
    ppermute x13, starting transfers between devices, flip(): lax.ppermute(x, 'dp', [(i, i ^ bits) for i in range(lax.axis_size('dp'))])  39.9 us
    all_to_all x3, blocking collectives, exchange(): lax.all_to_all(x, axes, split_axis=0, concat_axis=0, axis_index_groups=gr...  37.7 us
    all_to_all x2, starting transfers between devices, exchange(): lax.all_to_all(x, axes, split_axis=0, concat_axis=0, axis_index_groups=gr...  35.2 us
    pallas_call x9, Pallas kernels, call(): pl.pallas_call(kernel, out_shape=out_shape, scratch_shapes=list(scratch),...  9.04 us
  transfers between devices with their start and end apart: 15, of which 10 were waited for; matrix products, arithmetic and copies ran while one was open for 1% of the time, Pallas kernels for 1%

profile of v7, /device:TPU:2, one launch (start us, length us, event | category | flops | bytes accessed | tf_op | source)
XLA Modules:
  0.0 285.6 jit_solution(12656204000475466928)
XLA Ops:
  0.6 3.5 %collective-permute-start = (bf16[320,256]{1,0:T(8,128)(2,1)}, bf16[320,256]{1,0:T(8,128)(2,1)S(1)}, u32[]{:S(2)}, u32[]{:S(2)}) collective-permute-start(bf16[320,256]{1,0:T(8,128)(2,1)} %bitcast.40), channel_id=1, source_target_pairs={{0,32},{32,0},{64,96},{96,64},{128,160},{160,128},{192,224},{224,1... | collective-permute-start | bytes 491528 | tf_op jit(solution)/shard_map/tokens/ppermute | solution.py:183
  4.1 4.1 %collective-permute-start.1 = (bf16[320,256]{1,0:T(8,128)(2,1)}, bf16[320,256]{1,0:T(8,128)(2,1)S(1)}, u32[]{:S(2)}, u32[]{:S(2)}) collective-permute-start(bf16[320,256]{1,0:T(8,128)(2,1)} %bitcast.41), channel_id=1, source_target_pairs={{0,96},{32,64},{64,32},{96,0},{128,224},{160,192},{192,160},{224,1... | collective-permute-start | bytes 491528 | tf_op jit(solution)/shard_map/tokens/ppermute | solution.py:183
  8.2 2.6 collective-permute-start.2
  13.3 1.9 collective-permute-done.1.t2
  15.2 2.0 collective-permute-done.2.t3
  17.7 1.7 copy.12
  19.4 29.6 %all-to-all-start = ((bf16[64,2,3200]{2,1,0:T(2,128)(2,1)}), bf16[64,2,3200]{2,1,0:T(2,128)(2,1)}, u32[]{:S(2)}, u32[]{:S(2)}) async-start(bf16[64,2,3200]{2,1,0:T(2,128)(2,1)} %copy.12), calls=%async_computation | async-start | bytes 1638400 | tf_op jit(solution)/shard_map/dispatch/all_to_all | solution.py:179
  49.2 3.6 %collective-permute-start.7 = (bf16[320,1536]{1,0:T(8,128)(2,1)S(1)}, bf16[320,1536]{1,0:T(8,128)(2,1)S(1)}, u32[]{:S(2)}, u32[]{:S(2)}) collective-permute-start(bf16[320,1536]{1,0:T(8,128)(2,1)S(1)} %get-tuple-element.32), channel_id=1, source_target_pairs={{0,96},{32,64},{64,32},{96,0},{128,224},{160,192},{192,160},{224,1... | collective-permute-start | bytes 2949128 | tf_op jit(solution)/shard_map/gather/ppermute | solution.py:183
  52.9 3.6 %collective-permute-start.4 = (bf16[320,768]{1,0:T(8,128)(2,1)S(1)}, bf16[320,768]{1,0:T(8,128)(2,1)}, u32[]{:S(2)}, u32[]{:S(2)}) collective-permute-start(bf16[320,768]{1,0:T(8,128)(2,1)S(1)} %get-tuple-element.34), channel_id=1, source_target_pairs={{0,96},{32,64},{64,32},{96,0},{128,224},{160,192},{192,160},{224,1... | collective-permute-start | bytes 1474568 | tf_op jit(solution)/shard_map/gather/ppermute | solution.py:183
  56.5 1.9 collective-permute-start.6
  58.4 18.6 %collective-permute-done.7.w2 = bf16[320,1536]{1,0:T(8,128)(2,1)S(1)} collective-permute-done((bf16[320,1536]{1,0:T(8,128)(2,1)S(1)}, bf16[320,1536]{1,0:T(8,128)(2,1)S(1)}, u32[]{:S(2)}, u32[]{:S(2)}) %collective-permute-start.7) | collective-permute-done | bytes 983072 | tf_op jit(solution)/shard_map/gather/ppermute | solution.py:183
  77.0 1.9 collective-permute-start.8
  79.0 3.9 %collective-permute-start.3 = (bf16[320,768]{1,0:T(8,128)(2,1)S(1)}, bf16[320,768]{1,0:T(8,128)(2,1)}, u32[]{:S(2)}, u32[]{:S(2)}) collective-permute-start(bf16[320,768]{1,0:T(8,128)(2,1)S(1)} %get-tuple-element.23.w0), channel_id=1, source_target_pairs={{0,32},{32,0},{64,96},{96,64},{128,160},{160,128},{192,224},{224,1... | collective-permute-start | bytes 1474568 | tf_op jit(solution)/shard_map/gather/ppermute | solution.py:183
  82.9 3.8 %collective-permute-done.4.w2 = bf16[320,768]{1,0:T(8,128)(2,1)} collective-permute-done((bf16[320,768]{1,0:T(8,128)(2,1)S(1)}, bf16[320,768]{1,0:T(8,128)(2,1)}, u32[]{:S(2)}, u32[]{:S(2)}) %collective-permute-start.4) | collective-permute-done | bytes 491552 | tf_op jit(solution)/shard_map/gather/ppermute | solution.py:183
  86.7 1.9 collective-permute-start.5
  88.6 51.3 %all-to-all-done = bf16[64,2,3200]{2,1,0:T(2,128)(2,1)} async-done(((bf16[64,2,3200]{2,1,0:T(2,128)(2,1)}), bf16[64,2,3200]{2,1,0:T(2,128)(2,1)}, u32[]{:S(2)}, u32[]{:S(2)}) %all-to-all-start) | async-done | bytes 819232 | tf_op jit(solution)/shard_map/dispatch/all_to_all | solution.py:179
  141.2 3.4 %up.1 = bf16[320,1536]{1,0:T(8,128)(2,1)S(1)} custom-call(bf16[2,64,3200]{2,1,0:T(8,128)(2,1)S(1)} %bitcast.37, bf16[320,1536]{1,0:T(8,128)(2,1)S(1)} %get-tuple-element.33.w0, bf16[320,1536]{1,0:T(8,128)(2,1)S(1)} %collective-permute-done.6.w1, bf16[320,1536]{1,0:T(8,128)(2,1)S(1)} %collective-permute-done.7.w2, bf16[320,1536]{1,0:T(8,128)(2,1)} %collective-permute-done.8.w3), custom_call_target="tpu_custom_call" | custom-call | flops 1258291200 | bytes 4915200 | tf_op jit(solution)/shard_map/up/pallas_call | solution.py:274
  144.6 15.7 %all_to_all.25.parts_ref = bf16[4,80,1536]{2,1,0:T(8,128)(2,1)S(1)} all-to-all(bf16[4,80,1536]{2,1,0:T(8,128)(2,1)S(1)} %bitcast.35), channel_id=1, replica_groups={{0,128,256,384},{32,160,288,416},{64,192,320,448},{96,224,352,480},{1,1..., dimensions={0} | all-to-all | bytes 1966080 | tf_op jit(solution)/shard_map/up/all_to_all | solution.py:179
  160.5 10.3 %all_to_all.26 = bf16[4,80,768]{2,1,0:T(8,128)(2,1)S(1)} all-to-all(bf16[4,80,768]{2,1,0:T(8,128)(2,1)S(1)} %hidden.1), channel_id=1, replica_groups={{0,128,256,384},{32,160,288,416},{64,192,320,448},{96,224,352,480},{1,1..., dimensions={0} | all-to-all | bytes 983040 | tf_op jit(solution)/shard_map/hidden/all_to_all | solution.py:179
  170.8 2.9 %down.1 = bf16[128,3200]{1,0:T(8,128)(2,1)S(1)} custom-call(bf16[320,768]{1,0:T(8,128)(2,1)S(1)} %bitcast.38, bf16[320,768]{1,0:T(8,128)(2,1)S(1)} %get-tuple-element.23.w0, bf16[320,768]{1,0:T(8,128)(2,1)} %collective-permute-done.3.w1, bf16[320,768]{1,0:T(8,128)(2,1)} %collective-permute-done.4.w2, bf16[320,768]{1,0:T(8,128)(2,1)} %collective-permute-done.5.w3), custom_call_target="tpu_custom_call" | custom-call | flops 629145600 | bytes 2457600 | tf_op jit(solution)/shard_map/down/pallas_call | solution.py:23
  174.9 5.6 %all-to-all-start.3 = ((bf16[64,2,3200]{2,1,0:T(2,128)(2,1)}), bf16[64,2,3200]{2,1,0:T(2,128)(2,1)S(1)}, u32[]{:S(2)}, u32[]{:S(2)}) async-start(bf16[64,2,3200]{2,1,0:T(2,128)(2,1)} %reshape.30), calls=%async_computation.3 | async-start | bytes 1638400 | tf_op jit(solution)/shard_map/down/all_to_all | solution.py:179
  181.8 3.4 %collective-permute-start.9 = (bf16[8,32,512]{2,1,0:T(8,128)(2,1)S(1)}, bf16[8,32,512]{2,1,0:T(8,128)(2,1)S(1)}, u32[]{:S(2)}, u32[]{:S(2)}) collective-permute-start(bf16[8,32,512]{2,1,0:T(8,128)(2,1)S(1)} %bitcast.50), channel_id=1, source_target_pairs={{0,256},{32,288},{64,320},{96,352},{128,384},{160,416},{192,448},{... | collective-permute-start | bytes 786440 | tf_op jit(solution)/shard_map/latent/ppermute | solution.py:183
  185.2 8.3 %collective-permute-done.9 = bf16[8,32,512]{2,1,0:T(8,128)(2,1)S(1)} collective-permute-done((bf16[8,32,512]{2,1,0:T(8,128)(2,1)S(1)}, bf16[8,32,512]{2,1,0:T(8,128)(2,1)S(1)}, u32[]{:S(2)}, u32[]{:S(2)}) %collective-permute-start.9) | collective-permute-done | bytes 262176 | tf_op jit(solution)/shard_map/latent/ppermute | solution.py:183
  193.6 3.4 %collective-permute-start.10 = (bf16[4,32,512]{2,1,0:T(8,128)(2,1)S(1)}, bf16[4,32,512]{2,1,0:T(8,128)(2,1)S(1)}, u32[]{:S(2)}, u32[]{:S(2)}) collective-permute-start(bf16[4,32,512]{2,1,0:T(8,128)(2,1)S(1)} %broadcast_select_fusion.2), channel_id=1, source_target_pairs={{0,128},{32,160},{64,192},{96,224},{128,0},{160,32},{192,64},{224,... | collective-permute-start | bytes 393224 | tf_op jit(solution)/shard_map/latent/ppermute | solution.py:183
  196.9 3.5 %collective-permute-done.10 = bf16[4,32,512]{2,1,0:T(8,128)(2,1)S(1)} collective-permute-done((bf16[4,32,512]{2,1,0:T(8,128)(2,1)S(1)}, bf16[4,32,512]{2,1,0:T(8,128)(2,1)S(1)}, u32[]{:S(2)}, u32[]{:S(2)}) %collective-permute-start.10) | collective-permute-done | bytes 131104 | tf_op jit(solution)/shard_map/latent/ppermute | solution.py:183
  200.5 3.5 %collective-permute-start.11 = (bf16[2,32,512]{2,1,0:T(8,128)(2,1)S(1)}, bf16[2,32,512]{2,1,0:T(8,128)(2,1)S(1)}, u32[]{:S(2)}, u32[]{:S(2)}) collective-permute-start(bf16[2,32,512]{2,1,0:T(8,128)(2,1)S(1)} %broadcast_select_fusion.3), channel_id=1, source_target_pairs={{0,64},{32,96},{64,0},{96,32},{128,192},{160,224},{192,128},{224,1... | collective-permute-start | bytes 196616 | tf_op jit(solution)/shard_map/latent/ppermute | solution.py:183
  204.1 4.1 %collective-permute-done.11 = bf16[2,32,512]{2,1,0:T(8,128)(2,1)S(1)} collective-permute-done((bf16[2,32,512]{2,1,0:T(8,128)(2,1)S(1)}, bf16[2,32,512]{2,1,0:T(8,128)(2,1)S(1)}, u32[]{:S(2)}, u32[]{:S(2)}) %collective-permute-start.11) | collective-permute-done | bytes 65568 | tf_op jit(solution)/shard_map/latent/ppermute | solution.py:183
  208.2 2.5 collective-permute-start.12
  211.5 2.5 collective-permute-done.12
  214.8 56.8 %all-to-all-done.3 = bf16[64,2,3200]{2,1,0:T(2,128)(2,1)S(1)} async-done(((bf16[64,2,3200]{2,1,0:T(2,128)(2,1)}), bf16[64,2,3200]{2,1,0:T(2,128)(2,1)S(1)}, u32[]{:S(2)}, u32[]{:S(2)}) %all-to-all-start.3) | async-done | bytes 819232 | tf_op jit(solution)/shard_map/down/all_to_all | solution.py:179
  271.7 1.4 mix.2
  273.1 11.7 %all_to_all.27.parts_ref = bf16[4,320,256]{2,1,0:T(8,128)(2,1)S(1)} all-to-all(bf16[4,320,256]{2,1,0:T(8,128)(2,1)S(1)} %mix.2), channel_id=1, replica_groups={{0,32,64,96},{128,160,192,224},{256,288,320,352},{384,416,448,480},{1,3..., dimensions={0} | all-to-all | bytes 1310720 | tf_op jit(solution)/shard_map/mix/all_to_all | solution.py:179
  (48 shorter events, 9.4 us)
Async XLA Ops:
  0.6 12.7 %collective-permute-start = (bf16[320,256]{1,0:T(8,128)(2,1)}, bf16[320,256]{1,0:T(8,128)(2,1)S(1)}, u32[]{:S(2)}, u32[]{:S(2)}) collective-permute-start(bf16[320,256]{1,0:T(8,128)(2,1)} %bitcast.40), channel_id=1, source_target_pairs={{0,32},{32,0},{64,96},{96,64},{128,160},{160,128},{192,224},{224,1... | collective-permute-start | bytes 491528 | tf_op jit(solution)/shard_map/tokens/ppermute | solution.py:183
  4.1 11.1 %collective-permute-start.1 = (bf16[320,256]{1,0:T(8,128)(2,1)}, bf16[320,256]{1,0:T(8,128)(2,1)S(1)}, u32[]{:S(2)}, u32[]{:S(2)}) collective-permute-start(bf16[320,256]{1,0:T(8,128)(2,1)} %bitcast.41), channel_id=1, source_target_pairs={{0,96},{32,64},{64,32},{96,0},{128,224},{160,192},{192,160},{224,1... | collective-permute-start | bytes 491528 | tf_op jit(solution)/shard_map/tokens/ppermute | solution.py:183
  8.2 9.0 %collective-permute-start.2 = (bf16[320,256]{1,0:T(8,128)(2,1)}, bf16[320,256]{1,0:T(8,128)(2,1)S(1)}, u32[]{:S(2)}, u32[]{:S(2)}) collective-permute-start(bf16[320,256]{1,0:T(8,128)(2,1)} %bitcast.42), channel_id=1, source_target_pairs={{0,64},{32,96},{64,0},{96,32},{128,192},{160,224},{192,128},{224,1... | collective-permute-start | bytes 491528 | tf_op jit(solution)/shard_map/tokens/ppermute | solution.py:183
  11.0 0.9 copy-start
  11.9 0.7 copy-start.3
  17.7 31.4 %copy-start.9 = (bf16[2,320,1536]{2,1,0:T(8,128)(2,1)S(1)}, bf16[2,320,1536]{2,1,0:T(8,128)(2,1)}, u32[]{:S(2)}) copy-start(bf16[2,320,1536]{2,1,0:T(8,128)(2,1)} %param.12) | copy-start | bytes 5898244
  19.4 120.5 %all-to-all-start = ((bf16[64,2,3200]{2,1,0:T(2,128)(2,1)}), bf16[64,2,3200]{2,1,0:T(2,128)(2,1)}, u32[]{:S(2)}, u32[]{:S(2)}) async-start(bf16[64,2,3200]{2,1,0:T(2,128)(2,1)} %copy.12), calls=%async_computation | async-start | bytes 1638400 | tf_op jit(solution)/shard_map/dispatch/all_to_all | solution.py:179
  49.0 3.8 %copy-start.10 = (bf16[2,768,320]{1,2,0:T(8,128)(2,1)S(1)}, bf16[2,768,320]{1,2,0:T(8,128)(2,1)}, u32[]{:S(2)}) copy-start(bf16[2,768,320]{1,2,0:T(8,128)(2,1)} %param.13) | copy-start | bytes 2949124
  49.2 27.9 %collective-permute-start.7 = (bf16[320,1536]{1,0:T(8,128)(2,1)S(1)}, bf16[320,1536]{1,0:T(8,128)(2,1)S(1)}, u32[]{:S(2)}, u32[]{:S(2)}) collective-permute-start(bf16[320,1536]{1,0:T(8,128)(2,1)S(1)} %get-tuple-element.32), channel_id=1, source_target_pairs={{0,96},{32,64},{64,32},{96,0},{128,224},{160,192},{192,160},{224,1... | collective-permute-start | bytes 2949128 | tf_op jit(solution)/shard_map/gather/ppermute | solution.py:183
  52.9 33.8 %collective-permute-start.4 = (bf16[320,768]{1,0:T(8,128)(2,1)S(1)}, bf16[320,768]{1,0:T(8,128)(2,1)}, u32[]{:S(2)}, u32[]{:S(2)}) collective-permute-start(bf16[320,768]{1,0:T(8,128)(2,1)S(1)} %get-tuple-element.34), channel_id=1, source_target_pairs={{0,96},{32,64},{64,32},{96,0},{128,224},{160,192},{192,160},{224,1... | collective-permute-start | bytes 1474568 | tf_op jit(solution)/shard_map/gather/ppermute | solution.py:183
  56.5 84.7 %collective-permute-start.6 = (bf16[320,1536]{1,0:T(8,128)(2,1)S(1)}, bf16[320,1536]{1,0:T(8,128)(2,1)S(1)}, u32[]{:S(2)}, u32[]{:S(2)}) collective-permute-start(bf16[320,1536]{1,0:T(8,128)(2,1)S(1)} %get-tuple-element.33.w0), channel_id=1, source_target_pairs={{0,32},{32,0},{64,96},{96,64},{128,160},{160,128},{192,224},{224,1... | collective-permute-start | bytes 2949128 | tf_op jit(solution)/shard_map/gather/ppermute | solution.py:183
  77.0 64.1 %collective-permute-start.8 = (bf16[320,1536]{1,0:T(8,128)(2,1)S(1)}, bf16[320,1536]{1,0:T(8,128)(2,1)}, u32[]{:S(2)}, u32[]{:S(2)}) collective-permute-start(bf16[320,1536]{1,0:T(8,128)(2,1)S(1)} %collective-permute-done.7.w2), channel_id=1, source_target_pairs={{0,32},{32,0},{64,96},{96,64},{128,160},{160,128},{192,224},{224,1... | collective-permute-start | bytes 2949128 | tf_op jit(solution)/shard_map/gather/ppermute | solution.py:183
  79.0 62.2 %collective-permute-start.3 = (bf16[320,768]{1,0:T(8,128)(2,1)S(1)}, bf16[320,768]{1,0:T(8,128)(2,1)}, u32[]{:S(2)}, u32[]{:S(2)}) collective-permute-start(bf16[320,768]{1,0:T(8,128)(2,1)S(1)} %get-tuple-element.23.w0), channel_id=1, source_target_pairs={{0,32},{32,0},{64,96},{96,64},{128,160},{160,128},{192,224},{224,1... | collective-permute-start | bytes 1474568 | tf_op jit(solution)/shard_map/gather/ppermute | solution.py:183
  86.7 54.5 %collective-permute-start.5 = (bf16[320,768]{1,0:T(8,128)(2,1)}, bf16[320,768]{1,0:T(8,128)(2,1)}, u32[]{:S(2)}, u32[]{:S(2)}) collective-permute-start(bf16[320,768]{1,0:T(8,128)(2,1)} %collective-permute-done.4.w2), channel_id=1, source_target_pairs={{0,32},{32,0},{64,96},{96,64},{128,160},{160,128},{192,224},{224,1... | collective-permute-start | bytes 1474568 | tf_op jit(solution)/shard_map/gather/ppermute | solution.py:183
  173.7 6.9 %copy-start.1 = (bf16[256,320]{0,1:T(8,128)(2,1)S(1)}, bf16[256,320]{0,1:T(8,128)(2,1)}, u32[]{:S(2)}) copy-start(bf16[256,320]{0,1:T(8,128)(2,1)} %param.9) | copy-start | bytes 491524
  173.7 6.9 %copy-start.2 = (bf16[320,512]{1,0:T(8,128)(2,1)S(1)}, bf16[320,512]{1,0:T(8,128)(2,1)}, u32[]{:S(2)}) copy-start(bf16[320,512]{1,0:T(8,128)(2,1)} %weight_ref.1) | copy-start | bytes 983044
  173.7 6.9 %copy-start.7 = (s32[1,16]{1,0:T(1,128)S(1)}, s32[1,16]{1,0:T(1,128)}, u32[]{:S(2)}) copy-start(s32[1,16]{1,0:T(1,128)} %lengths_ref.1) | copy-start | bytes 196
  173.7 6.9 %copy-start.8 = (s32[1,16]{1,0:T(1,128)S(1)}, s32[1,16]{1,0:T(1,128)}, u32[]{:S(2)}) copy-start(s32[1,16]{1,0:T(1,128)} %placement_ref.1) | copy-start | bytes 196
  174.9 96.6 %all-to-all-start.3 = ((bf16[64,2,3200]{2,1,0:T(2,128)(2,1)}), bf16[64,2,3200]{2,1,0:T(2,128)(2,1)S(1)}, u32[]{:S(2)}, u32[]{:S(2)}) async-start(bf16[64,2,3200]{2,1,0:T(2,128)(2,1)} %reshape.30), calls=%async_computation.3 | async-start | bytes 1638400 | tf_op jit(solution)/shard_map/down/all_to_all | solution.py:179
  180.6 30.2 %copy-start.4 = (s32[256,4]{0,1:T(4,128)S(1)}, s32[256,4]{0,1:T(4,128)}, u32[]{:S(2)}) copy-start(s32[256,4]{0,1:T(4,128)} %param.10) | copy-start | bytes 12292
  180.6 30.2 %copy-start.5 = (f32[256,4]{0,1:T(4,128)S(1)}, f32[256,4]{0,1:T(4,128)}, u32[]{:S(2)}) copy-start(f32[256,4]{0,1:T(4,128)} %param.11) | copy-start | bytes 12292
  181.7 32.3 %copy-start.6 = (f32[512]{0:T(512)S(1)}, f32[512]{0:T(512)}, u32[]{:S(2)}) copy-start(f32[512]{0:T(512)} %param.15) | copy-start | bytes 6148
  181.8 11.7 %collective-permute-start.9 = (bf16[8,32,512]{2,1,0:T(8,128)(2,1)S(1)}, bf16[8,32,512]{2,1,0:T(8,128)(2,1)S(1)}, u32[]{:S(2)}, u32[]{:S(2)}) collective-permute-start(bf16[8,32,512]{2,1,0:T(8,128)(2,1)S(1)} %bitcast.50), channel_id=1, source_target_pairs={{0,256},{32,288},{64,320},{96,352},{128,384},{160,416},{192,448},{... | collective-permute-start | bytes 786440 | tf_op jit(solution)/shard_map/latent/ppermute | solution.py:183
  193.6 6.9 %collective-permute-start.10 = (bf16[4,32,512]{2,1,0:T(8,128)(2,1)S(1)}, bf16[4,32,512]{2,1,0:T(8,128)(2,1)S(1)}, u32[]{:S(2)}, u32[]{:S(2)}) collective-permute-start(bf16[4,32,512]{2,1,0:T(8,128)(2,1)S(1)} %broadcast_select_fusion.2), channel_id=1, source_target_pairs={{0,128},{32,160},{64,192},{96,224},{128,0},{160,32},{192,64},{224,... | collective-permute-start | bytes 393224 | tf_op jit(solution)/shard_map/latent/ppermute | solution.py:183
  200.5 7.7 %collective-permute-start.11 = (bf16[2,32,512]{2,1,0:T(8,128)(2,1)S(1)}, bf16[2,32,512]{2,1,0:T(8,128)(2,1)S(1)}, u32[]{:S(2)}, u32[]{:S(2)}) collective-permute-start(bf16[2,32,512]{2,1,0:T(8,128)(2,1)S(1)} %broadcast_select_fusion.3), channel_id=1, source_target_pairs={{0,64},{32,96},{64,0},{96,32},{128,192},{160,224},{192,128},{224,1... | collective-permute-start | bytes 196616 | tf_op jit(solution)/shard_map/latent/ppermute | solution.py:183
  208.2 5.8 %collective-permute-start.12 = (bf16[1,32,512]{2,1,0:T(8,128)(2,1)S(1)}, bf16[1,32,512]{2,1,0:T(8,128)(2,1)S(1)}, u32[]{:S(2)}, u32[]{:S(2)}) collective-permute-start(bf16[1,32,512]{2,1,0:T(8,128)(2,1)S(1)} %broadcast_select_fusion.4), channel_id=1, source_target_pairs={{0,32},{32,0},{64,96},{96,64},{128,160},{160,128},{192,224},{224,1... | collective-permute-start | bytes 98312 | tf_op jit(solution)/shard_map/latent/ppermute | solution.py:183
